TPU v7x, 256 devices: a whole 4x4x8 slice. The times are simulated.
256 devices in a mesh: rep: 8 (over z_lo, x), shard: 32 (over z_hi, y, core).
Axes of the slice: x: 4, y: 4, z: 8 (z_hi: 4, z_lo: 2; z = z_hi * 2 + z_lo), core: 2. Of those that a mesh axis runs over, the one named last changes fastest.
Arguments:
- images: bfloat16 [512, 16, 16, 1024], P(('rep', 'shard')), may hold values from -6 to 6
- kernel: bfloat16 [9216, 512], P('shard'), may hold values from -0.0625 to 0.0625
- gn_gain: float32 [1024], replicated, may hold values from 0.1 to 1.9
- gn_bias: float32 [1024], replicated, may hold values from -3 to 3
- conv_bias: float32 [512], replicated, may hold values from -3 to 3
- cotangent: bfloat16 [512, 8, 8, 512], P(('rep', 'shard')), may hold values from -6 to 6
Outputs:
- outputs: bfloat16 [512, 8, 8, 512], P(('rep', 'shard'))
- input_grad: bfloat16 [512, 16, 16, 1024], P(('rep', 'shard'))
- kernel_grad: float32 [9216, 512], P('shard')
- bias_grad: float32 [512], replicated
All inputs are finite; a program needn't handle non-finite values.
Results may differ from a plain program's by a relative error of at most 0.0041.
Values may be sent and summed in bfloat16 or wider, within the bound.
No kernel may reach another device: no remote copies, remote signals or barrier semaphores. Data moves between devices by JAX's collectives and lax.ppermute only.
A program may use at most 128 MiB of HBM per device.

v0:
```python
import jax
import jax.numpy as jnp
from jax import lax
from jax.sharding import PartitionSpec as P

GROUPS = 32


def norm_act(values, gain, shift):
    batch, rows, cols, chans = values.shape
    grouped = values.reshape(batch, rows, cols, GROUPS, chans // GROUPS)
    center = jnp.mean(grouped, axis=(1, 2, 4), keepdims=True)
    spread = jnp.mean(jnp.square(grouped - center), axis=(1, 2, 4), keepdims=True)
    normed = ((grouped - center) * lax.rsqrt(spread + 1e-05)).reshape(batch, rows, cols, chans)
    return jax.nn.silu(normed * gain + shift)


def make_patches(act):
    batch, rows, cols, chans = act.shape
    padded = jnp.pad(act, ((0, 0), (1, 1), (1, 1), (0, 0)))
    taps = []
    for ky in range(3):
        for kx in range(3):
            taps.append(padded[:, ky : ky + rows : 2, kx : kx + cols : 2, :])
    stacked = jnp.concatenate(taps, axis=3)
    return stacked.reshape(batch * (rows // 2) * (cols // 2), 9 * chans)


def fold_patches(dcols, batch, rows, cols, chans):
    parts = dcols.reshape(batch, rows // 2, cols // 2, 9, chans)
    total = jnp.zeros((batch, rows + 2, cols + 2, chans), jnp.float32)
    zero = jnp.zeros((), jnp.float32)
    for ky in range(3):
        for kx in range(3):
            piece = parts[:, :, :, 3 * ky + kx, :]
            total = total + lax.pad(
                piece, zero, ((0, 0, 0), (ky, 3 - ky, 1), (kx, 3 - kx, 1), (0, 0, 0))
            )
    return total[:, 1 : rows + 1, 1 : cols + 1, :]


def local(images, kernel, gn_gain, gn_bias, conv_bias, cotangent):
    count, side, _, channels = images.shape
    out_chans = cotangent.shape[3]
    full = lax.all_gather(kernel, "shard", axis=0, tiled=True)
    act, pull = jax.vjp(lambda v: norm_act(v, gn_gain, gn_bias), images.astype(jnp.float32))
    columns = make_patches(act.astype(jnp.bfloat16))
    result = (jnp.dot(columns, full, preferred_element_type=jnp.float32) + conv_bias).astype(
        jnp.bfloat16
    )
    grad_out = cotangent.reshape(-1, out_chans)
    dcols = lax.dot_general(
        grad_out, full, (((1,), (1,)), ((), ())), preferred_element_type=jnp.float32
    )
    dact = fold_patches(dcols, count, side, side, channels)
    input_grad = pull(dact)[0].astype(jnp.bfloat16)
    shard_count = lax.axis_size("shard")
    rep_count = lax.axis_size("rep")
    total_images = count * shard_count * rep_count
    summed = lax.psum_scatter(
        lax.dot_general(
            columns, grad_out, (((0,), (0,)), ((), ())), preferred_element_type=jnp.float32
        ),
        "shard",
        scatter_dimension=0,
        tiled=True,
    )
    summed = lax.psum(summed, "rep")
    bias_sum = lax.psum(jnp.sum(grad_out.astype(jnp.float32), axis=0), ("rep", "shard"))
    outputs = result.reshape(count, side // 2, side // 2, out_chans)
    return (outputs, input_grad, summed / total_images, bias_sum / total_images)


def solution(mesh):
    return jax.shard_map(
        local,
        mesh=mesh,
        in_specs=(
            P(("rep", "shard"), None, None, None),
            P("shard", None),
            P(),
            P(),
            P(),
            P(("rep", "shard"), None, None, None),
        ),
        out_specs=(
            P(("rep", "shard"), None, None, None),
            P(("rep", "shard"), None, None, None),
            P("shard", None),
            P(),
        ),
        check_vma=False,
    )
```

profile of v0, /device:TPU:8, one launch (start us, length us, event | category | flops | bytes accessed | tf_op | source)
XLA Modules:
  0.0 521.8 jit_solution(1409937052220931734)
XLA Ops:
  10.4 87.0 %all-gather.2.cloned.1.call-done = bf16[9216,512]{1,0:T(8,128)(2,1)} async-done(((bf16[288,512]{1,0:T(8,128)(2,1)}), bf16[9216,512]{1,0:T(8,128)(2,1)}) %all-gather.2.cloned.1.call-update) | async-done | bytes 9437200 | tf_op jit(solution)/shard_map/all_gather | solution.py:45
  97.4 6.8 %fusion.28 = f32[2,8,8,9,1024]{4,2,3,1,0:T(8,128)S(1)} fusion(bf16[9,1024,512,1,1]{2,1,0,4,3:T(8,128)(2,1)} %bitcast.55, bf16[2,8,8,512]{3,2,1,0:T(8,128)(2,1)S(1)} %copy-done.11), kind=kOutput, calls=%fused_computation.47 | convolution fusion | flops 1207959552 | bytes 14286848 | tf_op jit(solution)/shard_map/dot_general | solution.py:52
  106.5 6.4 %pad.46 = f32[2,16,16,1024]{3,2,1,0:T(8,128)S(1)} pad(f32[2,8,8,1024]{3,2,1,0:T(8,128)} %get-tuple-element.14, f32[]{:T(128)} %constant.18.clone.1), padding=0_0_0x1_0_1x1_0_1x0_0_0 | pad | bytes 2621444 | tf_op jit(solution)/shard_map/slice | solution.py:39
  112.9 9.6 %pad.45 = f32[2,16,16,1024]{3,2,1,0:T(8,128)} pad(f32[2,8,8,1024]{3,2,1,0:T(8,128)} %get-tuple-element.15, f32[]{:T(128)} %constant.18.clone.1), padding=0_0_0x1_0_1x0_1_1x0_0_0 | pad | bytes 2621444 | tf_op jit(solution)/shard_map/slice | solution.py:39
  122.5 9.7 %pad.43 = f32[2,16,16,1024]{3,2,1,0:T(8,128)} pad(f32[2,8,8,1024]{3,2,1,0:T(8,128)} %get-tuple-element.9, f32[]{:T(128)} %constant.18.clone.1), padding=0_0_0x0_1_1x1_0_1x0_0_0 | pad | bytes 2621444 | tf_op jit(solution)/shard_map/slice | solution.py:39
  132.2 9.6 %pad.42 = f32[2,16,16,1024]{3,2,1,0:T(8,128)} pad(f32[2,8,8,1024]{3,2,1,0:T(8,128)} %get-tuple-element.10, f32[]{:T(128)} %constant.18.clone.1), padding=0_0_0x0_1_1x0_1_1x0_0_0 | pad | bytes 2621444 | tf_op jit(solution)/shard_map/slice | solution.py:39
  141.8 10.2 %pad.34 = f32[2,18,18,1024]{3,2,1,0:T(8,128)} pad(f32[2,8,8,1024]{3,2,1,0:T(8,128)} %get-tuple-element.12, f32[]{:T(128)} %constant.18.clone.1), padding=0_0_0x0_3_1x2_1_1x0_0_0 | pad | bytes 3178500 | tf_op jit(solution)/shard_map/pad | solution.py:36
  152.0 10.2 %pad.32 = f32[2,18,18,1024]{3,2,1,0:T(8,128)} pad(f32[2,8,8,1024]{3,2,1,0:T(8,128)} %get-tuple-element.13, f32[]{:T(128)} %constant.18.clone.1), padding=0_0_0x0_3_1x0_3_1x0_0_0 | pad | bytes 3178500 | tf_op jit(solution)/shard_map/pad | solution.py:36
  162.3 10.3 %pad.33 = f32[2,18,18,1024]{3,2,1,0:T(8,128)} pad(f32[2,8,8,1024]{3,2,1,0:T(8,128)} %get-tuple-element.7, f32[]{:T(128)} %constant.18.clone.1), padding=0_0_0x0_3_1x1_2_1x0_0_0 | pad | bytes 3178500 | tf_op jit(solution)/shard_map/pad | solution.py:36
  172.6 10.2 %pad.48 = f32[2,16,17,1024]{3,2,1,0:T(8,128)} pad(f32[2,8,8,1024]{3,2,1,0:T(8,128)} %get-tuple-element.11, f32[]{:T(128)} %constant.18.clone.1), padding=0_0_0x0_1_1x0_2_1x0_0_0 | pad | bytes 2752516
  182.7 10.1 %pad.47 = f32[2,16,17,1024]{3,2,1,0:T(8,128)} pad(f32[2,8,8,1024]{3,2,1,0:T(8,128)} %get-tuple-element.8, f32[]{:T(128)} %constant.18.clone.1), padding=0_0_0x1_0_1x0_2_1x0_0_0 | pad | bytes 2752516
  192.9 5.5 %add_add_fusion = f32[2,18,18,1024]{3,2,1,0:T(8,128)S(1)} fusion(f32[2,18,18,1024]{3,2,1,0:T(8,128)} %pad.34, f32[2,18,18,1024]{3,2,1,0:T(8,128)} %pad.32, f32[2,18,18,1024]{3,2,1,0:T(8,128)} %pad.33), kind=kLoop, calls=%fused_computation.1 | loop fusion | flops 1327104 | bytes 10616832 | tf_op jit(solution)/shard_map/add | solution.py:36
  205.1 5.1 slice.57
  210.2 5.1 slice.58
  215.3 5.1 slice.59
  220.4 5.0 slice.60
  225.4 5.0 slice.61
  230.4 5.1 slice.62
  235.5 5.0 slice.63
  247.6 7.8 %convolution_bitcast_fusion = f32[9216,512]{1,0:T(8,128)} fusion(bf16[2,8,8,9216]{3,2,1,0:T(8,128)(2,1)S(1)} %constant_dynamic-update-slice_fusion, bf16[2,8,8,512]{3,2,1,0:T(8,128)(2,1)S(1)} %copy-done.11), kind=kOutput, calls=%fused_computation | convolution fusion | flops 1207959552 | bytes 21364736 | tf_op jit(solution)/shard_map/dot_general | solution.py:61
  255.5 75.2 %psum.15 = f32[512]{0:T(512)S(1)} all-reduce(f32[512]{0:T(512)S(1)} %convert_reduce_fusion.1), channel_id=1, replica_groups=mesh['rep'=8,'shard'=32] {'rep','shard'}, use_global_device_ids=true, to_apply=%region_13.14 | all-reduce | flops 512 | bytes 4096 | tf_op jit(solution)/shard_map/psum | solution.py:69
  334.0 97.4 %reduce-scatter.2.cloned.1.call-done = f32[288,512]{1,0:T(8,128)} async-done(((f32[9216,512]{1,0:T(8,128)}), f32[288,512]{1,0:T(8,128)}) %reduce-scatter.2.cloned.1.call-update) | async-done | bytes 589840 | tf_op jit(solution)/shard_map/reduce_scatter | solution.py:60
  431.4 6.5 %fusion.27 = bf16[128,512]{1,0:T(8,128)(2,1)} fusion(bf16[128,9216]{1,0:T(8,128)(2,1)} %bitcast.56, bf16[9216,512]{1,0:T(8,128)(2,1)} %all-gather.2.cloned.1.call-done, f32[512]{0:T(512)S(1)} %copy-done.14), kind=kOutput, calls=%fused_computation.35 | convolution fusion | flops 1208090624 | bytes 11929600 | tf_op jit(solution)/shard_map/dot_general | solution.py:48
  437.8 75.5 %all-reduce.12.cloned.1.call-done = f32[288,512]{1,0:T(8,128)} async-done(((f32[288,512]{1,0:T(8,128)}), f32[288,512]{1,0:T(8,128)}) %all-reduce.12.cloned.1.call-update) | async-done | bytes 589840 | tf_op jit(solution)/shard_map/psum | solution.py:68
  (79 shorter events, 24.3 us)
Async XLA Ops:
  7.2 2.6 copy-start
  7.2 90.2 %copy-start.11 = (bf16[2,8,8,512]{3,2,1,0:T(8,128)(2,1)S(1)}, bf16[2,8,8,512]{3,2,1,0:T(8,128)(2,1)}, u32[]{:S(2)}) copy-start(bf16[2,8,8,512]{3,2,1,0:T(8,128)(2,1)} %param.11) | copy-start | bytes 393220
  7.2 90.2 %all-gather.2.cloned.1.call-start = ((), (), s32[]{:S(2)}) async-start(), calls=%async_computation.1 | async-start | bytes 9732096 | tf_op jit(solution)/shard_map/all_gather | solution.py:45
  7.9 423.4 %reduce-scatter.2.cloned.1.call-start = ((), (), s32[]{:S(2)}) async-start(), calls=%async_computation.2 | async-start | bytes 19464192 | tf_op jit(solution)/shard_map/reduce_scatter | solution.py:60
  192.8 5.6 %copy-start.1 = (f32[2,16,17,1024]{3,2,1,0:T(8,128)S(1)}, f32[2,16,17,1024]{3,2,1,0:T(8,128)}, u32[]{:S(2)}) copy-start(f32[2,16,17,1024]{3,2,1,0:T(8,128)} %pad.48) | copy-start | bytes 6684676
  192.8 5.9 %copy-start.2 = (f32[2,16,17,1024]{3,2,1,0:T(8,128)S(1)}, f32[2,16,17,1024]{3,2,1,0:T(8,128)}, u32[]{:S(2)}) copy-start(f32[2,16,17,1024]{3,2,1,0:T(8,128)} %pad.47) | copy-start | bytes 6684676
  192.8 6.5 %copy-start.4 = (f32[2,16,16,1024]{3,2,1,0:T(8,128)S(1)}, f32[2,16,16,1024]{3,2,1,0:T(8,128)}, u32[]{:S(2)}) copy-start(f32[2,16,16,1024]{3,2,1,0:T(8,128)} %pad.45) | copy-start | bytes 6291460
  192.8 7.1 %copy-start.5 = (f32[2,16,16,1024]{3,2,1,0:T(8,128)S(1)}, f32[2,16,16,1024]{3,2,1,0:T(8,128)}, u32[]{:S(2)}) copy-start(f32[2,16,16,1024]{3,2,1,0:T(8,128)} %pad.43) | copy-start | bytes 6291460
  192.8 7.7 %copy-start.6 = (f32[2,16,16,1024]{3,2,1,0:T(8,128)S(1)}, f32[2,16,16,1024]{3,2,1,0:T(8,128)}, u32[]{:S(2)}) copy-start(f32[2,16,16,1024]{3,2,1,0:T(8,128)} %pad.42) | copy-start | bytes 6291460
  192.8 7.7 %copy-start.12 = (f32[1024]{0:T(1024)S(1)}, f32[1024]{0:T(1024)}, u32[]{:S(2)}) copy-start(f32[1024]{0:T(1024)} %param.9) | copy-start | bytes 12292
  192.8 7.7 %copy-start.13 = (f32[1024]{0:T(1024)S(1)}, f32[1024]{0:T(1024)}, u32[]{:S(2)}) copy-start(f32[1024]{0:T(1024)} %param.8) | copy-start | bytes 12292
  241.9 4.0 copy-start.10
  241.9 4.0 copy-start.9
  241.9 4.0 copy-start.8
  246.0 1.5 copy-start.7
  255.4 77.2 %copy-start.3 = (f32[2,16,16,1024]{3,2,1,0:T(8,128)S(1)}, f32[2,16,16,1024]{3,2,1,0:T(8,128)}, u32[]{:S(2)}) copy-start(f32[2,16,16,1024]{3,2,1,0:T(8,128)} %get-tuple-element.6) | copy-start | bytes 6291460
  255.4 258.0 %all-reduce.12.cloned.1.call-start = ((), (), s32[]{:S(2)}) async-start(), calls=%async_computation.3 | async-start | bytes 1179648 | tf_op jit(solution)/shard_map/psum | solution.py:68
  332.5 98.8 %copy-start.14 = (f32[512]{0:T(512)S(1)}, f32[512]{0:T(512)}, u32[]{:S(2)}) copy-start(f32[512]{0:T(512)} %param.10) | copy-start | bytes 6148
Sparse Core Ops, SparseCore 0:
  10.6 86.7 all-gather.1
  255.5 175.7 reduce-scatter.1
  434.2 79.1 all-reduce.11
where the time goes:
time: 530 us; the launch traced here: 522 us
  waiting for transfers between devices  261 us (49%)
  local copies, waits for them, and re-layouts  135 us (25%)
  blocking collectives  75.2 us (14%)
  matrix products  21.1 us (4%)
  other arithmetic  16 us (3%)
  between operations  14.1 us (3%)
    reduce_scatter x1, waiting for transfers between devices, local(): lax.psum_scatter(lax.dot_general(columns, grad_out, (((0,), (0,)), ((), (...  97.4 us
    all_gather x1, waiting for transfers between devices, local(): full = lax.all_gather(kernel, 'shard', axis=0, tiled=True)  87 us
    psum x1, waiting for transfers between devices, local(): summed = lax.psum(summed, 'rep')  75.5 us
    psum x1, blocking collectives, local(): lax.psum(jnp.sum(grad_out.astype(jnp.float32), axis=0), ('rep', 'shard'))  75.2 us
    slice x9, local copies, waits for them, and re-layouts, make_patches(): taps.append(padded[:, ky:ky + rows:2, kx:kx + cols:2, :])  36.7 us
    slice x4, local copies, waits for them, and re-layouts, fold_patches(): return total[:, 1:rows + 1, 1:cols + 1, :]  35.4 us
    pad x3, local copies, waits for them, and re-layouts, fold_patches(): lax.pad(piece, zero, ((0, 0, 0), (ky, 3 - ky, 1), (kx, 3 - kx, 1), (0, 0,...  30.7 us
    unnamed x40, local copies, waits for them, and re-layouts  28 us
  transfers between devices with their start and end apart: 3, of which 3 were waited for; matrix products, arithmetic and copies ran while one was open for 2% of the time, Pallas kernels for 0%

commit v1 on v0

v1 whole, which is shorter than its diff:
```python
import functools

import jax
import jax.numpy as jnp
from jax import lax
from jax.experimental import pallas as pl
from jax.experimental.pallas import tpu as pltpu
from jax.sharding import PartitionSpec as P

BF = jnp.bfloat16
F32 = jnp.float32
AXES = ("rep", "shard")
CIN, COUT, HALF = 1024, 512, 256
GSIZE = 32
IMAGES = 512
EPS = 1e-05
VMEM_MB = 56 * 1024 * 1024
CHUNK, PER_CHIP, NA, NB, QA, QB = 16, 36, 16, 20, 4, 5
TAPS = [(ky, kx) for ky in range(3) for kx in range(3)]


def source(k):
    return (0, 0) if k == 1 else (1, 1 if k == 0 else 0)


def position():
    rep, shard = lax.axis_index("rep"), lax.axis_index("shard")
    return lax.rem(rep, 4), lax.rem(shard // 2, 4), shard // 8, lax.rem(shard, 2)


def number(x, y, z, core):
    return ((z % 2) * 4 + x) * 32 + ((z // 2) * 4 + y) * 2 + core


@functools.lru_cache(maxsize=None)
def pairs(dx, dy, dz, swap):
    out = []
    for x in range(4):
        for y in range(4):
            for z in range(8):
                for core in range(2):
                    src = number((x + dx) % 4, (y + dy) % 4, (z + dz) % 8, core ^ swap)
                    out.append((src, number(x, y, z, core)))
    return sorted(out)


def fetch(value, dx=0, dy=0, dz=0, swap=0):
    return lax.ppermute(value, AXES, pairs(dx, dy, dz, swap))


def pair_low(value):
    out = []
    for x in range(4):
        for y in range(4):
            for z in range(8):
                for core in range(2):
                    out.append((number(x, y, z ^ 1, core), number(x, y, z, core)))
    return lax.ppermute(value, AXES, sorted(out))


def turn(index, step):
    return lax.rem(index + step, 4)


def call(body, outs, args, flops=0, moved=None, scratch=(), specs=None, out_specs=None, grid=None, **kw):
    if moved is None:
        moved = sum(a.size * a.dtype.itemsize for a in args) + sum(
            o.size * o.dtype.itemsize for o in outs
        )
    params = dict(kw)
    if grid is not None:
        params["grid"] = grid
    if specs is not None:
        params["in_specs"] = specs
    if out_specs is not None:
        params["out_specs"] = out_specs
    return pl.pallas_call(
        body,
        out_shape=outs,
        scratch_shapes=list(scratch),
        compiler_params=pltpu.CompilerParams(vmem_limit_bytes=VMEM_MB),
        cost_estimate=pl.CostEstimate(flops=flops, bytes_accessed=moved, transcendentals=0),
        **params,
    )(*args)


def arr(shape, dtype):
    return jax.ShapeDtypeStruct(shape, dtype)


def group_mean(rows):
    a = lax.broadcasted_iota(jnp.int32, (128, 128), 0) // GSIZE
    b = lax.broadcasted_iota(jnp.int32, (128, 128), 1) // GSIZE
    ones = jnp.where(a == b, 1.0, 0.0).astype(F32)
    total = lax.dot_general(
        rows,
        ones,
        (((1,), (0,)), ((), ())),
        precision=lax.Precision.HIGHEST,
        preferred_element_type=F32,
    )
    return total * (1.0 / (256 * GSIZE))


def stack_rows(a, b):
    row = lax.broadcasted_iota(jnp.int32, (8, 128), 0)
    return jnp.where(row == 0, a, jnp.where(row == 1, b, 0.0))


def norm_body(x_ref, gain_ref, bias_ref, act_ref, plane_ref, stat_ref, buf):
    x = x_ref[...].astype(F32).reshape(2, 256, 128)
    sums = [jnp.sum(x[i], axis=0, keepdims=True) for i in range(2)]
    mean = group_mean(stack_rows(*sums))
    sq = [jnp.sum(jnp.square(x[i] - mean[i : i + 1]), axis=0, keepdims=True) for i in range(2)]
    rstd = lax.rsqrt(group_mean(stack_rows(*sq)) + EPS)
    stat_ref[0] = mean
    stat_ref[1] = rstd
    buf[...] = x.reshape(512, 128)
    gain, bias = gain_ref[...], bias_ref[...]
    for pj in range(2):
        part = buf[pl.ds(pj, 256, stride=2), :].reshape(2, 8, 2, 64 // 8, 128)
        for pi in range(2):
            for i in range(2):
                xp = part[i, :, pi].reshape(64, 128)
                y = (xp - mean[i : i + 1]) * rstd[i : i + 1] * gain + bias
                rows = slice(64 * i, 64 * i + 64)
                act_ref[2 * pi + pj, rows, :] = (y * jax.nn.sigmoid(y)).astype(BF)
                plane_ref[2 * pi + pj, rows, :] = xp.astype(BF)


def norm_forward(images, gain, bias):
    plane = arr((4, 128, CIN), BF)
    vec = pl.BlockSpec((1, 128), lambda c: (0, c))
    block = pl.BlockSpec((4, 128, 128), lambda c: (0, 0, c))
    return call(
        norm_body,
        (plane, plane, arr((2, 8, CIN), F32)),
        (images, gain.reshape(1, CIN), bias.reshape(1, CIN)),
        flops=20 * images.size,
        scratch=(pltpu.VMEM((512, 128), F32),),
        grid=(CIN // 128,),
        specs=[pl.BlockSpec((2, 16, 16, 128), lambda c: (0, 0, 0, c)), vec, vec],
        out_specs=(block, block, pl.BlockSpec((2, 8, 128), lambda c: (0, 0, c))),
    )


def norm_back_body(xp_ref, own_ref, got_ref, gain_ref, bias_ref, stat_ref, out_ref, buf):
    gain, bias = gain_ref[...], bias_ref[...]
    mean, rstd = stat_ref[0], stat_ref[1]
    hats, grads, one, two = [], [], [], []
    for i in range(2):
        rows = slice(64 * i, 64 * i + 64)
        m, r = mean[i : i + 1], rstd[i : i + 1]
        h_list, g_list, s1, s2 = [], [], 0.0, 0.0
        for p in range(4):
            hat = (xp_ref[p, rows, :].astype(F32) - m) * r
            y = hat * gain + bias
            s = jax.nn.sigmoid(y)
            d = own_ref[p, rows, :] + got_ref[p, rows, :]
            g = d * (s * (1.0 + y * (1.0 - s))) * gain
            s1 = s1 + jnp.sum(g, axis=0, keepdims=True)
            s2 = s2 + jnp.sum(g * hat, axis=0, keepdims=True)
            h_list.append(hat)
            g_list.append(g)
        hats.append(h_list)
        grads.append(g_list)
        one.append(s1)
        two.append(s2)
    mean1 = group_mean(stack_rows(*one))
    mean2 = group_mean(stack_rows(*two))
    for pj in range(2):
        parts = []
        for i in range(2):
            both = []
            for pi in range(2):
                p = 2 * pi + pj
                dx = rstd[i : i + 1] * (
                    grads[i][p] - mean1[i : i + 1] - hats[i][p] * mean2[i : i + 1]
                )
                both.append(dx.reshape(8, 1, 8, 128))
            parts.append(jnp.concatenate(both, axis=1).reshape(128, 128))
        buf[pl.ds(pj, 256, stride=2), :] = jnp.concatenate(parts, axis=0)
    out_ref[...] = buf[...].astype(BF).reshape(2, 16, 16, 128)


def norm_backward(planes, own, got, gain, bias, stat):
    vec = pl.BlockSpec((1, 128), lambda c: (0, c))
    block = pl.BlockSpec((4, 128, 128), lambda c: (0, 0, c))
    return call(
        norm_back_body,
        (arr((2, 16, 16, CIN), BF),),
        (planes, own, got, gain.reshape(1, CIN), bias.reshape(1, CIN), stat),
        flops=40 * planes.size,
        scratch=(pltpu.VMEM((512, 128), F32),),
        grid=(CIN // 128,),
        specs=[block, block, block, vec, vec, pl.BlockSpec((2, 8, 128), lambda c: (0, 0, c))],
        out_specs=(pl.BlockSpec((2, 16, 16, 128), lambda c: (0, 0, 0, c)),),
    )[0]


def shifted(cot, si, sj):
    row = lax.broadcasted_iota(jnp.int32, cot.shape, 0)
    value = cot
    if sj:
        value = jnp.where(row % 8 == 7, 0.0, pltpu.roll(value, cot.shape[0] - 1, 0))
    if si:
        value = jnp.where((row // 8) % 8 == 7, 0.0, pltpu.roll(value, cot.shape[0] - 8, 0))
    return value


def delayed(acc, si, sj):
    row = lax.broadcasted_iota(jnp.int32, acc.shape, 0)
    value = acc
    if sj:
        value = jnp.where(row % 8 == 0, 0.0, pltpu.roll(value, 1, 0))
    if si:
        value = jnp.where((row // 8) % 8 == 0, 0.0, pltpu.roll(value, 8, 0))
    return value


def cot_rows(own_ref, got_ref):
    return jnp.concatenate([own_ref[...], got_ref[...]], axis=0).astype(F32)


def wgrad_body(act_own, act_got, cot_own, cot_got, *refs):
    outs_a, outs_b = refs[:4], refs[4:8]
    whole, tail, sem = refs[8], refs[9], refs[10]
    x, y, _, _ = position()
    cot = cot_rows(cot_own, cot_got)
    moved = {(si, sj): shifted(cot, si, sj).astype(BF) for si in range(2) for sj in range(2)}
    for t, (ky, kx) in enumerate(TAPS):
        (pi, si), (pj, sj) = source(ky), source(kx)
        act = jnp.concatenate([act_own[2 * pi + pj], act_got[2 * pi + pj]], axis=0)
        grad = lax.dot_general(
            act, moved[si, sj], (((0,), (0,)), ((), ())), preferred_element_type=F32
        ).astype(BF)
        for q in range(16):
            n = t * 64 + 4 * q
            r, k = n // PER_CHIP, n % PER_CHIP
            whole[r // 4, r % 4, k : k + 4] = grad[64 * q : 64 * q + 64].reshape(4, CHUNK, HALF)
    bias = jnp.sum(cot, axis=0, keepdims=True)
    high = bias.astype(BF).astype(F32)
    low = bias - high
    row = lax.broadcasted_iota(jnp.int32, (CHUNK, HALF), 0)
    tail[0] = jnp.where(row == 0, high, jnp.where(row == 1, low, 0.0)).astype(BF)
    copies = []
    for d in range(4):
        there = turn(x, d)
        copies.append(
            pltpu.make_async_copy(
                whole.at[:, :, pl.ds(QA * there, QA)], outs_a[d], sem.at[len(copies)]
            )
        )
        there = turn(y, d)
        for z in range(4):
            copies.append(
                pltpu.make_async_copy(
                    whole.at[z, there, pl.ds(NA, NB)],
                    outs_b[d].at[pl.ds(NB * z, NB)],
                    sem.at[len(copies)],
                )
            )
        copies.append(
            pltpu.make_async_copy(tail, outs_b[d].at[pl.ds(4 * NB, 1)], sem.at[len(copies)])
        )
    for copy in copies:
        copy.start()
    for copy in copies:
        copy.wait()


def wgrad(act_own, act_got, cot_own, cot_got):
    vm = pl.BlockSpec(memory_space=pltpu.VMEM)
    hbm = pl.BlockSpec(memory_space=pl.ANY)
    outs = (arr((4, 4, QA, CHUNK, HALF), BF),) * 4 + (arr((4 * NB + 1, CHUNK, HALF), BF),) * 4
    res = call(
        wgrad_body,
        outs,
        (act_own, act_got, cot_own, cot_got),
        flops=2 * 256 * 9216 * HALF,
        scratch=(
            pltpu.VMEM((4, 4, PER_CHIP, CHUNK, HALF), BF),
            pltpu.VMEM((1, CHUNK, HALF), BF),
            pltpu.SemaphoreType.DMA((24,)),
        ),
        specs=[vm] * 4,
        out_specs=(hbm,) * 8,
    )
    return res[:4], res[4:]


def conv_body(*refs):
    ka, kb = refs[:4], refs[4:8]
    act_own, act_got, cot_own, cot_got, cbias = refs[8:13]
    out_own, out_other, dact_own, dact_other = refs[13:17]
    whole, sem = refs[17], refs[18]
    x, y, _, _ = position()
    copies = []
    for d in range(4):
        copies.append(
            pltpu.make_async_copy(
                ka[d], whole.at[:, :, pl.ds(QA * turn(x, d), QA)], sem.at[2 * d]
            )
        )
        copies.append(
            pltpu.make_async_copy(
                kb[d], whole.at[:, turn(y, d), pl.ds(NA, NB)], sem.at[2 * d + 1]
            )
        )
    for copy in copies:
        copy.start()
    cot = cot_rows(cot_own, cot_got)
    moved = {(si, sj): shifted(cot, si, sj).astype(BF) for si in range(2) for sj in range(2)}
    for copy in copies:
        copy.wait()

    def tap(t):
        parts = []
        for q in range(16):
            n = t * 64 + 4 * q
            r, k = n // PER_CHIP, n % PER_CHIP
            parts.append(whole[r // 4, r % 4, k : k + 4].reshape(64, HALF))
        return jnp.concatenate(parts, axis=0)

    total = None
    for si in range(2):
        for sj in range(2):
            acc = None
            for t, (ky, kx) in enumerate(TAPS):
                (pi, a), (pj, b) = source(ky), source(kx)
                if (a, b) != (si, sj):
                    continue
                act = jnp.concatenate([act_own[2 * pi + pj], act_got[2 * pi + pj]], axis=0)
                term = jnp.dot(act, tap(t), preferred_element_type=F32)
                acc = term if acc is None else acc + term
            acc = delayed(acc, si, sj)
            total = acc if total is None else total + acc
    result = (total + cbias[...]).astype(BF)
    out_own[...] = result[:128]
    out_other[...] = result[128:]
    for pi in range(2):
        for pj in range(2):
            acc = None
            for t, (ky, kx) in enumerate(TAPS):
                (a, si), (b, sj) = source(ky), source(kx)
                if (a, b) != (pi, pj):
                    continue
                term = lax.dot_general(
                    moved[si, sj], tap(t), (((1,), (1,)), ((), ())), preferred_element_type=F32
                )
                acc = term if acc is None else acc + term
            dact_own[2 * pi + pj] = acc[:128]
            dact_other[2 * pi + pj] = acc[128:]


def conv(ka, kb, act_own, act_got, cot_own, cot_got, cbias):
    vm = pl.BlockSpec(memory_space=pltpu.VMEM)
    hbm = pl.BlockSpec(memory_space=pl.ANY)
    out, dact = arr((128, HALF), BF), arr((4, 128, CIN), F32)
    return call(
        conv_body,
        (out, out, dact, dact),
        (*ka, *kb, act_own, act_got, cot_own, cot_got, cbias),
        flops=4 * 256 * 9216 * HALF,
        scratch=(
            pltpu.VMEM((4, 4, PER_CHIP, CHUNK, HALF), BF),
            pltpu.SemaphoreType.DMA((8,)),
        ),
        specs=[hbm] * 8 + [vm] * 5,
        out_specs=(vm,) * 4,
    )


def spread_z_body(a0, a1, a2, a3, a_ref, b_ref):
    _, _, z, _ = position()
    for d, ref in enumerate((a0, a1, a2, a3)):
        there = turn(z, d)
        a_ref[there] = ref[:QA]
        b_ref[there] = ref[QA:]


def spread_xy_body(a0, a1, a2, a3, b0, b1, b2, b3, a_ref, b_ref):
    x, y, _, _ = position()
    for d, (a, b) in enumerate(((a0, b0), (a1, b1), (a2, b2), (a3, b3))):
        there = turn(y, d)
        for z in range(4):
            a_ref[z, there] = a[z]
        there = turn(x, d)
        for z in range(4):
            b_ref[z, pl.ds(QB * there, QB)] = b[z]


def gather_kernel(kernel, core):
    halves = kernel.reshape(18, CHUNK, COUT)
    left, right = halves[:, :, :HALF], halves[:, :, HALF:]
    mine = jnp.where(core == 0, left, right)
    theirs = fetch(jnp.where(core == 0, right, left), swap=1)
    block = jnp.concatenate(
        [jnp.where(core == 0, mine, theirs), jnp.where(core == 0, theirs, mine)], axis=0
    )
    x = position()[0]
    piece = jnp.concatenate(
        [
            lax.dynamic_slice_in_dim(block, QA * x, QA, 0),
            lax.dynamic_slice_in_dim(block, NA + QB * x, QB, 0),
        ],
        axis=0,
    )
    got = [piece] + [fetch(piece, dz=2 * d) for d in range(1, 4)]
    a, b = call(
        spread_z_body, (arr((4, QA, CHUNK, HALF), BF), arr((4, QB, CHUNK, HALF), BF)), got
    )
    got_a = [a] + [fetch(a, dy=d) for d in range(1, 4)]
    got_b = [b] + [fetch(b, dx=d) for d in range(1, 4)]
    a, b = call(
        spread_xy_body,
        (arr((4, 4, QA, CHUNK, HALF), BF), arr((4, NB, CHUNK, HALF), BF)),
        (*got_a, *got_b),
    )
    ka = [a] + [fetch(a, dx=d) for d in range(1, 4)]
    kb = [b] + [fetch(b, dy=d) for d in range(1, 4)]
    return ka, kb


def four(refs, index):
    v = [ref[index].astype(F32) for ref in refs]
    return (v[0] + v[2]) + (v[1] + v[3])


def bias_four(refs, index):
    v = [ref[index].astype(F32) for ref in refs]
    v = [w[0:1] + w[1:2] for w in v]
    return (v[0] + v[2]) + (v[1] + v[3])


def bias_chunk(total):
    high = total.astype(BF).astype(F32)
    row = lax.broadcasted_iota(jnp.int32, (CHUNK, HALF), 0)
    return jnp.where(row == 0, high, jnp.where(row == 1, total - high, 0.0)).astype(BF)


def sum_xy_body(*refs):
    a, b = refs[:4], refs[4:8]
    out_a, out_b = refs[8:12], refs[12:16]
    x, y, _, _ = position()
    bias = bias_chunk(bias_four(b, 4 * NB))
    for d in range(4):
        there = turn(y, d)
        for z in range(4):
            out_a[d][z] = four(a, (z, there)).astype(BF)
        there = turn(x, d)
        for z in range(4):
            out_b[d][QB * z : QB * z + QB] = four(b, pl.ds(NB * z + QB * there, QB)).astype(BF)
        out_b[d][4 * QB] = bias


def sum_yx_body(*refs):
    a, b = refs[:4], refs[4:8]
    outs = refs[8:12]
    _, _, z, _ = position()
    bias = bias_chunk(bias_four(b, 4 * QB))
    for d in range(4):
        there = turn(z, d)
        outs[d][:QA] = four(a, there).astype(BF)
        outs[d][QA : QA + QB] = four(b, pl.ds(QB * there, QB)).astype(BF)
        outs[d][QA + QB] = bias


def sum_z_body(*refs):
    ins, out = refs[:4], refs[4]
    out[: QA + QB] = four(ins, pl.ds(0, QA + QB))
    row = lax.broadcasted_iota(jnp.int32, (CHUNK, HALF), 0)
    out[QA + QB] = jnp.where(row == 0, bias_four(ins, QA + QB), 0.0)


def place_body(f0, f1, f2, f3, mine, theirs, whole):
    x, _, _, core = position()
    for d, ref in enumerate((f0, f1, f2, f3)):
        there = turn(x, d)
        whole[pl.ds(QA * there, QA)] = ref[:QA]
        whole[pl.ds(NA + QB * there, QB)] = ref[QA : QA + QB]
    mine[:18] = whole[pl.ds(18 * core, 18)]
    theirs[:18] = whole[pl.ds(18 * (1 - core), 18)]
    mine[18] = f0[QA + QB]
    theirs[18] = f0[QA + QB]


def reduce_gradient(send_a, send_b, core):
    a = [send_a[0]] + [fetch(send_a[4 - d], dx=d) for d in range(1, 4)]
    b = [send_b[0]] + [fetch(send_b[4 - d], dy=d) for d in range(1, 4)]
    res = call(
        sum_xy_body,
        (arr((4, QA, CHUNK, HALF), BF),) * 4 + (arr((4 * QB + 1, CHUNK, HALF), BF),) * 4,
        (*a, *b),
    )
    send_a, send_b = res[:4], res[4:]
    a = [send_a[0]] + [fetch(send_a[4 - d], dy=d) for d in range(1, 4)]
    b = [send_b[0]] + [fetch(send_b[4 - d], dx=d) for d in range(1, 4)]
    send = call(sum_yx_body, (arr((QA + QB + 1, CHUNK, HALF), BF),) * 4, (*a, *b))
    got = [send[0]] + [fetch(send[4 - d], dz=2 * d) for d in range(1, 4)]
    part = call(sum_z_body, (arr((QA + QB + 1, CHUNK, HALF), F32),), got)[0]
    full = (part + pair_low(part)) * (1.0 / IMAGES)
    rows = full[: QA + QB]
    every = [full] + [fetch(rows, dx=d) for d in range(1, 4)]
    mine, theirs = call(
        place_body,
        (arr((19, CHUNK, HALF), F32),) * 2,
        every,
        scratch=(pltpu.VMEM((PER_CHIP, CHUNK, HALF), F32),),
    )
    got = fetch(theirs, swap=1)
    both = jnp.where(
        core == 0, jnp.concatenate([mine, got], axis=-1), jnp.concatenate([got, mine], axis=-1)
    )
    return both[:18].reshape(288, COUT), both[18, 0]


def local(images, kernel, gn_gain, gn_bias, conv_bias, cotangent):
    core = position()[3]
    cot = cotangent.reshape(128, COUT)
    left, right = cot[:, :HALF], cot[:, HALF:]
    cot_own = jnp.where(core == 0, left, right)
    cot_got = fetch(jnp.where(core == 0, right, left), swap=1)
    ka, kb = gather_kernel(kernel, core)
    act, planes, stat = norm_forward(images, gn_gain, gn_bias)
    act_got = fetch(act, swap=1)
    send_a, send_b = wgrad(act, act_got, cot_own, cot_got)
    kernel_grad, bias_grad = reduce_gradient(send_a, send_b, core)
    cbias = jnp.where(core == 0, conv_bias[:HALF], conv_bias[HALF:]).reshape(1, HALF)
    out_own, out_other, dact_own, dact_other = conv(
        ka, kb, act, act_got, cot_own, cot_got, cbias
    )
    out_got = fetch(out_other, swap=1)
    dact_got = fetch(dact_other, swap=1)
    outputs = jnp.where(
        core == 0,
        jnp.concatenate([out_own, out_got], axis=-1),
        jnp.concatenate([out_got, out_own], axis=-1),
    ).reshape(cotangent.shape)
    input_grad = norm_backward(planes, dact_own, dact_got, gn_gain, gn_bias, stat)
    return outputs, input_grad, kernel_grad, bias_grad


def solution(mesh):
    return jax.shard_map(
        local,
        mesh=mesh,
        in_specs=(
            P(AXES, None, None, None),
            P("shard", None),
            P(),
            P(),
            P(),
            P(AXES, None, None, None),
        ),
        out_specs=(
            P(AXES, None, None, None),
            P(AXES, None, None, None),
            P("shard", None),
            P(),
        ),
        check_vma=False,
    )
```

time: 530 us -> 209 us (0.39)
  the two profiles are of different devices: /device:TPU:8 before, /device:TPU:1 now
where the time goes in v1:
time: 209 us; the launch traced here: 208 us
  waiting for transfers between devices  85.6 us (41%)
  starting transfers between devices  63.6 us (30%)
  Pallas kernels  43.5 us (21%)
  local copies, waits for them, and re-layouts  8.52 us (4%)
  other arithmetic  6.14 us (3%)
    ppermute x39, waiting for transfers between devices, fetch(): return lax.ppermute(value, AXES, pairs(dx, dy, dz, swap))  81.2 us
    ppermute x39, starting transfers between devices, fetch(): return lax.ppermute(value, AXES, pairs(dx, dy, dz, swap))  63.6 us
    pallas_call x10, Pallas kernels, call(): pl.pallas_call(body, out_shape=outs, scratch_shapes=list(scratch), compil...  43.5 us
    unnamed x92, local copies, waits for them, and re-layouts  7.06 us
    ppermute x1, waiting for transfers between devices, pair_low(): return lax.ppermute(value, AXES, sorted(out))  4.38 us
  transfers between devices with their start and end apart: 40, of which 24 were waited for; matrix products, arithmetic and copies ran while one was open for 3% of the time, Pallas kernels for 17%

profile of v1, /device:TPU:1, one launch (start us, length us, event | category | flops | bytes accessed | tf_op | source)
XLA Modules:
  0.0 208.3 jit_solution(8814353438321446209)
XLA Ops:
  1.7 3.3 %collective-permute-start = (bf16[18,16,256]{2,1,0:T(8,128)(2,1)S(1)}, bf16[18,16,256]{2,1,0:T(8,128)(2,1)S(1)}, u32[]{:S(2)}, u32[]{:S(2)}) collective-permute-start(bf16[18,16,256]{2,1,0:T(8,128)(2,1)S(1)} %broadcast_select_fusion.2), channel_id=1, source_target_pairs={{0,1},{1,0},{2,3},{3,2},{4,5},{5,4},{6,7},{7,6},{8,9},{9,8},{10,11... | collective-permute-start | bytes 442376 | tf_op jit(solution)/shard_map/ppermute | solution.py:48
  5.0 7.8 %shard_map.95 = (bf16[4,128,1024]{2,1,0:T(8,128)(2,1)}, bf16[4,128,1024]{2,1,0:T(8,128)(2,1)}, f32[2,8,1024]{2,1,0:T(8,128)}) custom-call(bf16[2,16,16,1024]{3,2,1,0:T(8,128)(2,1)} %x_ref.1, f32[1,1024]{1,0:T(1,128)} %bitcast.15, f32[1,1024]{1,0:T(1,128)} %bitcast.17), custom_call_target="tpu_custom_call" | custom-call | flops 10485760 | bytes 3219456 | tf_op jit(solution)/shard_map/pallas_call | solution.py:77
  15.3 5.1 %collective-permute-start.2 = (bf16[9,16,256]{2,1,0:T(8,128)(2,1)S(1)}, bf16[9,16,256]{2,1,0:T(8,128)(2,1)S(1)}, u32[]{:S(2)}, u32[]{:S(2)}) collective-permute-start(bf16[9,16,256]{2,1,0:T(8,128)(2,1)S(1)} %pad_maximum_fusion.a0), channel_id=1, source_target_pairs={{0,16},{1,17},{2,18},{3,19},{4,20},{5,21},{6,22},{7,23},{8,24},{9,... | collective-permute-start | bytes 221192 | tf_op jit(solution)/shard_map/ppermute | solution.py:48
  20.4 2.4 %collective-permute-start.1 = (bf16[9,16,256]{2,1,0:T(8,128)(2,1)S(1)}, bf16[9,16,256]{2,1,0:T(8,128)(2,1)S(1)}, u32[]{:S(2)}, u32[]{:S(2)}) collective-permute-start(bf16[9,16,256]{2,1,0:T(8,128)(2,1)S(1)} %pad_maximum_fusion.a0), channel_id=1, source_target_pairs={{0,24},{1,25},{2,26},{3,27},{4,28},{5,29},{6,30},{7,31},{8,0},{9,1... | collective-permute-start | bytes 221192 | tf_op jit(solution)/shard_map/ppermute | solution.py:48
  25.1 3.3 %collective-permute-done.1.a1 = bf16[9,16,256]{2,1,0:T(8,128)(2,1)S(1)} collective-permute-done((bf16[9,16,256]{2,1,0:T(8,128)(2,1)S(1)}, bf16[9,16,256]{2,1,0:T(8,128)(2,1)S(1)}, u32[]{:S(2)}, u32[]{:S(2)}) %collective-permute-start.1) | collective-permute-done | bytes 73760 | tf_op jit(solution)/shard_map/ppermute | solution.py:48
  32.1 2.6 %collective-permute-start.5 = (bf16[4,4,16,256]{3,2,1,0:T(8,128)(2,1)}, bf16[4,4,16,256]{3,2,1,0:T(8,128)(2,1)S(1)}, u32[]{:S(2)}, u32[]{:S(2)}) collective-permute-start(bf16[4,4,16,256]{3,2,1,0:T(8,128)(2,1)} %get-tuple-element.37.a0), channel_id=1, source_target_pairs={{0,4},{1,5},{2,6},{3,7},{4,0},{5,1},{6,2},{7,3},{8,12},{9,13},{10,... | collective-permute-start | bytes 393224 | tf_op jit(solution)/shard_map/ppermute | solution.py:48
  36.0 2.5 %collective-permute-start.8 = (bf16[4,5,16,256]{3,2,1,0:T(8,128)(2,1)}, bf16[4,5,16,256]{3,2,1,0:T(8,128)(2,1)S(1)}, u32[]{:S(2)}, u32[]{:S(2)}) collective-permute-start(bf16[4,5,16,256]{3,2,1,0:T(8,128)(2,1)} %get-tuple-element.38.b0), channel_id=1, source_target_pairs={{0,64},{1,65},{2,66},{3,67},{4,68},{5,69},{6,70},{7,71},{8,72},{9,... | collective-permute-start | bytes 491528 | tf_op jit(solution)/shard_map/ppermute | solution.py:48
  40.7 4.3 %collective-permute-done.4.a1 = bf16[4,4,16,256]{3,2,1,0:T(8,128)(2,1)S(1)} collective-permute-done((bf16[4,4,16,256]{3,2,1,0:T(8,128)(2,1)}, bf16[4,4,16,256]{3,2,1,0:T(8,128)(2,1)S(1)}, u32[]{:S(2)}, u32[]{:S(2)}) %collective-permute-start.4) | collective-permute-done | bytes 131104 | tf_op jit(solution)/shard_map/ppermute | solution.py:48
  46.5 2.4 %shard_map.94 = (bf16[4,4,4,16,256]{4,3,2,1,0:T(8,128)(2,1)}, bf16[4,20,16,256]{3,2,1,0:T(8,128)(2,1)}) custom-call(bf16[4,4,16,256]{3,2,1,0:T(8,128)(2,1)} %get-tuple-element.37.a0, bf16[4,4,16,256]{3,2,1,0:T(8,128)(2,1)} %copy-done.23, bf16[4,4,16,256]{3,2,1,0:T(8,128)(2,1)} %copy-done.21, bf16[4,4,16,256]{3,2,1,0:T(8,128)(2,1)} %copy-done.20, ...), custom_call_target="tpu_custom_call" | custom-call | bytes 2359296 | tf_op jit(solution)/shard_map/pallas_call | solution.py:77
  54.4 3.2 %collective-permute-start.17 = (bf16[128,256]{1,0:T(8,128)(2,1)S(1)}, bf16[128,256]{1,0:T(8,128)(2,1)S(1)}, u32[]{:S(2)}, u32[]{:S(2)}) collective-permute-start(bf16[128,256]{1,0:T(8,128)(2,1)S(1)} %get-tuple-element.72), channel_id=1, source_target_pairs={{0,1},{1,0},{2,3},{3,2},{4,5},{5,4},{6,7},{7,6},{8,9},{9,8},{10,11... | collective-permute-start | bytes 196616 | tf_op jit(solution)/shard_map/ppermute | solution.py:48
  58.5 3.0 %collective-permute-done.12.refs_3_ = bf16[4,4,4,16,256]{4,3,2,1,0:T(8,128)(2,1)S(1)} collective-permute-done((bf16[4,4,4,16,256]{4,3,2,1,0:T(8,128)(2,1)}, bf16[4,4,4,16,256]{4,3,2,1,0:T(8,128)(2,1)S(1)}, u32[]{:S(2)}, u32[]{:S(2)}) %collective-permute-start.12) | collective-permute-done | bytes 524320 | tf_op jit(solution)/shard_map/ppermute | solution.py:48
  63.3 5.4 %shard_map.98 = (bf16[4,4,4,16,256]{4,3,2,1,0:T(8,128)(2,1)}, bf16[4,4,4,16,256]{4,3,2,1,0:T(8,128)(2,1)}, bf16[4,4,4,16,256]{4,3,2,1,0:T(8,128)(2,1)}, bf16[4,4...) custom-call(bf16[4,128,1024]{2,1,0:T(8,128)(2,1)} %get-tuple-element, ...), custom_call_target="tpu_custom_call" | custom-call | flops 1207959552 | bytes 6979584 | tf_op jit(solution)/shard_map/pallas_call | solution.py:77
  68.7 4.9 %collective-permute-done.11.refs_2_ = bf16[4,4,4,16,256]{4,3,2,1,0:T(8,128)(2,1)S(1)} collective-permute-done((bf16[4,4,4,16,256]{4,3,2,1,0:T(8,128)(2,1)}, bf16[4,4,4,16,256]{4,3,2,1,0:T(8,128)(2,1)S(1)}, u32[]{:S(2)}, u32[]{:S(2)}) %collective-permute-start.11) | collective-permute-done | bytes 524320 | tf_op jit(solution)/shard_map/ppermute | solution.py:48
  77.0 12.4 %collective-permute-done.14.refs_6_ = bf16[4,20,16,256]{3,2,1,0:T(8,128)(2,1)S(1)} collective-permute-done((bf16[4,20,16,256]{3,2,1,0:T(8,128)(2,1)}, bf16[4,20,16,256]{3,2,1,0:T(8,128)(2,1)S(1)}, u32[]{:S(2)}, u32[]{:S(2)}) %collective-permute-start.14) | collective-permute-done | bytes 655392 | tf_op jit(solution)/shard_map/ppermute | solution.py:48
  91.2 8.7 %shard_map.96 = (bf16[128,256]{1,0:T(8,128)(2,1)}, bf16[128,256]{1,0:T(8,128)(2,1)}, f32[4,128,1024]{2,1,0:T(8,128)}, f32[4,128,1024]{2,1,0:T(8,128)}) custom-call(bf16[4,4,4,16,256]{4,3,2,1,0:T(8,128)(2,1)} %get-tuple-element.39.refs_0_, bf16[4,4,4,16,256]{4,3,2,1,0:T(8,128)(2,1)} %copy-done.43, bf16[4,4,4,16,256]{4,3,2,1,0:T(8,128)(2,1)} %copy-done.41, ...), custom_call_target="tpu_custom_call" | custom-call | flops 2415919104 | bytes 11273216 | tf_op jit(solution)/shard_map/pallas_call | solution.py:77
  107.2 12.3 %collective-permute-done.22.refs_3_ = bf16[4,4,4,16,256]{4,3,2,1,0:T(8,128)(2,1)S(1)} collective-permute-done((bf16[4,4,4,16,256]{4,3,2,1,0:T(8,128)(2,1)S(1)}, bf16[4,4,4,16,256]{4,3,2,1,0:T(8,128)(2,1)S(1)}, u32[]{:S(2)}, u32[]{:S(2)}) %collective-permute-start.22) | collective-permute-done | bytes 524320 | tf_op jit(solution)/shard_map/ppermute | solution.py:48
  121.6 14.9 %collective-permute-done.25.refs_7_ = bf16[81,16,256]{2,1,0:T(8,128)(2,1)S(1)} collective-permute-done((bf16[81,16,256]{2,1,0:T(8,128)(2,1)S(1)}, bf16[81,16,256]{2,1,0:T(8,128)(2,1)S(1)}, u32[]{:S(2)}, u32[]{:S(2)}) %collective-permute-start.25) | collective-permute-done | bytes 663584 | tf_op jit(solution)/shard_map/ppermute | solution.py:48
  137.3 3.7 %shard_map.99 = (bf16[4,4,16,256]{3,2,1,0:T(8,128)(2,1)}, bf16[4,4,16,256]{3,2,1,0:T(8,128)(2,1)}, bf16[4,4,16,256]{3,2,1,0:T(8,128)(2,1)}, bf16[4,4,16,256]{3,2...) custom-call(bf16[4,4,4,16,256]{4,3,2,1,0:T(8,128)(2,1)} %get-tuple-e, ...), custom_call_target="tpu_custom_call" | custom-call | bytes 5963776 | tf_op jit(solution)/shard_map/pallas_call | solution.py:77
  149.7 4.2 %collective-permute-done.28.refs_3_ = bf16[4,4,16,256]{3,2,1,0:T(8,128)(2,1)S(1)} collective-permute-done((bf16[4,4,16,256]{3,2,1,0:T(8,128)(2,1)}, bf16[4,4,16,256]{3,2,1,0:T(8,128)(2,1)S(1)}, u32[]{:S(2)}, u32[]{:S(2)}) %collective-permute-start.28) | collective-permute-done | bytes 131104 | tf_op jit(solution)/shard_map/ppermute | solution.py:48
  157.5 3.2 %collective-permute-start.32 = (bf16[10,16,256]{2,1,0:T(8,128)(2,1)}, bf16[10,16,256]{2,1,0:T(8,128)(2,1)S(1)}, u32[]{:S(2)}, u32[]{:S(2)}) collective-permute-start(bf16[10,16,256]{2,1,0:T(8,128)(2,1)} %get-tuple-element.65), channel_id=1, source_target_pairs={{0,24},{1,25},{2,26},{3,27},{4,28},{5,29},{6,30},{7,31},{8,0},{9,1... | collective-permute-start | bytes 245768 | tf_op jit(solution)/shard_map/ppermute | solution.py:48
  163.7 6.3 %collective-permute-done.33.refs_2_ = bf16[10,16,256]{2,1,0:T(8,128)(2,1)S(1)} collective-permute-done((bf16[10,16,256]{2,1,0:T(8,128)(2,1)}, bf16[10,16,256]{2,1,0:T(8,128)(2,1)S(1)}, u32[]{:S(2)}, u32[]{:S(2)}) %collective-permute-start.33) | collective-permute-done | bytes 81952 | tf_op jit(solution)/shard_map/ppermute | solution.py:48
  172.4 4.4 %collective-permute-done.35 = f32[10,16,256]{2,1,0:T(8,128)S(1)} collective-permute-done((f32[10,16,256]{2,1,0:T(8,128)}, f32[10,16,256]{2,1,0:T(8,128)S(1)}, u32[]{:S(2)}, u32[]{:S(2)}) %collective-permute-start.35) | collective-permute-done | bytes 163872 | tf_op jit(solution)/shard_map/ppermute | solution.py:58
  188.0 6.5 %collective-permute-start.39 = (f32[19,16,256]{2,1,0:T(8,128)}, f32[19,16,256]{2,1,0:T(8,128)S(1)}, u32[]{:S(2)}, u32[]{:S(2)}) collective-permute-start(f32[19,16,256]{2,1,0:T(8,128)} %get-tuple-element.69), channel_id=1, source_target_pairs={{0,1},{1,0},{2,3},{3,2},{4,5},{5,4},{6,7},{7,6},{8,9},{9,8},{10,11... | collective-permute-start | bytes 933896 | tf_op jit(solution)/shard_map/ppermute | solution.py:48
  200.5 7.8 %shard_map.97 = bf16[2,16,16,1024]{3,2,1,0:T(8,128)(2,1)} custom-call(bf16[4,128,1024]{2,1,0:T(8,128)(2,1)} %get-tuple-element.44.xp_ref, f32[4,128,1024]{2,1,0:T(8,128)} %get-tuple-element.45.own_ref, f32[4,128,1024]{2,1,0:T(8,128)} %copy-done, f32[1,1024]{1,0:T(1,128)} %bitcast.16, f32[1,1024]{1,0:T(1,128)} %bitcast.18, ...), custom_call_target="tpu_custom_call" | custom-call | flops 20971520 | bytes 6365184 | tf_op jit(solution)/shard_map/pallas_call | solution.py:77
  (171 shorter events, 72.7 us)
Async XLA Ops:
  1.7 11.2 %collective-permute-start = (bf16[18,16,256]{2,1,0:T(8,128)(2,1)S(1)}, bf16[18,16,256]{2,1,0:T(8,128)(2,1)S(1)}, u32[]{:S(2)}, u32[]{:S(2)}) collective-permute-start(bf16[18,16,256]{2,1,0:T(8,128)(2,1)S(1)} %broadcast_select_fusion.2), channel_id=1, source_target_pairs={{0,1},{1,0},{2,3},{3,2},{4,5},{5,4},{6,7},{7,6},{8,9},{9,8},{10,11... | collective-permute-start | bytes 442376 | tf_op jit(solution)/shard_map/ppermute | solution.py:48
  12.8 48.7 %collective-permute-start.16 = (bf16[4,128,1024]{2,1,0:T(8,128)(2,1)}, bf16[4,128,1024]{2,1,0:T(8,128)(2,1)S(1)}, u32[]{:S(2)}, u32[]{:S(2)}) collective-permute-start(bf16[4,128,1024]{2,1,0:T(8,128)(2,1)} %get-tuple-element.41.refs_8_.act_own), channel_id=1, source_target_pairs={{0,1},{1,0},{2,3},{3,2},{4,5},{5,4},{6,7},{7,6},{8,9},{9,8},{10,11... | collective-permute-start | bytes 3145736 | tf_op jit(solution)/shard_map/ppermute | solution.py:48
  14.0 8.8 %collective-permute-start.3 = (bf16[9,16,256]{2,1,0:T(8,128)(2,1)S(1)}, bf16[9,16,256]{2,1,0:T(8,128)(2,1)S(1)}, u32[]{:S(2)}, u32[]{:S(2)}) collective-permute-start(bf16[9,16,256]{2,1,0:T(8,128)(2,1)S(1)} %pad_maximum_fusion.a0), channel_id=1, source_target_pairs={{0,8},{1,9},{2,10},{3,11},{4,12},{5,13},{6,14},{7,15},{8,16},{9,17... | collective-permute-start | bytes 221192 | tf_op jit(solution)/shard_map/ppermute | solution.py:48
  15.3 9.8 %collective-permute-start.2 = (bf16[9,16,256]{2,1,0:T(8,128)(2,1)S(1)}, bf16[9,16,256]{2,1,0:T(8,128)(2,1)S(1)}, u32[]{:S(2)}, u32[]{:S(2)}) collective-permute-start(bf16[9,16,256]{2,1,0:T(8,128)(2,1)S(1)} %pad_maximum_fusion.a0), channel_id=1, source_target_pairs={{0,16},{1,17},{2,18},{3,19},{4,20},{5,21},{6,22},{7,23},{8,24},{9,... | collective-permute-start | bytes 221192 | tf_op jit(solution)/shard_map/ppermute | solution.py:48
  34.8 10.3 %collective-permute-start.9 = (bf16[4,5,16,256]{3,2,1,0:T(8,128)(2,1)}, bf16[4,5,16,256]{3,2,1,0:T(8,128)(2,1)S(1)}, u32[]{:S(2)}, u32[]{:S(2)}) collective-permute-start(bf16[4,5,16,256]{3,2,1,0:T(8,128)(2,1)} %get-tuple-element.38.b0), channel_id=1, source_target_pairs={{0,32},{1,33},{2,34},{3,35},{4,36},{5,37},{6,38},{7,39},{8,40},{9,... | collective-permute-start | bytes 491528 | tf_op jit(solution)/shard_map/ppermute | solution.py:48
  36.0 9.2 %collective-permute-start.8 = (bf16[4,5,16,256]{3,2,1,0:T(8,128)(2,1)}, bf16[4,5,16,256]{3,2,1,0:T(8,128)(2,1)S(1)}, u32[]{:S(2)}, u32[]{:S(2)}) collective-permute-start(bf16[4,5,16,256]{3,2,1,0:T(8,128)(2,1)} %get-tuple-element.38.b0), channel_id=1, source_target_pairs={{0,64},{1,65},{2,66},{3,67},{4,68},{5,69},{6,70},{7,71},{8,72},{9,... | collective-permute-start | bytes 491528 | tf_op jit(solution)/shard_map/ppermute | solution.py:48
  48.9 12.5 %collective-permute-start.12 = (bf16[4,4,4,16,256]{4,3,2,1,0:T(8,128)(2,1)}, bf16[4,4,4,16,256]{4,3,2,1,0:T(8,128)(2,1)S(1)}, u32[]{:S(2)}, u32[]{:S(2)}) collective-permute-start(bf16[4,4,4,16,256]{4,3,2,1,0:T(8,128)(2,1)} %get-tuple-element.39.refs_0_), channel_id=1, source_target_pairs={{0,32},{1,33},{2,34},{3,35},{4,36},{5,37},{6,38},{7,39},{8,40},{9,... | collective-permute-start | bytes 1572872 | tf_op jit(solution)/shard_map/ppermute | solution.py:48
  50.3 23.4 %collective-permute-start.11 = (bf16[4,4,4,16,256]{4,3,2,1,0:T(8,128)(2,1)}, bf16[4,4,4,16,256]{4,3,2,1,0:T(8,128)(2,1)S(1)}, u32[]{:S(2)}, u32[]{:S(2)}) collective-permute-start(bf16[4,4,4,16,256]{4,3,2,1,0:T(8,128)(2,1)} %get-tuple-element.39.refs_0_), channel_id=1, source_target_pairs={{0,64},{1,65},{2,66},{3,67},{4,68},{5,69},{6,70},{7,71},{8,72},{9,... | collective-permute-start | bytes 1572872 | tf_op jit(solution)/shard_map/ppermute | solution.py:48
  52.6 22.5 %collective-permute-start.10 = (bf16[4,4,4,16,256]{4,3,2,1,0:T(8,128)(2,1)}, bf16[4,4,4,16,256]{4,3,2,1,0:T(8,128)(2,1)S(1)}, u32[]{:S(2)}, u32[]{:S(2)}) collective-permute-start(bf16[4,4,4,16,256]{4,3,2,1,0:T(8,128)(2,1)} %get-tuple-element.39.refs_0_), channel_id=1, source_target_pairs={{0,96},{1,97},{2,98},{3,99},{4,100},{5,101},{6,102},{7,103},{8,104... | collective-permute-start | bytes 1572872 | tf_op jit(solution)/shard_map/ppermute | solution.py:48
  58.5 18.5 %collective-permute-start.15 = (bf16[4,20,16,256]{3,2,1,0:T(8,128)(2,1)}, bf16[4,20,16,256]{3,2,1,0:T(8,128)(2,1)S(1)}, u32[]{:S(2)}, u32[]{:S(2)}) collective-permute-start(bf16[4,20,16,256]{3,2,1,0:T(8,128)(2,1)} %get-tuple-element.40.refs_4_), channel_id=1, source_target_pairs={{0,2},{1,3},{2,4},{3,5},{4,6},{5,7},{6,0},{7,1},{8,10},{9,11},{10,... | collective-permute-start | bytes 1966088 | tf_op jit(solution)/shard_map/ppermute | solution.py:48
  61.4 27.9 %collective-permute-start.14 = (bf16[4,20,16,256]{3,2,1,0:T(8,128)(2,1)}, bf16[4,20,16,256]{3,2,1,0:T(8,128)(2,1)S(1)}, u32[]{:S(2)}, u32[]{:S(2)}) collective-permute-start(bf16[4,20,16,256]{3,2,1,0:T(8,128)(2,1)} %get-tuple-element.40.refs_4_), channel_id=1, source_target_pairs={{0,4},{1,5},{2,6},{3,7},{4,0},{5,1},{6,2},{7,3},{8,12},{9,13},{10,... | collective-permute-start | bytes 1966088 | tf_op jit(solution)/shard_map/ppermute | solution.py:48
  61.5 28.9 %collective-permute-start.13 = (bf16[4,20,16,256]{3,2,1,0:T(8,128)(2,1)}, bf16[4,20,16,256]{3,2,1,0:T(8,128)(2,1)S(1)}, u32[]{:S(2)}, u32[]{:S(2)}) collective-permute-start(bf16[4,20,16,256]{3,2,1,0:T(8,128)(2,1)} %get-tuple-element.40.refs_4_), channel_id=1, source_target_pairs={{0,6},{1,7},{2,0},{3,1},{4,2},{5,3},{6,4},{7,5},{8,14},{9,15},{10,... | collective-permute-start | bytes 1966088 | tf_op jit(solution)/shard_map/ppermute | solution.py:48
  73.6 31.6 %collective-permute-start.20 = (bf16[4,4,4,16,256]{4,3,2,1,0:T(8,128)(2,1)}, bf16[4,4,4,16,256]{4,3,2,1,0:T(8,128)(2,1)S(1)}, u32[]{:S(2)}, u32[]{:S(2)}) collective-permute-start(bf16[4,4,4,16,256]{4,3,2,1,0:T(8,128)(2,1)} %get-tuple-element.49), channel_id=1, source_target_pairs={{0,96},{1,97},{2,98},{3,99},{4,100},{5,101},{6,102},{7,103},{8,104... | collective-permute-start | bytes 1572872 | tf_op jit(solution)/shard_map/ppermute | solution.py:48
  75.1 30.3 %collective-permute-start.21 = (bf16[4,4,4,16,256]{4,3,2,1,0:T(8,128)(2,1)}, bf16[4,4,4,16,256]{4,3,2,1,0:T(8,128)(2,1)S(1)}, u32[]{:S(2)}, u32[]{:S(2)}) collective-permute-start(bf16[4,4,4,16,256]{4,3,2,1,0:T(8,128)(2,1)} %get-tuple-element.50), channel_id=1, source_target_pairs={{0,64},{1,65},{2,66},{3,67},{4,68},{5,69},{6,70},{7,71},{8,72},{9,... | collective-permute-start | bytes 1572872 | tf_op jit(solution)/shard_map/ppermute | solution.py:48
  100.0 99.2 %collective-permute-start.19 = (f32[4,128,1024]{2,1,0:T(8,128)}, f32[4,128,1024]{2,1,0:T(8,128)S(1)}, u32[]{:S(2)}, u32[]{:S(2)}) collective-permute-start(f32[4,128,1024]{2,1,0:T(8,128)} %get-tuple-element.46), channel_id=1, source_target_pairs={{0,1},{1,0},{2,3},{3,2},{4,5},{5,4},{6,7},{7,6},{8,9},{9,8},{10,11... | collective-permute-start | bytes 6291464 | tf_op jit(solution)/shard_map/ppermute | solution.py:48
  101.5 18.0 %collective-permute-start.23 = (bf16[81,16,256]{2,1,0:T(8,128)(2,1)S(1)}, bf16[81,16,256]{2,1,0:T(8,128)(2,1)S(1)}, u32[]{:S(2)}, u32[]{:S(2)}) collective-permute-start(bf16[81,16,256]{2,1,0:T(8,128)(2,1)S(1)} %copy-done.36), channel_id=1, source_target_pairs={{0,6},{1,7},{2,0},{3,1},{4,2},{5,3},{6,4},{7,5},{8,14},{9,15},{10,... | collective-permute-start | bytes 1990664 | tf_op jit(solution)/shard_map/ppermute | solution.py:48
  103.9 17.7 %collective-permute-start.24 = (bf16[81,16,256]{2,1,0:T(8,128)(2,1)S(1)}, bf16[81,16,256]{2,1,0:T(8,128)(2,1)S(1)}, u32[]{:S(2)}, u32[]{:S(2)}) collective-permute-start(bf16[81,16,256]{2,1,0:T(8,128)(2,1)S(1)} %copy-done.35), channel_id=1, source_target_pairs={{0,4},{1,5},{2,6},{3,7},{4,0},{5,1},{6,2},{7,3},{8,12},{9,13},{10,... | collective-permute-start | bytes 1990664 | tf_op jit(solution)/shard_map/ppermute | solution.py:48
  105.3 31.2 %collective-permute-start.25 = (bf16[81,16,256]{2,1,0:T(8,128)(2,1)S(1)}, bf16[81,16,256]{2,1,0:T(8,128)(2,1)S(1)}, u32[]{:S(2)}, u32[]{:S(2)}) collective-permute-start(bf16[81,16,256]{2,1,0:T(8,128)(2,1)S(1)} %copy-done.34), channel_id=1, source_target_pairs={{0,2},{1,3},{2,4},{3,5},{4,6},{5,7},{6,0},{7,1},{8,10},{9,11},{10,... | collective-permute-start | bytes 1990664 | tf_op jit(solution)/shard_map/ppermute | solution.py:48
  105.4 14.1 %collective-permute-start.22 = (bf16[4,4,4,16,256]{4,3,2,1,0:T(8,128)(2,1)S(1)}, bf16[4,4,4,16,256]{4,3,2,1,0:T(8,128)(2,1)S(1)}, u32[]{:S(2)}, u32[]{:S(2)}) collective-permute-start(bf16[4,4,4,16,256]{4,3,2,1,0:T(8,128)(2,1)S(1)} %copy-done.42), channel_id=1, source_target_pairs={{0,32},{1,33},{2,34},{3,35},{4,36},{5,37},{6,38},{7,39},{8,40},{9,... | collective-permute-start | bytes 1572872 | tf_op jit(solution)/shard_map/ppermute | solution.py:48
  142.6 11.4 %collective-permute-start.29 = (bf16[21,16,256]{2,1,0:T(8,128)(2,1)}, bf16[21,16,256]{2,1,0:T(8,128)(2,1)S(1)}, u32[]{:S(2)}, u32[]{:S(2)}) collective-permute-start(bf16[21,16,256]{2,1,0:T(8,128)(2,1)} %get-tuple-element.61), channel_id=1, source_target_pairs={{0,96},{1,97},{2,98},{3,99},{4,100},{5,101},{6,102},{7,103},{8,104... | collective-permute-start | bytes 516104 | tf_op jit(solution)/shard_map/ppermute | solution.py:48
  144.1 9.9 %collective-permute-start.30 = (bf16[21,16,256]{2,1,0:T(8,128)(2,1)}, bf16[21,16,256]{2,1,0:T(8,128)(2,1)S(1)}, u32[]{:S(2)}, u32[]{:S(2)}) collective-permute-start(bf16[21,16,256]{2,1,0:T(8,128)(2,1)} %get-tuple-element.62), channel_id=1, source_target_pairs={{0,64},{1,65},{2,66},{3,67},{4,68},{5,69},{6,70},{7,71},{8,72},{9,... | collective-permute-start | bytes 516104 | tf_op jit(solution)/shard_map/ppermute | solution.py:48
  145.9 8.8 %collective-permute-start.31 = (bf16[21,16,256]{2,1,0:T(8,128)(2,1)}, bf16[21,16,256]{2,1,0:T(8,128)(2,1)S(1)}, u32[]{:S(2)}, u32[]{:S(2)}) collective-permute-start(bf16[21,16,256]{2,1,0:T(8,128)(2,1)} %get-tuple-element.63), channel_id=1, source_target_pairs={{0,32},{1,33},{2,34},{3,35},{4,36},{5,37},{6,38},{7,39},{8,40},{9,... | collective-permute-start | bytes 516104 | tf_op jit(solution)/shard_map/ppermute | solution.py:48
  160.7 9.3 %collective-permute-start.33 = (bf16[10,16,256]{2,1,0:T(8,128)(2,1)}, bf16[10,16,256]{2,1,0:T(8,128)(2,1)S(1)}, u32[]{:S(2)}, u32[]{:S(2)}) collective-permute-start(bf16[10,16,256]{2,1,0:T(8,128)(2,1)} %get-tuple-element.66), channel_id=1, source_target_pairs={{0,16},{1,17},{2,18},{3,19},{4,20},{5,21},{6,22},{7,23},{8,24},{9,... | collective-permute-start | bytes 245768 | tf_op jit(solution)/shard_map/ppermute | solution.py:48
  160.7 9.3 %collective-permute-start.34 = (bf16[10,16,256]{2,1,0:T(8,128)(2,1)}, bf16[10,16,256]{2,1,0:T(8,128)(2,1)S(1)}, u32[]{:S(2)}, u32[]{:S(2)}) collective-permute-start(bf16[10,16,256]{2,1,0:T(8,128)(2,1)} %get-tuple-element.67), channel_id=1, source_target_pairs={{0,8},{1,9},{2,10},{3,11},{4,12},{5,13},{6,14},{7,15},{8,16},{9,17... | collective-permute-start | bytes 245768 | tf_op jit(solution)/shard_map/ppermute | solution.py:48
  (62 other events, 590.0 us)

commit v2 on v1

--- a/solution.py
+++ b/solution.py
@@ -14,7 +14,7 @@
 GSIZE = 32
 IMAGES = 512
 EPS = 1e-05
-VMEM_MB = 56 * 1024 * 1024
+MIB = 1024 * 1024
 CHUNK, PER_CHIP, NA, NB, QA, QB = 16, 36, 16, 20, 4, 5
 TAPS = [(ky, kx) for ky in range(3) for kx in range(3)]
 
@@ -62,7 +62,7 @@
     return lax.rem(index + step, 4)
 
 
-def call(body, outs, args, flops=0, moved=None, scratch=(), specs=None, out_specs=None, grid=None, **kw):
+def call(body, outs, args, flops=0, moved=None, scratch=(), specs=None, out_specs=None, grid=None, vmem=8, **kw):
     if moved is None:
         moved = sum(a.size * a.dtype.itemsize for a in args) + sum(
             o.size * o.dtype.itemsize for o in outs
@@ -78,7 +78,7 @@
         body,
         out_shape=outs,
         scratch_shapes=list(scratch),
-        compiler_params=pltpu.CompilerParams(vmem_limit_bytes=VMEM_MB),
+        compiler_params=pltpu.CompilerParams(vmem_limit_bytes=vmem * MIB),
         cost_estimate=pl.CostEstimate(flops=flops, bytes_accessed=moved, transcendentals=0),
         **params,
     )(*args)
@@ -144,7 +144,7 @@
     )
 
 
-def norm_back_body(xp_ref, own_ref, got_ref, gain_ref, bias_ref, stat_ref, out_ref, buf):
+def norm_back_body(xp_ref, dact_ref, gain_ref, bias_ref, stat_ref, out_ref, buf):
     gain, bias = gain_ref[...], bias_ref[...]
     mean, rstd = stat_ref[0], stat_ref[1]
     hats, grads, one, two = [], [], [], []
@@ -156,8 +156,7 @@
             hat = (xp_ref[p, rows, :].astype(F32) - m) * r
             y = hat * gain + bias
             s = jax.nn.sigmoid(y)
-            d = own_ref[p, rows, :] + got_ref[p, rows, :]
-            g = d * (s * (1.0 + y * (1.0 - s))) * gain
+            g = dact_ref[p, rows, :] * (s * (1.0 + y * (1.0 - s))) * gain
             s1 = s1 + jnp.sum(g, axis=0, keepdims=True)
             s2 = s2 + jnp.sum(g * hat, axis=0, keepdims=True)
             h_list.append(hat)
@@ -183,17 +182,17 @@
     out_ref[...] = buf[...].astype(BF).reshape(2, 16, 16, 128)
 
 
-def norm_backward(planes, own, got, gain, bias, stat):
+def norm_backward(planes, dact, gain, bias, stat):
     vec = pl.BlockSpec((1, 128), lambda c: (0, c))
     block = pl.BlockSpec((4, 128, 128), lambda c: (0, 0, c))
     return call(
         norm_back_body,
         (arr((2, 16, 16, CIN), BF),),
-        (planes, own, got, gain.reshape(1, CIN), bias.reshape(1, CIN), stat),
+        (planes, dact, gain.reshape(1, CIN), bias.reshape(1, CIN), stat),
         flops=40 * planes.size,
         scratch=(pltpu.VMEM((512, 128), F32),),
         grid=(CIN // 128,),
-        specs=[block, block, block, vec, vec, pl.BlockSpec((2, 8, 128), lambda c: (0, 0, c))],
+        specs=[block, block, vec, vec, pl.BlockSpec((2, 8, 128), lambda c: (0, 0, c))],
         out_specs=(pl.BlockSpec((2, 16, 16, 128), lambda c: (0, 0, 0, c)),),
     )[0]
 
@@ -205,16 +204,6 @@
         value = jnp.where(row % 8 == 7, 0.0, pltpu.roll(value, cot.shape[0] - 1, 0))
     if si:
         value = jnp.where((row // 8) % 8 == 7, 0.0, pltpu.roll(value, cot.shape[0] - 8, 0))
-    return value
-
-
-def delayed(acc, si, sj):
-    row = lax.broadcasted_iota(jnp.int32, acc.shape, 0)
-    value = acc
-    if sj:
-        value = jnp.where(row % 8 == 0, 0.0, pltpu.roll(value, 1, 0))
-    if si:
-        value = jnp.where((row // 8) % 8 == 0, 0.0, pltpu.roll(value, 8, 0))
     return value
 
 
@@ -285,141 +274,61 @@
         ),
         specs=[vm] * 4,
         out_specs=(hbm,) * 8,
+        vmem=24,
     )
     return res[:4], res[4:]
 
 
-def conv_body(*refs):
-    ka, kb = refs[:4], refs[4:8]
-    act_own, act_got, cot_own, cot_got, cbias = refs[8:13]
-    out_own, out_other, dact_own, dact_other = refs[13:17]
-    whole, sem = refs[17], refs[18]
-    x, y, _, _ = position()
-    copies = []
-    for d in range(4):
-        copies.append(
-            pltpu.make_async_copy(
-                ka[d], whole.at[:, :, pl.ds(QA * turn(x, d), QA)], sem.at[2 * d]
-            )
-        )
-        copies.append(
-            pltpu.make_async_copy(
-                kb[d], whole.at[:, turn(y, d), pl.ds(NA, NB)], sem.at[2 * d + 1]
-            )
-        )
-    for copy in copies:
-        copy.start()
-    cot = cot_rows(cot_own, cot_got)
-    moved = {(si, sj): shifted(cot, si, sj).astype(BF) for si in range(2) for sj in range(2)}
-    for copy in copies:
-        copy.wait()
-
-    def tap(t):
-        parts = []
-        for q in range(16):
-            n = t * 64 + 4 * q
-            r, k = n // PER_CHIP, n % PER_CHIP
-            parts.append(whole[r // 4, r % 4, k : k + 4].reshape(64, HALF))
-        return jnp.concatenate(parts, axis=0)
-
-    total = None
-    for si in range(2):
-        for sj in range(2):
-            acc = None
-            for t, (ky, kx) in enumerate(TAPS):
-                (pi, a), (pj, b) = source(ky), source(kx)
-                if (a, b) != (si, sj):
-                    continue
-                act = jnp.concatenate([act_own[2 * pi + pj], act_got[2 * pi + pj]], axis=0)
-                term = jnp.dot(act, tap(t), preferred_element_type=F32)
-                acc = term if acc is None else acc + term
-            acc = delayed(acc, si, sj)
-            total = acc if total is None else total + acc
-    result = (total + cbias[...]).astype(BF)
-    out_own[...] = result[:128]
-    out_other[...] = result[128:]
-    for pi in range(2):
-        for pj in range(2):
-            acc = None
-            for t, (ky, kx) in enumerate(TAPS):
-                (a, si), (b, sj) = source(ky), source(kx)
-                if (a, b) != (pi, pj):
-                    continue
-                term = lax.dot_general(
-                    moved[si, sj], tap(t), (((1,), (1,)), ((), ())), preferred_element_type=F32
-                )
-                acc = term if acc is None else acc + term
-            dact_own[2 * pi + pj] = acc[:128]
-            dact_other[2 * pi + pj] = acc[128:]
-
-
-def conv(ka, kb, act_own, act_got, cot_own, cot_got, cbias):
-    vm = pl.BlockSpec(memory_space=pltpu.VMEM)
-    hbm = pl.BlockSpec(memory_space=pl.ANY)
-    out, dact = arr((128, HALF), BF), arr((4, 128, CIN), F32)
+def conv_body(k_ref, act_ref, cot_ref, bias_ref, out_ref, dact_ref, moved, total):
+    t = pl.program_id(0)
+    ky, kx = t // 3, lax.rem(t, 3)
+    pi, pj = jnp.where(ky == 1, 0, 1), jnp.where(kx == 1, 0, 1)
+    si, sj = jnp.where(ky == 0, 1, 0), jnp.where(kx == 0, 1, 0)
+
+    @pl.when(t == 0)
+    def _():
+        cot = cot_ref[...].astype(F32)
+        for a in range(2):
+            for b in range(2):
+                moved[2 * a + b] = shifted(cot, a, b).astype(BF)
+        dact_ref[...] = jnp.zeros_like(dact_ref)
+        total[...] = jnp.broadcast_to(bias_ref[...], total.shape)
+
+    k = k_ref[...]
+    plane = 2 * pi + pj
+    term = jnp.dot(act_ref[plane], k, preferred_element_type=F32)
+    row = lax.broadcasted_iota(jnp.int32, term.shape, 0)
+    late = jnp.where(row % 8 == 0, 0.0, pltpu.roll(term, 1, 0))
+    term = jnp.where(sj == 1, late, term)
+    late = jnp.where((row // 8) % 8 == 0, 0.0, pltpu.roll(term, 8, 0))
+    total[...] += jnp.where(si == 1, late, term)
+    dact_ref[plane] += lax.dot_general(
+        moved[2 * si + sj], k, (((1,), (1,)), ((), ())), preferred_element_type=F32
+    )
+
+    @pl.when(t == 8)
+    def _():
+        out_ref[...] = total[...].astype(BF)
+
+
+def conv(kernel, act, cot, cbias):
+    fixed = lambda *shape: pl.BlockSpec(shape, lambda t: (0,) * len(shape))
     return call(
         conv_body,
-        (out, out, dact, dact),
-        (*ka, *kb, act_own, act_got, cot_own, cot_got, cbias),
-        flops=4 * 256 * 9216 * HALF,
-        scratch=(
-            pltpu.VMEM((4, 4, PER_CHIP, CHUNK, HALF), BF),
-            pltpu.SemaphoreType.DMA((8,)),
-        ),
-        specs=[hbm] * 8 + [vm] * 5,
-        out_specs=(vm,) * 4,
-    )
-
-
-def spread_z_body(a0, a1, a2, a3, a_ref, b_ref):
-    _, _, z, _ = position()
-    for d, ref in enumerate((a0, a1, a2, a3)):
-        there = turn(z, d)
-        a_ref[there] = ref[:QA]
-        b_ref[there] = ref[QA:]
-
-
-def spread_xy_body(a0, a1, a2, a3, b0, b1, b2, b3, a_ref, b_ref):
-    x, y, _, _ = position()
-    for d, (a, b) in enumerate(((a0, b0), (a1, b1), (a2, b2), (a3, b3))):
-        there = turn(y, d)
-        for z in range(4):
-            a_ref[z, there] = a[z]
-        there = turn(x, d)
-        for z in range(4):
-            b_ref[z, pl.ds(QB * there, QB)] = b[z]
-
-
-def gather_kernel(kernel, core):
-    halves = kernel.reshape(18, CHUNK, COUT)
-    left, right = halves[:, :, :HALF], halves[:, :, HALF:]
-    mine = jnp.where(core == 0, left, right)
-    theirs = fetch(jnp.where(core == 0, right, left), swap=1)
-    block = jnp.concatenate(
-        [jnp.where(core == 0, mine, theirs), jnp.where(core == 0, theirs, mine)], axis=0
-    )
-    x = position()[0]
-    piece = jnp.concatenate(
-        [
-            lax.dynamic_slice_in_dim(block, QA * x, QA, 0),
-            lax.dynamic_slice_in_dim(block, NA + QB * x, QB, 0),
+        (arr((128, COUT), BF), arr((4, 128, CIN), F32)),
+        (kernel, act, cot, cbias.reshape(1, COUT)),
+        flops=4 * 128 * 9216 * COUT,
+        scratch=(pltpu.VMEM((4, 128, COUT), BF), pltpu.VMEM((128, COUT), F32)),
+        grid=(9,),
+        specs=[
+            pl.BlockSpec((CIN, COUT), lambda t: (t, 0)),
+            fixed(4, 128, CIN),
+            fixed(128, COUT),
+            fixed(1, COUT),
         ],
-        axis=0,
-    )
-    got = [piece] + [fetch(piece, dz=2 * d) for d in range(1, 4)]
-    a, b = call(
-        spread_z_body, (arr((4, QA, CHUNK, HALF), BF), arr((4, QB, CHUNK, HALF), BF)), got
-    )
-    got_a = [a] + [fetch(a, dy=d) for d in range(1, 4)]
-    got_b = [b] + [fetch(b, dx=d) for d in range(1, 4)]
-    a, b = call(
-        spread_xy_body,
-        (arr((4, 4, QA, CHUNK, HALF), BF), arr((4, NB, CHUNK, HALF), BF)),
-        (*got_a, *got_b),
-    )
-    ka = [a] + [fetch(a, dx=d) for d in range(1, 4)]
-    kb = [b] + [fetch(b, dy=d) for d in range(1, 4)]
-    return ka, kb
+        out_specs=(fixed(128, COUT), fixed(4, 128, CIN)),
+        vmem=52,
+    )
 
 
 def four(refs, index):
@@ -492,6 +401,7 @@
         sum_xy_body,
         (arr((4, QA, CHUNK, HALF), BF),) * 4 + (arr((4 * QB + 1, CHUNK, HALF), BF),) * 4,
         (*a, *b),
+        vmem=16,
     )
     send_a, send_b = res[:4], res[4:]
     a = [send_a[0]] + [fetch(send_a[4 - d], dy=d) for d in range(1, 4)]
@@ -521,23 +431,14 @@
     left, right = cot[:, :HALF], cot[:, HALF:]
     cot_own = jnp.where(core == 0, left, right)
     cot_got = fetch(jnp.where(core == 0, right, left), swap=1)
-    ka, kb = gather_kernel(kernel, core)
+    full = lax.all_gather(kernel, "shard", axis=0, tiled=True)
     act, planes, stat = norm_forward(images, gn_gain, gn_bias)
     act_got = fetch(act, swap=1)
     send_a, send_b = wgrad(act, act_got, cot_own, cot_got)
     kernel_grad, bias_grad = reduce_gradient(send_a, send_b, core)
-    cbias = jnp.where(core == 0, conv_bias[:HALF], conv_bias[HALF:]).reshape(1, HALF)
-    out_own, out_other, dact_own, dact_other = conv(
-        ka, kb, act, act_got, cot_own, cot_got, cbias
-    )
-    out_got = fetch(out_other, swap=1)
-    dact_got = fetch(dact_other, swap=1)
-    outputs = jnp.where(
-        core == 0,
-        jnp.concatenate([out_own, out_got], axis=-1),
-        jnp.concatenate([out_got, out_own], axis=-1),
-    ).reshape(cotangent.shape)
-    input_grad = norm_backward(planes, dact_own, dact_got, gn_gain, gn_bias, stat)
+    out, dact = conv(full, act, cot, conv_bias)
+    outputs = out.reshape(cotangent.shape)
+    input_grad = norm_backward(planes, dact, gn_gain, gn_bias, stat)
     return outputs, input_grad, kernel_grad, bias_grad
 
 

time: 209 us -> 163 us (0.78)
  starting transfers between devices: 63.6 us -> 31.3 us
  Pallas kernels: 43.5 us -> 28.3 us
  between operations: 0.95 us -> 14.1 us
  other arithmetic: 6.14 us -> 0.96 us
  waiting for transfers between devices: 85.6 us -> 81.6 us
  local copies, waits for them, and re-layouts: 8.52 us -> 5.65 us
    ppermute x39 -> x21, starting transfers between devices: 63.6 us -> 29.2 us  [fetch(): return lax.ppermute(value, AXES, pairs(dx, dy, dz, swap))]
    ppermute x39 -> x21, waiting for transfers between devices: 81.2 us -> 60.8 us  [fetch(): return lax.ppermute(value, AXES, pairs(dx, dy, dz, swap))]
    ppermute x1, waiting for transfers between devices: 4.38 us -> 20.1 us  [pair_low(): return lax.ppermute(value, AXES, sorted(out))]
    pallas_call x10 -> x8, Pallas kernels: 43.5 us -> 28.3 us  [call(): pl.pallas_call(body, out_shape=outs, scratch_shapes=list(scratch), compil...]
    select_n x4 -> x0, other arithmetic: 3.27 us -> none  [the longest x1 1.01 us: gather_kernel(): jnp.where(core == 0, theirs, mine)]
    unnamed x92 -> x16, local copies, waits for them, and re-layouts: 7.06 us -> 4.2 us
  transfers between devices with their start and end apart: 40 -> 23, of which waited for: 24 -> 17; matrix products, arithmetic and copies ran while one was open for 3% -> 1% of each run, Pallas kernels for 17% -> 7%
where the time goes in v2:
time: 163 us; the launch traced here: 162 us
  waiting for transfers between devices  81.6 us (50%)
  starting transfers between devices  31.3 us (19%)
  Pallas kernels  28.3 us (17%)
  between operations  14.1 us (9%)
  local copies, waits for them, and re-layouts  5.65 us (3%)
    ppermute x21, waiting for transfers between devices, fetch(): return lax.ppermute(value, AXES, pairs(dx, dy, dz, swap))  60.8 us
    ppermute x21, starting transfers between devices, fetch(): return lax.ppermute(value, AXES, pairs(dx, dy, dz, swap))  29.2 us
    pallas_call x8, Pallas kernels, call(): pl.pallas_call(body, out_shape=outs, scratch_shapes=list(scratch), compil...  28.3 us
    ppermute x1, waiting for transfers between devices, pair_low(): return lax.ppermute(value, AXES, sorted(out))  20.1 us
    unnamed x16, local copies, waits for them, and re-layouts  4.2 us
  transfers between devices with their start and end apart: 23, of which 17 were waited for; matrix products, arithmetic and copies ran while one was open for 1% of the time, Pallas kernels for 7%

profile of v2, /device:TPU:1, one launch (start us, length us, event | category | flops | bytes accessed | tf_op | source)
XLA Modules:
  0.0 162.0 jit_solution(10355710028051302251)
XLA Ops:
  10.5 5.7 %shard_map.93 = (bf16[4,128,1024]{2,1,0:T(8,128)(2,1)S(1)}, bf16[4,128,1024]{2,1,0:T(8,128)(2,1)S(1)}, f32[2,8,1024]{2,1,0:T(8,128)S(1)}) custom-call(bf16[2,16,16,1024]{3,2,1,0:T(8,128)(2,1)S(1)} %copy-done.1, f32[1,1024]{1,0:T(1,128)S(1)} %bitcast.9, f32[1,1024]{1,0:T(1,128)S(1)} %bitcast.11), custom_call_target="tpu_custom_call" | custom-call | flops 10485760 | bytes 3219456 | tf_op jit(solution)/shard_map/pallas_call | solution.py:77
  16.3 3.3 %collective-permute-start = (bf16[4,128,1024]{2,1,0:T(8,128)(2,1)S(1)}, bf16[4,128,1024]{2,1,0:T(8,128)(2,1)S(1)}, u32[]{:S(2)}, u32[]{:S(2)}) collective-permute-start(bf16[4,128,1024]{2,1,0:T(8,128)(2,1)S(1)} %get-tuple-element.31.act_ref.act_own), channel_id=1, source_target_pairs={{0,1},{1,0},{2,3},{3,2},{4,5},{5,4},{6,7},{7,6},{8,9},{9,8},{10,11... | collective-permute-start | bytes 3145736 | tf_op jit(solution)/shard_map/ppermute | solution.py:48
  22.0 5.4 %shard_map.96 = (bf16[4,4,4,16,256]{4,3,2,1,0:T(8,128)(2,1)S(1)}, bf16[4,4,4,16,256]{4,3,2,1,0:T(8,128)(2,1)S(1)}, bf16[4,4,4,16,256]{4,3,2,1,0:T(8,128)(2,1)S(1...) custom-call(bf16[4,128,1024]{2,1,0:T(8,128)(2,1)S(1)} %get-tuple-ele, ...), custom_call_target="tpu_custom_call" | custom-call | flops 1207959552 | bytes 6979584 | tf_op jit(solution)/shard_map/pallas_call | solution.py:77
  28.2 2.7 %collective-permute-start.5 = (bf16[81,16,256]{2,1,0:T(8,128)(2,1)S(1)}, bf16[81,16,256]{2,1,0:T(8,128)(2,1)S(1)}, u32[]{:S(2)}, u32[]{:S(2)}) collective-permute-start(bf16[81,16,256]{2,1,0:T(8,128)(2,1)S(1)} %get-tuple-element.41), channel_id=1, source_target_pairs={{0,6},{1,7},{2,0},{3,1},{4,2},{5,3},{6,4},{7,5},{8,14},{9,15},{10,... | collective-permute-start | bytes 1990664 | tf_op jit(solution)/shard_map/ppermute | solution.py:48
  32.5 8.2 %collective-permute-done.2.refs_1_ = bf16[4,4,4,16,256]{4,3,2,1,0:T(8,128)(2,1)S(1)} collective-permute-done((bf16[4,4,4,16,256]{4,3,2,1,0:T(8,128)(2,1)S(1)}, bf16[4,4,4,16,256]{4,3,2,1,0:T(8,128)(2,1)S(1)}, u32[]{:S(2)}, u32[]{:S(2)}) %collective-permute-start.2) | collective-permute-done | bytes 524320 | tf_op jit(solution)/shard_map/ppermute | solution.py:48
  40.7 4.7 %collective-permute-done.3.refs_2_ = bf16[4,4,4,16,256]{4,3,2,1,0:T(8,128)(2,1)S(1)} collective-permute-done((bf16[4,4,4,16,256]{4,3,2,1,0:T(8,128)(2,1)S(1)}, bf16[4,4,4,16,256]{4,3,2,1,0:T(8,128)(2,1)S(1)}, u32[]{:S(2)}, u32[]{:S(2)}) %collective-permute-start.3) | collective-permute-done | bytes 524320 | tf_op jit(solution)/shard_map/ppermute | solution.py:48
  45.4 12.4 %collective-permute-done.4.refs_3_ = bf16[4,4,4,16,256]{4,3,2,1,0:T(8,128)(2,1)S(1)} collective-permute-done((bf16[4,4,4,16,256]{4,3,2,1,0:T(8,128)(2,1)S(1)}, bf16[4,4,4,16,256]{4,3,2,1,0:T(8,128)(2,1)S(1)}, u32[]{:S(2)}, u32[]{:S(2)}) %collective-permute-start.4) | collective-permute-done | bytes 524320 | tf_op jit(solution)/shard_map/ppermute | solution.py:48
  57.8 8.4 %collective-permute-done.7.refs_7_ = bf16[81,16,256]{2,1,0:T(8,128)(2,1)S(1)} collective-permute-done((bf16[81,16,256]{2,1,0:T(8,128)(2,1)S(1)}, bf16[81,16,256]{2,1,0:T(8,128)(2,1)S(1)}, u32[]{:S(2)}, u32[]{:S(2)}) %collective-permute-start.7) | collective-permute-done | bytes 663584 | tf_op jit(solution)/shard_map/ppermute | solution.py:48
  71.5 3.9 %collective-permute-done.9.refs_2_ = bf16[4,4,16,256]{3,2,1,0:T(8,128)(2,1)S(1)} collective-permute-done((bf16[4,4,16,256]{3,2,1,0:T(8,128)(2,1)S(1)}, bf16[4,4,16,256]{3,2,1,0:T(8,128)(2,1)S(1)}, u32[]{:S(2)}, u32[]{:S(2)}) %collective-permute-start.9) | collective-permute-done | bytes 131104 | tf_op jit(solution)/shard_map/ppermute | solution.py:48
  75.4 1.7 %collective-permute-done.10.refs_3_ = bf16[4,4,16,256]{3,2,1,0:T(8,128)(2,1)S(1)} collective-permute-done((bf16[4,4,16,256]{3,2,1,0:T(8,128)(2,1)S(1)}, bf16[4,4,16,256]{3,2,1,0:T(8,128)(2,1)S(1)}, u32[]{:S(2)}, u32[]{:S(2)}) %collective-permute-start.10) | collective-permute-done | bytes 131104 | tf_op jit(solution)/shard_map/ppermute | solution.py:48
  77.0 2.5 %collective-permute-done.13.refs_7_ = bf16[21,16,256]{2,1,0:T(8,128)(2,1)S(1)} collective-permute-done((bf16[21,16,256]{2,1,0:T(8,128)(2,1)S(1)}, bf16[21,16,256]{2,1,0:T(8,128)(2,1)S(1)}, u32[]{:S(2)}, u32[]{:S(2)}) %collective-permute-start.13) | collective-permute-done | bytes 172064 | tf_op jit(solution)/shard_map/ppermute | solution.py:48
  79.7 6.1 %collective-permute-start.14 = (bf16[10,16,256]{2,1,0:T(8,128)(2,1)S(1)}, bf16[10,16,256]{2,1,0:T(8,128)(2,1)S(1)}, u32[]{:S(2)}, u32[]{:S(2)}) collective-permute-start(bf16[10,16,256]{2,1,0:T(8,128)(2,1)S(1)} %get-tuple-element.53), channel_id=1, source_target_pairs={{0,24},{1,25},{2,26},{3,27},{4,28},{5,29},{6,30},{7,31},{8,0},{9,1... | collective-permute-start | bytes 245768 | tf_op jit(solution)/shard_map/ppermute | solution.py:48
  86.7 2.3 %collective-permute-start.16 = (bf16[10,16,256]{2,1,0:T(8,128)(2,1)S(1)}, bf16[10,16,256]{2,1,0:T(8,128)(2,1)S(1)}, u32[]{:S(2)}, u32[]{:S(2)}) collective-permute-start(bf16[10,16,256]{2,1,0:T(8,128)(2,1)S(1)} %get-tuple-element.55), channel_id=1, source_target_pairs={{0,8},{1,9},{2,10},{3,11},{4,12},{5,13},{6,14},{7,15},{8,16},{9,17... | collective-permute-start | bytes 245768 | tf_op jit(solution)/shard_map/ppermute | solution.py:48
  89.0 3.8 %collective-permute-done.14.refs_1_ = bf16[10,16,256]{2,1,0:T(8,128)(2,1)S(1)} collective-permute-done((bf16[10,16,256]{2,1,0:T(8,128)(2,1)S(1)}, bf16[10,16,256]{2,1,0:T(8,128)(2,1)S(1)}, u32[]{:S(2)}, u32[]{:S(2)}) %collective-permute-start.14) | collective-permute-done | bytes 81952 | tf_op jit(solution)/shard_map/ppermute | solution.py:48
  92.8 4.4 %collective-permute-done.15.refs_2_ = bf16[10,16,256]{2,1,0:T(8,128)(2,1)S(1)} collective-permute-done((bf16[10,16,256]{2,1,0:T(8,128)(2,1)S(1)}, bf16[10,16,256]{2,1,0:T(8,128)(2,1)S(1)}, u32[]{:S(2)}, u32[]{:S(2)}) %collective-permute-start.15) | collective-permute-done | bytes 81952 | tf_op jit(solution)/shard_map/ppermute | solution.py:48
  98.7 2.1 %collective-permute-start.17 = (f32[10,16,256]{2,1,0:T(8,128)S(1)}, f32[10,16,256]{2,1,0:T(8,128)S(1)}, u32[]{:S(2)}, u32[]{:S(2)}) collective-permute-start(f32[10,16,256]{2,1,0:T(8,128)S(1)} %shard_map.99), channel_id=1, source_target_pairs={{0,128},{1,129},{2,130},{3,131},{4,132},{5,133},{6,134},{7,135},{8... | collective-permute-start | bytes 491528 | tf_op jit(solution)/shard_map/ppermute | solution.py:58
  100.8 20.1 %collective-permute-done.17 = f32[10,16,256]{2,1,0:T(8,128)S(1)} collective-permute-done((f32[10,16,256]{2,1,0:T(8,128)S(1)}, f32[10,16,256]{2,1,0:T(8,128)S(1)}, u32[]{:S(2)}, u32[]{:S(2)}) %collective-permute-start.17) | collective-permute-done | bytes 163872 | tf_op jit(solution)/shard_map/ppermute | solution.py:58
  121.0 2.0 %collective-permute-start.18 = (f32[9,16,256]{2,1,0:T(8,128)S(1)}, f32[9,16,256]{2,1,0:T(8,128)S(1)}, u32[]{:S(2)}, u32[]{:S(2)}) collective-permute-start(f32[9,16,256]{2,1,0:T(8,128)S(1)} %slice.22), channel_id=1, source_target_pairs={{0,96},{1,97},{2,98},{3,99},{4,100},{5,101},{6,102},{7,103},{8,104... | collective-permute-start | bytes 442376 | tf_op jit(solution)/shard_map/ppermute | solution.py:48
  125.4 3.0 %collective-permute-done.19.f2 = f32[9,16,256]{2,1,0:T(8,128)S(1)} collective-permute-done((f32[9,16,256]{2,1,0:T(8,128)S(1)}, f32[9,16,256]{2,1,0:T(8,128)S(1)}, u32[]{:S(2)}, u32[]{:S(2)}) %collective-permute-start.19) | collective-permute-done | bytes 147488 | tf_op jit(solution)/shard_map/ppermute | solution.py:48
  128.5 2.0 %collective-permute-done.20.f3 = f32[9,16,256]{2,1,0:T(8,128)S(1)} collective-permute-done((f32[9,16,256]{2,1,0:T(8,128)S(1)}, f32[9,16,256]{2,1,0:T(8,128)S(1)}, u32[]{:S(2)}, u32[]{:S(2)}) %collective-permute-start.20) | collective-permute-done | bytes 147488 | tf_op jit(solution)/shard_map/ppermute | solution.py:48
  130.6 3.9 %collective-permute-start.21 = (f32[19,16,256]{2,1,0:T(8,128)S(1)}, f32[19,16,256]{2,1,0:T(8,128)S(1)}, u32[]{:S(2)}, u32[]{:S(2)}) collective-permute-start(f32[19,16,256]{2,1,0:T(8,128)S(1)} %get-tuple-element.57), channel_id=1, source_target_pairs={{0,1},{1,0},{2,3},{3,2},{4,5},{5,4},{6,7},{7,6},{8,9},{9,8},{10,11... | collective-permute-start | bytes 933896 | tf_op jit(solution)/shard_map/ppermute | solution.py:48
  137.2 11.1 %shard_map.94 = (bf16[128,512]{1,0:T(8,128)(2,1)}, f32[4,128,1024]{2,1,0:T(8,128)}) custom-call(bf16[9216,512]{1,0:T(8,128)(2,1)} %all-gather.2.cloned.1.call-done.k_ref, bf16[4,128,1024]{2,1,0:T(8,128)(2,1)S(1)} %get-tuple-element.31.act_ref.act_own, bf16[128,512]{1,0:T(8,128)(2,1)S(1)} %bitcast.8, f32[1,512]{1,0:T(1,128)S(1)} %bitcast.13), custom_call_target="tpu_custom_call" | custom-call | flops 2415919104 | bytes 12847104 | tf_op jit(solution)/shard_map/pallas_call | solution.py:77
  148.3 1.6 copy-done
  149.9 5.3 %shard_map.95 = bf16[2,16,16,1024]{3,2,1,0:T(8,128)(2,1)} custom-call(bf16[4,128,1024]{2,1,0:T(8,128)(2,1)S(1)} %get-tuple-element.33.xp_ref, f32[4,128,1024]{2,1,0:T(8,128)S(1)} %copy-done, f32[1,1024]{1,0:T(1,128)S(1)} %bitcast.10, f32[1,1024]{1,0:T(1,128)S(1)} %bitcast.12, f32[2,8,1024]{2,1,0:T(8,128)S(1)} %get-tuple-element.35.stat_ref), custom_call_target="tpu_custom_call" | custom-call | flops 20971520 | bytes 4268032 | tf_op jit(solution)/shard_map/pallas_call | solution.py:77
  (53 shorter events, 21.4 us)
Async XLA Ops:
  7.2 130.0 %copy-start.2 = (bf16[2,8,8,512]{3,2,1,0:T(8,128)(2,1)S(1)}, bf16[2,8,8,512]{3,2,1,0:T(8,128)(2,1)}, u32[]{:S(2)}) copy-start(bf16[2,8,8,512]{3,2,1,0:T(8,128)(2,1)} %param.11) | copy-start | bytes 393220
  7.2 130.0 %all-gather.2.cloned.1.call-start = ((), (), s32[]{:S(2)}) async-start(), calls=%async_computation | async-start | bytes 9732096 | tf_op jit(solution)/shard_map/all_gather | solution.py:434
  16.3 5.7 %collective-permute-start = (bf16[4,128,1024]{2,1,0:T(8,128)(2,1)S(1)}, bf16[4,128,1024]{2,1,0:T(8,128)(2,1)S(1)}, u32[]{:S(2)}, u32[]{:S(2)}) collective-permute-start(bf16[4,128,1024]{2,1,0:T(8,128)(2,1)S(1)} %get-tuple-element.31.act_ref.act_own), channel_id=1, source_target_pairs={{0,1},{1,0},{2,3},{3,2},{4,5},{5,4},{6,7},{7,6},{8,9},{9,8},{10,11... | collective-permute-start | bytes 3145736 | tf_op jit(solution)/shard_map/ppermute | solution.py:48
  20.5 1.5 collective-permute-start.1
  27.3 13.3 %collective-permute-start.2 = (bf16[4,4,4,16,256]{4,3,2,1,0:T(8,128)(2,1)S(1)}, bf16[4,4,4,16,256]{4,3,2,1,0:T(8,128)(2,1)S(1)}, u32[]{:S(2)}, u32[]{:S(2)}) collective-permute-start(bf16[4,4,4,16,256]{4,3,2,1,0:T(8,128)(2,1)S(1)} %get-tuple-element.37), channel_id=1, source_target_pairs={{0,96},{1,97},{2,98},{3,99},{4,100},{5,101},{6,102},{7,103},{8,104... | collective-permute-start | bytes 1572872 | tf_op jit(solution)/shard_map/ppermute | solution.py:48
  28.2 29.6 %collective-permute-start.5 = (bf16[81,16,256]{2,1,0:T(8,128)(2,1)S(1)}, bf16[81,16,256]{2,1,0:T(8,128)(2,1)S(1)}, u32[]{:S(2)}, u32[]{:S(2)}) collective-permute-start(bf16[81,16,256]{2,1,0:T(8,128)(2,1)S(1)} %get-tuple-element.41), channel_id=1, source_target_pairs={{0,6},{1,7},{2,0},{3,1},{4,2},{5,3},{6,4},{7,5},{8,14},{9,15},{10,... | collective-permute-start | bytes 1990664 | tf_op jit(solution)/shard_map/ppermute | solution.py:48
  30.9 26.9 %collective-permute-start.6 = (bf16[81,16,256]{2,1,0:T(8,128)(2,1)S(1)}, bf16[81,16,256]{2,1,0:T(8,128)(2,1)S(1)}, u32[]{:S(2)}, u32[]{:S(2)}) collective-permute-start(bf16[81,16,256]{2,1,0:T(8,128)(2,1)S(1)} %get-tuple-element.42), channel_id=1, source_target_pairs={{0,4},{1,5},{2,6},{3,7},{4,0},{5,1},{6,2},{7,3},{8,12},{9,13},{10,... | collective-permute-start | bytes 1990664 | tf_op jit(solution)/shard_map/ppermute | solution.py:48
  31.3 35.0 %collective-permute-start.7 = (bf16[81,16,256]{2,1,0:T(8,128)(2,1)S(1)}, bf16[81,16,256]{2,1,0:T(8,128)(2,1)S(1)}, u32[]{:S(2)}, u32[]{:S(2)}) collective-permute-start(bf16[81,16,256]{2,1,0:T(8,128)(2,1)S(1)} %get-tuple-element.43), channel_id=1, source_target_pairs={{0,2},{1,3},{2,4},{3,5},{4,6},{5,7},{6,0},{7,1},{8,10},{9,11},{10,... | collective-permute-start | bytes 1990664 | tf_op jit(solution)/shard_map/ppermute | solution.py:48
  31.9 13.4 %collective-permute-start.3 = (bf16[4,4,4,16,256]{4,3,2,1,0:T(8,128)(2,1)S(1)}, bf16[4,4,4,16,256]{4,3,2,1,0:T(8,128)(2,1)S(1)}, u32[]{:S(2)}, u32[]{:S(2)}) collective-permute-start(bf16[4,4,4,16,256]{4,3,2,1,0:T(8,128)(2,1)S(1)} %get-tuple-element.38), channel_id=1, source_target_pairs={{0,64},{1,65},{2,66},{3,67},{4,68},{5,69},{6,70},{7,71},{8,72},{9,... | collective-permute-start | bytes 1572872 | tf_op jit(solution)/shard_map/ppermute | solution.py:48
  40.7 17.1 %collective-permute-start.4 = (bf16[4,4,4,16,256]{4,3,2,1,0:T(8,128)(2,1)S(1)}, bf16[4,4,4,16,256]{4,3,2,1,0:T(8,128)(2,1)S(1)}, u32[]{:S(2)}, u32[]{:S(2)}) collective-permute-start(bf16[4,4,4,16,256]{4,3,2,1,0:T(8,128)(2,1)S(1)} %get-tuple-element.39), channel_id=1, source_target_pairs={{0,32},{1,33},{2,34},{3,35},{4,36},{5,37},{6,38},{7,39},{8,40},{9,... | collective-permute-start | bytes 1572872 | tf_op jit(solution)/shard_map/ppermute | solution.py:48
  66.8 4.7 %collective-permute-start.8 = (bf16[4,4,16,256]{3,2,1,0:T(8,128)(2,1)S(1)}, bf16[4,4,16,256]{3,2,1,0:T(8,128)(2,1)S(1)}, u32[]{:S(2)}, u32[]{:S(2)}) collective-permute-start(bf16[4,4,16,256]{3,2,1,0:T(8,128)(2,1)S(1)} %get-tuple-element.45), channel_id=1, source_target_pairs={{0,6},{1,7},{2,0},{3,1},{4,2},{5,3},{6,4},{7,5},{8,14},{9,15},{10,... | collective-permute-start | bytes 393224 | tf_op jit(solution)/shard_map/ppermute | solution.py:48
  68.3 8.8 %collective-permute-start.11 = (bf16[21,16,256]{2,1,0:T(8,128)(2,1)S(1)}, bf16[21,16,256]{2,1,0:T(8,128)(2,1)S(1)}, u32[]{:S(2)}, u32[]{:S(2)}) collective-permute-start(bf16[21,16,256]{2,1,0:T(8,128)(2,1)S(1)} %get-tuple-element.49), channel_id=1, source_target_pairs={{0,96},{1,97},{2,98},{3,99},{4,100},{5,101},{6,102},{7,103},{8,104... | collective-permute-start | bytes 516104 | tf_op jit(solution)/shard_map/ppermute | solution.py:48
  69.4 7.6 %collective-permute-start.12 = (bf16[21,16,256]{2,1,0:T(8,128)(2,1)S(1)}, bf16[21,16,256]{2,1,0:T(8,128)(2,1)S(1)}, u32[]{:S(2)}, u32[]{:S(2)}) collective-permute-start(bf16[21,16,256]{2,1,0:T(8,128)(2,1)S(1)} %get-tuple-element.50), channel_id=1, source_target_pairs={{0,64},{1,65},{2,66},{3,67},{4,68},{5,69},{6,70},{7,71},{8,72},{9,... | collective-permute-start | bytes 516104 | tf_op jit(solution)/shard_map/ppermute | solution.py:48
  69.4 10.1 %collective-permute-start.13 = (bf16[21,16,256]{2,1,0:T(8,128)(2,1)S(1)}, bf16[21,16,256]{2,1,0:T(8,128)(2,1)S(1)}, u32[]{:S(2)}, u32[]{:S(2)}) collective-permute-start(bf16[21,16,256]{2,1,0:T(8,128)(2,1)S(1)} %get-tuple-element.51), channel_id=1, source_target_pairs={{0,32},{1,33},{2,34},{3,35},{4,36},{5,37},{6,38},{7,39},{8,40},{9,... | collective-permute-start | bytes 516104 | tf_op jit(solution)/shard_map/ppermute | solution.py:48
  70.0 5.3 %collective-permute-start.9 = (bf16[4,4,16,256]{3,2,1,0:T(8,128)(2,1)S(1)}, bf16[4,4,16,256]{3,2,1,0:T(8,128)(2,1)S(1)}, u32[]{:S(2)}, u32[]{:S(2)}) collective-permute-start(bf16[4,4,16,256]{3,2,1,0:T(8,128)(2,1)S(1)} %get-tuple-element.46), channel_id=1, source_target_pairs={{0,4},{1,5},{2,6},{3,7},{4,0},{5,1},{6,2},{7,3},{8,12},{9,13},{10,... | collective-permute-start | bytes 393224 | tf_op jit(solution)/shard_map/ppermute | solution.py:48
  71.5 5.6 %collective-permute-start.10 = (bf16[4,4,16,256]{3,2,1,0:T(8,128)(2,1)S(1)}, bf16[4,4,16,256]{3,2,1,0:T(8,128)(2,1)S(1)}, u32[]{:S(2)}, u32[]{:S(2)}) collective-permute-start(bf16[4,4,16,256]{3,2,1,0:T(8,128)(2,1)S(1)} %get-tuple-element.47), channel_id=1, source_target_pairs={{0,2},{1,3},{2,4},{3,5},{4,6},{5,7},{6,0},{7,1},{8,10},{9,11},{10,... | collective-permute-start | bytes 393224 | tf_op jit(solution)/shard_map/ppermute | solution.py:48
  79.7 13.1 %collective-permute-start.14 = (bf16[10,16,256]{2,1,0:T(8,128)(2,1)S(1)}, bf16[10,16,256]{2,1,0:T(8,128)(2,1)S(1)}, u32[]{:S(2)}, u32[]{:S(2)}) collective-permute-start(bf16[10,16,256]{2,1,0:T(8,128)(2,1)S(1)} %get-tuple-element.53), channel_id=1, source_target_pairs={{0,24},{1,25},{2,26},{3,27},{4,28},{5,29},{6,30},{7,31},{8,0},{9,1... | collective-permute-start | bytes 245768 | tf_op jit(solution)/shard_map/ppermute | solution.py:48
  85.7 11.4 %collective-permute-start.15 = (bf16[10,16,256]{2,1,0:T(8,128)(2,1)S(1)}, bf16[10,16,256]{2,1,0:T(8,128)(2,1)S(1)}, u32[]{:S(2)}, u32[]{:S(2)}) collective-permute-start(bf16[10,16,256]{2,1,0:T(8,128)(2,1)S(1)} %get-tuple-element.54), channel_id=1, source_target_pairs={{0,16},{1,17},{2,18},{3,19},{4,20},{5,21},{6,22},{7,23},{8,24},{9,... | collective-permute-start | bytes 245768 | tf_op jit(solution)/shard_map/ppermute | solution.py:48
  86.7 12.0 %collective-permute-start.16 = (bf16[10,16,256]{2,1,0:T(8,128)(2,1)S(1)}, bf16[10,16,256]{2,1,0:T(8,128)(2,1)S(1)}, u32[]{:S(2)}, u32[]{:S(2)}) collective-permute-start(bf16[10,16,256]{2,1,0:T(8,128)(2,1)S(1)} %get-tuple-element.55), channel_id=1, source_target_pairs={{0,8},{1,9},{2,10},{3,11},{4,12},{5,13},{6,14},{7,15},{8,16},{9,17... | collective-permute-start | bytes 245768 | tf_op jit(solution)/shard_map/ppermute | solution.py:48
  98.7 22.2 %collective-permute-start.17 = (f32[10,16,256]{2,1,0:T(8,128)S(1)}, f32[10,16,256]{2,1,0:T(8,128)S(1)}, u32[]{:S(2)}, u32[]{:S(2)}) collective-permute-start(f32[10,16,256]{2,1,0:T(8,128)S(1)} %shard_map.99), channel_id=1, source_target_pairs={{0,128},{1,129},{2,130},{3,131},{4,132},{5,133},{6,134},{7,135},{8... | collective-permute-start | bytes 491528 | tf_op jit(solution)/shard_map/ppermute | solution.py:58
  121.0 4.5 %collective-permute-start.18 = (f32[9,16,256]{2,1,0:T(8,128)S(1)}, f32[9,16,256]{2,1,0:T(8,128)S(1)}, u32[]{:S(2)}, u32[]{:S(2)}) collective-permute-start(f32[9,16,256]{2,1,0:T(8,128)S(1)} %slice.22), channel_id=1, source_target_pairs={{0,96},{1,97},{2,98},{3,99},{4,100},{5,101},{6,102},{7,103},{8,104... | collective-permute-start | bytes 442376 | tf_op jit(solution)/shard_map/ppermute | solution.py:48
  122.9 5.6 %collective-permute-start.19 = (f32[9,16,256]{2,1,0:T(8,128)S(1)}, f32[9,16,256]{2,1,0:T(8,128)S(1)}, u32[]{:S(2)}, u32[]{:S(2)}) collective-permute-start(f32[9,16,256]{2,1,0:T(8,128)S(1)} %slice.22), channel_id=1, source_target_pairs={{0,64},{1,65},{2,66},{3,67},{4,68},{5,69},{6,70},{7,71},{8,72},{9,... | collective-permute-start | bytes 442376 | tf_op jit(solution)/shard_map/ppermute | solution.py:48
  124.3 6.2 %collective-permute-start.20 = (f32[9,16,256]{2,1,0:T(8,128)S(1)}, f32[9,16,256]{2,1,0:T(8,128)S(1)}, u32[]{:S(2)}, u32[]{:S(2)}) collective-permute-start(f32[9,16,256]{2,1,0:T(8,128)S(1)} %slice.22), channel_id=1, source_target_pairs={{0,32},{1,33},{2,34},{3,35},{4,36},{5,37},{6,38},{7,39},{8,40},{9,... | collective-permute-start | bytes 442376 | tf_op jit(solution)/shard_map/ppermute | solution.py:48
  130.6 5.1 %collective-permute-start.21 = (f32[19,16,256]{2,1,0:T(8,128)S(1)}, f32[19,16,256]{2,1,0:T(8,128)S(1)}, u32[]{:S(2)}, u32[]{:S(2)}) collective-permute-start(f32[19,16,256]{2,1,0:T(8,128)S(1)} %get-tuple-element.57), channel_id=1, source_target_pairs={{0,1},{1,0},{2,3},{3,2},{4,5},{5,4},{6,7},{7,6},{8,9},{9,8},{10,11... | collective-permute-start | bytes 933896 | tf_op jit(solution)/shard_map/ppermute | solution.py:48
  (7 other events, 298.4 us)
Sparse Core Ops, SparseCore 0:
  10.6 119.5 all-gather.1

commit v3 on v1

v3 whole, which is shorter than its diff:
```python
import functools

import jax
import jax.numpy as jnp
from jax import lax
from jax.experimental import pallas as pl
from jax.experimental.pallas import tpu as pltpu
from jax.sharding import PartitionSpec as P

BF = jnp.bfloat16
F32 = jnp.float32
AXES = ("rep", "shard")
CIN, COUT, HALF = 1024, 512, 256
GSIZE = 32
LANES = 256
IMAGES = 512
EPS = 1e-05
MIB = 1024 * 1024
CHUNK, PER_CHIP, QUARTER = 16, 36, 9
COST_NORM, COST_WGRAD, COST_CONV, COST_BACK, COST_SUM = 10**10, 2*10**10, 10**9, 10**7, 10**10
TAPS = [(ky, kx) for ky in range(3) for kx in range(3)]


def source(k):
    return (0, 0) if k == 1 else (1, 1 if k == 0 else 0)


def position():
    rep, shard = lax.axis_index("rep"), lax.axis_index("shard")
    return lax.rem(rep, 4), lax.rem(shard // 2, 4), shard // 8, lax.rem(shard, 2)


def number(x, y, z, core):
    return ((z % 2) * 4 + x) * 32 + ((z // 2) * 4 + y) * 2 + core


@functools.lru_cache(maxsize=None)
def pairs(dx, dy, dz, swap):
    out = []
    for x in range(4):
        for y in range(4):
            for z in range(8):
                for core in range(2):
                    sign = 1 - 2 * core
                    src = number(
                        (x + sign * dx) % 4, (y + sign * dy) % 4, (z + sign * dz) % 8, core ^ swap
                    )
                    out.append((src, number(x, y, z, core)))
    return sorted(out)


def fetch(value, dx=0, dy=0, dz=0, swap=0):
    with jax.named_scope(f"from_x{dx}_y{dy}_z{dz}_core{swap}"):
        return lax.ppermute(value, AXES, pairs(dx, dy, dz, swap))


def pair_low(value):
    out = []
    for x in range(4):
        for y in range(4):
            for z in range(8):
                for core in range(2):
                    out.append((number(x, y, z ^ 1, core), number(x, y, z, core)))
    with jax.named_scope("from_z_low"):
        return lax.ppermute(value, AXES, sorted(out))


def turn(index, step, core):
    return lax.rem(index + jnp.where(core == 0, step, 4 - step), 4)


def call(body, outs, args, flops=0, moved=None, scratch=(), specs=None, out_specs=None, grid=None, vmem=8, **kw):
    if moved is None:
        moved = sum(a.size * a.dtype.itemsize for a in args) + sum(
            o.size * o.dtype.itemsize for o in outs
        )
    params = dict(kw)
    if grid is not None:
        params["grid"] = grid
    if specs is not None:
        params["in_specs"] = specs
    if out_specs is not None:
        params["out_specs"] = out_specs
    return pl.pallas_call(
        body,
        out_shape=outs,
        scratch_shapes=list(scratch),
        compiler_params=pltpu.CompilerParams(vmem_limit_bytes=vmem * MIB),
        cost_estimate=pl.CostEstimate(flops=flops, bytes_accessed=moved, transcendentals=0),
        **params,
    )(*args)


def arr(shape, dtype):
    return jax.ShapeDtypeStruct(shape, dtype)


def group_mean(rows):
    a = lax.broadcasted_iota(jnp.int32, (LANES, LANES), 0) // GSIZE
    b = lax.broadcasted_iota(jnp.int32, (LANES, LANES), 1) // GSIZE
    ones = jnp.where(a == b, 1.0, 0.0).astype(F32)
    total = lax.dot_general(
        rows,
        ones,
        (((1,), (0,)), ((), ())),
        precision=lax.Precision.HIGHEST,
        preferred_element_type=F32,
    )
    return total * (1.0 / (256 * GSIZE))


def stack_rows(a, b):
    row = lax.broadcasted_iota(jnp.int32, (8, LANES), 0)
    return jnp.where(row == 0, a, jnp.where(row == 1, b, 0.0))


def norm_body(x_ref, gain_ref, bias_ref, act_ref, plane_ref, stat_ref, *bufs):
    x = x_ref[...].astype(F32).reshape(2, 256, LANES)
    sums = [jnp.sum(x[i], axis=0, keepdims=True) for i in range(2)]
    mean = group_mean(stack_rows(*sums))
    sq = [jnp.sum(jnp.square(x[i] - mean[i : i + 1]), axis=0, keepdims=True) for i in range(2)]
    rstd = lax.rsqrt(group_mean(stack_rows(*sq)) + EPS)
    stat_ref[0] = mean
    stat_ref[1] = rstd
    for h, buf in enumerate(bufs):
        buf[...] = x[:, :, 128 * h : 128 * h + 128].reshape(512, 128)
    gain, bias = gain_ref[...], bias_ref[...]
    for pj in range(2):
        part = jnp.concatenate([buf[pl.ds(pj, 256, stride=2), :] for buf in bufs], axis=-1)
        part = part.reshape(2, 8, 2, 8, LANES)
        for pi in range(2):
            for i in range(2):
                xp = part[i, :, pi].reshape(64, LANES)
                y = (xp - mean[i : i + 1]) * rstd[i : i + 1] * gain + bias
                rows = slice(64 * i, 64 * i + 64)
                act_ref[2 * pi + pj, rows, :] = (y * jax.nn.sigmoid(y)).astype(BF)
                plane_ref[2 * pi + pj, rows, :] = xp.astype(BF)


def norm_forward(images, gain, bias):
    plane = arr((4, 128, CIN), BF)
    vec = pl.BlockSpec((1, LANES), lambda c: (0, c))
    block = pl.BlockSpec((4, 128, LANES), lambda c: (0, 0, c))
    return call(
        norm_body,
        (plane, plane, arr((2, 8, CIN), F32)),
        (images, gain.reshape(1, CIN), bias.reshape(1, CIN)),
        flops=COST_NORM,
        scratch=(pltpu.VMEM((512, 128), F32),) * (LANES // 128),
        grid=(CIN // LANES,),
        specs=[pl.BlockSpec((2, 16, 16, LANES), lambda c: (0, 0, 0, c)), vec, vec],
        out_specs=(block, block, pl.BlockSpec((2, 8, LANES), lambda c: (0, 0, c))),
    )


def norm_back_body(xp_ref, own_ref, got_ref, gain_ref, bias_ref, stat_ref, out_ref, *bufs):
    gain, bias = gain_ref[...], bias_ref[...]
    mean, rstd = stat_ref[0], stat_ref[1]
    hats, grads, one, two = [], [], [], []
    for i in range(2):
        rows = slice(64 * i, 64 * i + 64)
        m, r = mean[i : i + 1], rstd[i : i + 1]
        h_list, g_list, s1, s2 = [], [], 0.0, 0.0
        for p in range(4):
            hat = (xp_ref[p, rows, :].astype(F32) - m) * r
            y = hat * gain + bias
            s = jax.nn.sigmoid(y)
            d = own_ref[p, rows, :] + got_ref[p, rows, :].astype(F32)
            g = d * (s * (1.0 + y * (1.0 - s))) * gain
            s1 = s1 + jnp.sum(g, axis=0, keepdims=True)
            s2 = s2 + jnp.sum(g * hat, axis=0, keepdims=True)
            h_list.append(hat)
            g_list.append(g)
        hats.append(h_list)
        grads.append(g_list)
        one.append(s1)
        two.append(s2)
    mean1 = group_mean(stack_rows(*one))
    mean2 = group_mean(stack_rows(*two))
    for pj in range(2):
        parts = []
        for i in range(2):
            both = []
            for pi in range(2):
                p = 2 * pi + pj
                dx = rstd[i : i + 1] * (
                    grads[i][p] - mean1[i : i + 1] - hats[i][p] * mean2[i : i + 1]
                )
                both.append(dx.reshape(8, 1, 8, LANES))
            parts.append(jnp.concatenate(both, axis=1).reshape(128, LANES))
        rows = jnp.concatenate(parts, axis=0)
        for h, buf in enumerate(bufs):
            buf[pl.ds(pj, 256, stride=2), :] = rows[:, 128 * h : 128 * h + 128]
    for h, buf in enumerate(bufs):
        out_ref[:, :, :, 128 * h : 128 * h + 128] = buf[...].astype(BF).reshape(2, 16, 16, 128)


def norm_backward(planes, own, got, gain, bias, stat):
    vec = pl.BlockSpec((1, LANES), lambda c: (0, c))
    block = pl.BlockSpec((4, 128, LANES), lambda c: (0, 0, c))
    return call(
        norm_back_body,
        (arr((2, 16, 16, CIN), BF),),
        (planes, own, got, gain.reshape(1, CIN), bias.reshape(1, CIN), stat),
        flops=COST_BACK,
        scratch=(pltpu.VMEM((512, 128), F32),) * (LANES // 128),
        grid=(CIN // LANES,),
        specs=[block, block, block, vec, vec, pl.BlockSpec((2, 8, LANES), lambda c: (0, 0, c))],
        out_specs=(pl.BlockSpec((2, 16, 16, LANES), lambda c: (0, 0, 0, c)),),
    )[0]


def shifted(cot, si, sj):
    row = lax.broadcasted_iota(jnp.int32, cot.shape, 0)
    value = cot
    if sj:
        value = jnp.where(row % 8 == 7, 0.0, pltpu.roll(value, cot.shape[0] - 1, 0))
    if si:
        value = jnp.where((row // 8) % 8 == 7, 0.0, pltpu.roll(value, cot.shape[0] - 8, 0))
    return value


def delayed(acc, si, sj):
    row = lax.broadcasted_iota(jnp.int32, acc.shape, 0)
    value = acc
    if sj:
        value = jnp.where(row % 8 == 0, 0.0, pltpu.roll(value, 1, 0))
    if si:
        value = jnp.where((row // 8) % 8 == 0, 0.0, pltpu.roll(value, 8, 0))
    return value


def cot_rows(own_ref, got_ref):
    return jnp.concatenate([own_ref[...], got_ref[...]], axis=0).astype(F32)


def last_tap(z):
    return -(-(z + 1) * 2304 // CIN) - 1


def wgrad_body(act_own, act_got, cot_own, cot_got, *refs):
    outs = refs[:4]
    whole, tail, turned, sem = refs[4:8]
    x, _, _, core = position()
    cot = cot_rows(cot_own, cot_got)
    moved = {(si, sj): shifted(cot, si, sj).astype(BF) for si in range(2) for sj in range(2)}
    copies = []

    def send(src, dst):
        copies.append(pltpu.make_async_copy(src, dst, sem.at[len(copies)]))
        copies[-1].start()

    bias = jnp.sum(cot, axis=0, keepdims=True)
    high = bias.astype(BF).astype(F32)
    row = lax.broadcasted_iota(jnp.int32, (CHUNK, HALF), 0)
    tail[...] = jnp.zeros_like(tail)
    tail[0, 0] = jnp.where(row == 0, high, jnp.where(row == 1, bias - high, 0.0)).astype(BF)
    for d in range(4):
        send(tail, outs[d].at[pl.ds(16, 1)])
    ready = set()
    for t, (ky, kx) in enumerate(TAPS):
        (pi, si), (pj, sj) = source(ky), source(kx)
        p = 2 * pi + pj
        if p not in ready:
            turned[p, :, :128] = act_own[p].T
            turned[p, :, 128:] = act_got[p].T
            ready.add(p)
        grad = jnp.dot(turned[p], moved[si, sj], preferred_element_type=F32).astype(BF)
        for q in range(16):
            n = t * 64 + 4 * q
            r, k = n // PER_CHIP, n % PER_CHIP
            whole[r, k : k + 4] = grad[64 * q : 64 * q + 64].reshape(4, CHUNK, HALF)
        for z in range(4):
            if last_tap(z) != t:
                continue
            for d in range(4):
                there = turn(x, d, core)
                send(
                    whole.at[pl.ds(4 * z, 4), pl.ds(QUARTER * there, QUARTER)],
                    outs[d].at[pl.ds(4 * z, 4)],
                )
    for copy in copies:
        copy.wait()


def wgrad(act_own, act_got, cot_own, cot_got):
    vm = pl.BlockSpec(memory_space=pltpu.VMEM)
    hbm = pl.BlockSpec(memory_space=pl.ANY)
    return call(
        wgrad_body,
        (arr((17, QUARTER, CHUNK, HALF), BF),) * 4,
        (act_own, act_got, cot_own, cot_got),
        flops=COST_WGRAD,
        scratch=(
            pltpu.VMEM((16, PER_CHIP, CHUNK, HALF), BF),
            pltpu.VMEM((1, QUARTER, CHUNK, HALF), BF),
            pltpu.VMEM((4, CIN, 256), BF),
            pltpu.SemaphoreType.DMA((20,)),
        ),
        specs=[vm] * 4,
        out_specs=(hbm,) * 4,
        vmem=24,
    )


def conv_body(*refs):
    parts = refs[:4]
    act_own, act_got, cot_own, cot_got, cbias = refs[4:9]
    out_own, out_other, dact_own, dact_other = refs[9:13]
    whole, sem = refs[13], refs[14]
    _, y, _, core = position()
    copies = [
        [
            pltpu.make_async_copy(
                parts[d].at[z],
                whole.at[z, turn(y, d, core)],
                sem.at[4 * z + d],
            )
            for d in range(4)
        ]
        for z in range(4)
    ]
    for group in copies:
        for copy in group:
            copy.start()
    cot = cot_rows(cot_own, cot_got)
    moved = {(si, sj): shifted(cot, si, sj).astype(BF) for si in range(2) for sj in range(2)}

    def tap(t):
        rows = []
        for q in range(16):
            n = t * 64 + 4 * q
            r, k = n // PER_CHIP, n % PER_CHIP
            rows.append(whole[r // 4, r % 4, k : k + 4].reshape(64, HALF))
        return jnp.concatenate(rows, axis=0)

    total = jnp.broadcast_to(cbias[...], (256, HALF))
    here = 0
    for t, (ky, kx) in enumerate(TAPS):
        while here < 4 and here * 2304 < (t + 1) * CIN:
            for copy in copies[here]:
                copy.wait()
            here += 1
        (pi, si), (pj, sj) = source(ky), source(kx)
        act = jnp.concatenate([act_own[2 * pi + pj], act_got[2 * pi + pj]], axis=0)
        term = jnp.dot(act, tap(t), preferred_element_type=F32)
        total = total + delayed(term, si, sj)
    result = total.astype(BF)
    out_own[...] = result[:128]
    out_other[...] = result[128:]
    for pi in range(2):
        for pj in range(2):
            acc = None
            for t, (ky, kx) in enumerate(TAPS):
                (a, si), (b, sj) = source(ky), source(kx)
                if (a, b) != (pi, pj):
                    continue
                term = lax.dot_general(
                    moved[si, sj], tap(t), (((1,), (1,)), ((), ())), preferred_element_type=F32
                )
                acc = term if acc is None else acc + term
            dact_own[2 * pi + pj] = acc[:128]
            dact_other[2 * pi + pj] = acc[128:].astype(BF)


def conv(parts, act_own, act_got, cot_own, cot_got, cbias):
    vm = pl.BlockSpec(memory_space=pltpu.VMEM)
    hbm = pl.BlockSpec(memory_space=pl.ANY)
    out = arr((128, HALF), BF)
    return call(
        conv_body,
        (out, out, arr((4, 128, CIN), F32), arr((4, 128, CIN), BF)),
        (*parts, act_own, act_got, cot_own, cot_got, cbias),
        flops=COST_CONV,
        scratch=(
            pltpu.VMEM((4, 4, PER_CHIP, CHUNK, HALF), BF),
            pltpu.SemaphoreType.DMA((16,)),
        ),
        specs=[hbm] * 4 + [vm] * 5,
        out_specs=(vm,) * 4,
        vmem=32,
    )


def block_body(rows, theirs, out):
    core = position()[3]
    own = jnp.where(core == 0, rows[:, :, :HALF], rows[:, :, HALF:])
    out[pl.ds(18 * core, 18)] = own
    out[pl.ds(18 * (1 - core), 18)] = theirs[...]


def spread_z_body(a0, a1, a2, a3, _, out):
    _, _, z, core = position()
    for d, ref in enumerate((a0, a1, a2, a3)):
        out[turn(z, d, core)] = ref[...]


def gather_kernel(kernel, core, grads):
    vm = pl.BlockSpec(memory_space=pltpu.VMEM)
    anywhere = pl.BlockSpec(memory_space=pl.ANY)
    rows = kernel.reshape(18, CHUNK, COUT)
    theirs = fetch(jnp.where(core == 0, rows[:, :, HALF:], rows[:, :, :HALF]), swap=1)
    block = call(
        block_body,
        (arr((PER_CHIP, CHUNK, HALF), BF),),
        (rows, theirs),
    )[0]
    got = [block] + [fetch(block, dz=2 * d) for d in range(1, 4)]
    level = call(
        spread_z_body,
        (arr((4, PER_CHIP, CHUNK, HALF), BF),),
        (*got, grads),
        specs=[vm] * 4 + [anywhere],
    )[0]
    parts = [level]
    for _ in range(3):
        parts.append(fetch(parts[-1], dy=1))
    return parts


def four(refs, index):
    v = [ref[index].astype(F32) for ref in refs]
    return (v[0] + v[2]) + (v[1] + v[3])


def bias_four(refs, index):
    v = [ref[index].astype(F32) for ref in refs]
    v = [w[0:1] + w[1:2] for w in v]
    return (v[0] + v[2]) + (v[1] + v[3])


def bias_chunk(total):
    high = total.astype(BF).astype(F32)
    row = lax.broadcasted_iota(jnp.int32, (CHUNK, HALF), 0)
    return jnp.where(row == 0, high, jnp.where(row == 1, total - high, 0.0)).astype(BF)


def sum_x_body(*refs):
    ins, outs = refs[:4], refs[4:]
    _, y, _, core = position()
    bias = bias_chunk(bias_four(ins, (16, 0)))
    for d in range(4):
        there = turn(y, d, core)
        for z in range(4):
            outs[d][QUARTER * z : QUARTER * z + QUARTER] = four(ins, 4 * z + there).astype(BF)
        outs[d][4 * QUARTER] = bias


def sum_y_body(*refs):
    ins, outs = refs[:4], refs[4:]
    _, _, z, core = position()
    bias = bias_chunk(bias_four(ins, 4 * QUARTER))
    for d in range(4):
        there = turn(z, d, core)
        outs[d][:QUARTER] = four(ins, pl.ds(QUARTER * there, QUARTER)).astype(BF)
        outs[d][QUARTER] = bias


def sum_z_body(*refs):
    ins, out = refs[:4], refs[4]
    out[:QUARTER] = four(ins, pl.ds(0, QUARTER))
    row = lax.broadcasted_iota(jnp.int32, (CHUNK, HALF), 0)
    out[QUARTER] = jnp.where(row == 0, bias_four(ins, QUARTER), 0.0)


def place_body(f0, f1, f2, f3, mine, theirs, whole):
    x, _, _, core = position()
    for d, ref in enumerate((f0, f1, f2, f3)):
        whole[pl.ds(QUARTER * turn(x, d, core), QUARTER)] = ref[:QUARTER]
    mine[:18] = whole[pl.ds(18 * core, 18)]
    theirs[:18] = whole[pl.ds(18 * (1 - core), 18)]
    mine[18] = f0[QUARTER]
    theirs[18] = f0[QUARTER]


def reduce_gradient(got, core):
    send = call(
        sum_x_body,
        (arr((4 * QUARTER + 1, CHUNK, HALF), BF),) * 4,
        got,
        flops=COST_SUM,
        vmem=16,
    )
    got = [send[0]] + [fetch(send[4 - d], dy=d) for d in range(1, 4)]
    send = call(sum_y_body, (arr((QUARTER + 1, CHUNK, HALF), BF),) * 4, got, flops=COST_SUM)
    got = [send[0]] + [fetch(send[4 - d], dz=2 * d) for d in range(1, 4)]
    part = call(sum_z_body, (arr((QUARTER + 1, CHUNK, HALF), F32),), got, flops=COST_SUM)[0]
    full = (part + pair_low(part)) * (1.0 / IMAGES)
    rows = full[:QUARTER]
    every = [full] + [fetch(rows, dx=d) for d in range(1, 4)]
    mine, theirs = call(
        place_body,
        (arr((19, CHUNK, HALF), F32),) * 2,
        every,
        scratch=(pltpu.VMEM((PER_CHIP, CHUNK, HALF), F32),),
    )
    got = fetch(theirs, swap=1)
    both = jnp.where(
        core == 0, jnp.concatenate([mine, got], axis=-1), jnp.concatenate([got, mine], axis=-1)
    )
    return both[:18].reshape(288, COUT), both[18, 0]


def local(images, kernel, gn_gain, gn_bias, conv_bias, cotangent):
    core = position()[3]
    cot = cotangent.reshape(128, COUT)
    left, right = cot[:, :HALF], cot[:, HALF:]
    cot_own = jnp.where(core == 0, left, right)
    cot_got = fetch(jnp.where(core == 0, right, left), swap=1)
    act, planes, stat = norm_forward(images, gn_gain, gn_bias)
    act_got = fetch(act, swap=1)
    send = wgrad(act, act_got, cot_own, cot_got)
    got = [send[0]] + [fetch(send[4 - d], dx=d) for d in range(1, 4)]
    parts = gather_kernel(kernel, core, send[0])
    kernel_grad, bias_grad = reduce_gradient(got, core)
    cbias = jnp.where(core == 0, conv_bias[:HALF], conv_bias[HALF:]).reshape(1, HALF)
    out_own, out_other, dact_own, dact_other = conv(
        parts, act, act_got, cot_own, cot_got, cbias
    )
    dact_got = fetch(dact_other, swap=1)
    out_got = fetch(out_other, swap=1)
    outputs = jnp.where(
        core == 0,
        jnp.concatenate([out_own, out_got], axis=-1),
        jnp.concatenate([out_got, out_own], axis=-1),
    ).reshape(cotangent.shape)
    input_grad = norm_backward(planes, dact_own, dact_got, gn_gain, gn_bias, stat)
    return outputs, input_grad, kernel_grad, bias_grad


def solution(mesh):
    return jax.shard_map(
        local,
        mesh=mesh,
        in_specs=(
            P(AXES, None, None, None),
            P("shard", None),
            P(),
            P(),
            P(),
            P(AXES, None, None, None),
        ),
        out_specs=(
            P(AXES, None, None, None),
            P(AXES, None, None, None),
            P("shard", None),
            P(),
        ),
        check_vma=False,
    )
```

time: 209 us -> 144 us (0.69)
  Pallas kernels: 43.5 us -> 17.4 us
  starting transfers between devices: 63.6 us -> 46.8 us
  waiting for transfers between devices: 85.6 us -> 72.8 us
  other arithmetic: 6.14 us -> 1.67 us
  local copies, waits for them, and re-layouts: 8.52 us -> 4.05 us
    pallas_call x10, Pallas kernels: 43.5 us -> 17.4 us  [call(): pl.pallas_call(body, out_shape=outs, scratch_shapes=list(scratch), compil...]
    ppermute x39 -> x24, starting transfers between devices: 63.6 us -> 46.7 us  [fetch(): return lax.ppermute(value, AXES, pairs(dx, dy, dz, swap))]
    ppermute x39 -> x24, waiting for transfers between devices: 81.2 us -> 72.8 us  [fetch(): return lax.ppermute(value, AXES, pairs(dx, dy, dz, swap))]
    unnamed x92 -> x14, local copies, waits for them, and re-layouts: 7.06 us -> 2.61 us
    ppermute x1, waiting for transfers between devices: 4.38 us -> 0.01 us  [pair_low(): return lax.ppermute(value, AXES, sorted(out))]
  transfers between devices with their start and end apart: 40 -> 25, of which waited for: 24 -> 17; matrix products, arithmetic and copies ran while one was open for 3% -> 2% of each run, Pallas kernels for 17% -> 6%
where the time goes in v3:
time: 144 us
  waiting for transfers between devices  72.8 us (51%)
  starting transfers between devices  46.8 us (32%)
  Pallas kernels  17.4 us (12%)
  local copies, waits for them, and re-layouts  4.05 us (3%)
  other arithmetic  1.67 us (1%)
    ppermute x24, waiting for transfers between devices, fetch(): return lax.ppermute(value, AXES, pairs(dx, dy, dz, swap))  72.8 us
    ppermute x24, starting transfers between devices, fetch(): return lax.ppermute(value, AXES, pairs(dx, dy, dz, swap))  46.7 us
    pallas_call x10, Pallas kernels, call(): pl.pallas_call(body, out_shape=outs, scratch_shapes=list(scratch), compil...  17.4 us
  transfers between devices with their start and end apart: 25, of which 17 were waited for; matrix products, arithmetic and copies ran while one was open for 2% of the time, Pallas kernels for 6%

profile of v3, /device:TPU:1, one launch (start us, length us, event | category | flops | bytes accessed | tf_op | source)
XLA Modules:
  0.0 143.5 jit_solution(4340501289020643649)
XLA Ops:
  3.2 4.2 %shard_map.94 = (bf16[4,128,1024]{2,1,0:T(8,128)(2,1)S(1)}, bf16[4,128,1024]{2,1,0:T(8,128)(2,1)S(1)}, f32[2,8,1024]{2,1,0:T(8,128)S(1)}) custom-call(bf16[2,16,16,1024]{3,2,1,0:T(8,128)(2,1)S(1)} %copy-done.5, f32[1,1024]{1,0:T(1,128)S(1)} %bitcast.13, f32[1,1024]{1,0:T(1,128)S(1)} %bitcast.15), custom_call_target="tpu_custom_call" | custom-call | flops 10000000000 | bytes 3219456 | tf_op jit(solution)/shard_map/pallas_call | solution.py:84
  7.4 3.3 %collective-permute-start.4 = (bf16[4,128,1024]{2,1,0:T(8,128)(2,1)S(1)}, bf16[4,128,1024]{2,1,0:T(8,128)(2,1)S(1)}, u32[]{:S(2)}, u32[]{:S(2)}) collective-permute-start(bf16[4,128,1024]{2,1,0:T(8,128)(2,1)S(1)} %get-tuple-element.25.act_own.refs_4_), channel_id=1, source_target_pairs={{0,1},{1,0},{2,3},{3,2},{4,5},{5,4},{6,7},{7,6},{8,9},{9,8},{10,11... | collective-permute-start | bytes 3145736 | tf_op jit(solution)/shard_map/from_x0_y0_z0_core1/ppermute | solution.py:54
  14.6 5.1 %collective-permute-start.2 = (bf16[36,16,256]{2,1,0:T(8,128)(2,1)S(1)}, bf16[36,16,256]{2,1,0:T(8,128)(2,1)S(1)}, u32[]{:S(2)}, u32[]{:S(2)}) collective-permute-start(bf16[36,16,256]{2,1,0:T(8,128)(2,1)S(1)} %shard_map.93.a0), channel_id=1, source_target_pairs={{0,16},{1,17},{2,18},{3,19},{4,20},{5,21},{6,22},{7,23},{8,24},{9,... | collective-permute-start | bytes 884744 | tf_op jit(solution)/shard_map/from_x0_y0_z4_core0/ppermute | solution.py:54
  19.8 2.4 %collective-permute-start.3 = (bf16[36,16,256]{2,1,0:T(8,128)(2,1)S(1)}, bf16[36,16,256]{2,1,0:T(8,128)(2,1)S(1)}, u32[]{:S(2)}, u32[]{:S(2)}) collective-permute-start(bf16[36,16,256]{2,1,0:T(8,128)(2,1)S(1)} %shard_map.93.a0), channel_id=1, source_target_pairs={{0,8},{1,25},{2,10},{3,27},{4,12},{5,29},{6,14},{7,31},{8,16},{9,1... | collective-permute-start | bytes 884744 | tf_op jit(solution)/shard_map/from_x0_y0_z6_core0/ppermute | solution.py:54
  22.1 3.2 %shard_map.95 = (bf16[17,9,16,256]{3,2,1,0:T(8,128)(2,1)S(1)}, bf16[17,9,16,256]{3,2,1,0:T(8,128)(2,1)S(1)}, bf16[17,9,16,256]{3,2,1,0:T(8,128)(2,1)S(1)}, bf16[17,9,16,256]{3,2,1,0:T(8,128)(2,1)S(1)}) custom-call(bf16[4,128,1024]{2,1,0:T(8,128)(2,1)S(1)} %get-tuple-element.25.act_own.refs_4_, ...), custom_call_target="tpu_custom_call" | custom-call | flops 20000000000 | bytes 7241728 | tf_op jit(solution)/shard_map/pallas_call | solution.py:84
  26.7 2.4 %collective-permute-start.12 = (bf16[17,9,16,256]{3,2,1,0:T(8,128)(2,1)S(1)}, bf16[17,9,16,256]{3,2,1,0:T(8,128)(2,1)S(1)}, u32[]{:S(2)}, u32[]{:S(2)}) collective-permute-start(bf16[17,9,16,256]{3,2,1,0:T(8,128)(2,1)S(1)} %get-tuple-element.34), channel_id=1, source_target_pairs={{0,64},{1,65},{2,66},{3,67},{4,68},{5,69},{6,70},{7,71},{8,72},{9,... | collective-permute-start | bytes 3760136 | tf_op jit(solution)/shard_map/from_x2_y0_z0_core0/ppermute | solution.py:54
  30.3 8.1 %collective-permute-done.2.a2 = bf16[36,16,256]{2,1,0:T(8,128)(2,1)S(1)} collective-permute-done((bf16[36,16,256]{2,1,0:T(8,128)(2,1)S(1)}, bf16[36,16,256]{2,1,0:T(8,128)(2,1)S(1)}, u32[]{:S(2)}, u32[]{:S(2)}) %collective-permute-start.2) | collective-permute-done | bytes 294944 | tf_op jit(solution)/shard_map/from_x0_y0_z4_core0/ppermute | solution.py:54
  38.5 7.2 %collective-permute-start.6 = (bf16[4,36,16,256]{3,2,1,0:T(8,128)(2,1)S(1)}, bf16[4,36,16,256]{3,2,1,0:T(8,128)(2,1)S(1)}, u32[]{:S(2)}, u32[]{:S(2)}) collective-permute-start(bf16[4,36,16,256]{3,2,1,0:T(8,128)(2,1)S(1)} %shard_map.96.refs_0_), channel_id=1, source_target_pairs={{0,6},{1,3},{2,0},{3,5},{4,2},{5,7},{6,4},{7,1},{8,14},{9,11},{10,... | collective-permute-start | bytes 3538952 | tf_op jit(solution)/shard_map/from_x0_y1_z0_core0/ppermute | solution.py:54
  45.8 15.3 %collective-permute-done.6.refs_1_ = bf16[4,36,16,256]{3,2,1,0:T(8,128)(2,1)S(1)} collective-permute-done((bf16[4,36,16,256]{3,2,1,0:T(8,128)(2,1)S(1)}, bf16[4,36,16,256]{3,2,1,0:T(8,128)(2,1)S(1)}, u32[]{:S(2)}, u32[]{:S(2)}) %collective-permute-start.6) | collective-permute-done | bytes 1179680 | tf_op jit(solution)/shard_map/from_x0_y1_z0_core0/ppermute | solution.py:54
  61.1 13.4 %collective-permute-done.11.refs_1_ = bf16[17,9,16,256]{3,2,1,0:T(8,128)(2,1)S(1)} collective-permute-done((bf16[17,9,16,256]{3,2,1,0:T(8,128)(2,1)S(1)}, bf16[17,9,16,256]{3,2,1,0:T(8,128)(2,1)S(1)}, u32[]{:S(2)}, u32[]{:S(2)}) %collective-permute-start.11) | collective-permute-done | bytes 1253408 | tf_op jit(solution)/shard_map/from_x1_y0_z0_core0/ppermute | solution.py:54
  74.5 6.7 %collective-permute-done.12.refs_2_ = bf16[17,9,16,256]{3,2,1,0:T(8,128)(2,1)S(1)} collective-permute-done((bf16[17,9,16,256]{3,2,1,0:T(8,128)(2,1)S(1)}, bf16[17,9,16,256]{3,2,1,0:T(8,128)(2,1)S(1)}, u32[]{:S(2)}, u32[]{:S(2)}) %collective-permute-start.12) | collective-permute-done | bytes 1253408 | tf_op jit(solution)/shard_map/from_x2_y0_z0_core0/ppermute | solution.py:54
  84.6 2.6 %collective-permute-start.15 = (bf16[37,16,256]{2,1,0:T(8,128)(2,1)S(1)}, bf16[37,16,256]{2,1,0:T(8,128)(2,1)S(1)}, u32[]{:S(2)}, u32[]{:S(2)}) collective-permute-start(bf16[37,16,256]{2,1,0:T(8,128)(2,1)S(1)} %get-tuple-element.38), channel_id=1, source_target_pairs={{0,4},{1,5},{2,6},{3,7},{4,0},{5,1},{6,2},{7,3},{8,12},{9,13},{10,... | collective-permute-start | bytes 909320 | tf_op jit(solution)/shard_map/from_x0_y2_z0_core0/ppermute | solution.py:54
  90.2 7.8 %collective-permute-done.15.refs_2_ = bf16[37,16,256]{2,1,0:T(8,128)(2,1)S(1)} collective-permute-done((bf16[37,16,256]{2,1,0:T(8,128)(2,1)S(1)}, bf16[37,16,256]{2,1,0:T(8,128)(2,1)S(1)}, u32[]{:S(2)}, u32[]{:S(2)}) %collective-permute-start.15) | collective-permute-done | bytes 303136 | tf_op jit(solution)/shard_map/from_x0_y2_z0_core0/ppermute | solution.py:54
  98.0 3.1 %collective-permute-done.16.refs_3_ = bf16[37,16,256]{2,1,0:T(8,128)(2,1)S(1)} collective-permute-done((bf16[37,16,256]{2,1,0:T(8,128)(2,1)S(1)}, bf16[37,16,256]{2,1,0:T(8,128)(2,1)S(1)}, u32[]{:S(2)}, u32[]{:S(2)}) %collective-permute-start.16) | collective-permute-done | bytes 303136 | tf_op jit(solution)/shard_map/from_x0_y3_z0_core0/ppermute | solution.py:54
  102.1 1.9 %collective-permute-start.18 = (bf16[10,16,256]{2,1,0:T(8,128)(2,1)S(1)}, bf16[10,16,256]{2,1,0:T(8,128)(2,1)S(1)}, u32[]{:S(2)}, u32[]{:S(2)}) collective-permute-start(bf16[10,16,256]{2,1,0:T(8,128)(2,1)S(1)} %get-tuple-element.42), channel_id=1, source_target_pairs={{0,16},{1,17},{2,18},{3,19},{4,20},{5,21},{6,22},{7,23},{8,24},{9,... | collective-permute-start | bytes 245768 | tf_op jit(solution)/shard_map/from_x0_y0_z4_core0/ppermute | solution.py:54
  104.1 2.4 %collective-permute-start.19 = (bf16[10,16,256]{2,1,0:T(8,128)(2,1)S(1)}, bf16[10,16,256]{2,1,0:T(8,128)(2,1)S(1)}, u32[]{:S(2)}, u32[]{:S(2)}) collective-permute-start(bf16[10,16,256]{2,1,0:T(8,128)(2,1)S(1)} %get-tuple-element.43), channel_id=1, source_target_pairs={{0,8},{1,25},{2,10},{3,27},{4,12},{5,29},{6,14},{7,31},{8,16},{9,1... | collective-permute-start | bytes 245768 | tf_op jit(solution)/shard_map/from_x0_y0_z6_core0/ppermute | solution.py:54
  107.2 2.1 %collective-permute-done.18.refs_2_ = bf16[10,16,256]{2,1,0:T(8,128)(2,1)S(1)} collective-permute-done((bf16[10,16,256]{2,1,0:T(8,128)(2,1)S(1)}, bf16[10,16,256]{2,1,0:T(8,128)(2,1)S(1)}, u32[]{:S(2)}, u32[]{:S(2)}) %collective-permute-start.18) | collective-permute-done | bytes 81952 | tf_op jit(solution)/shard_map/from_x0_y0_z4_core0/ppermute | solution.py:54
  109.3 4.2 %collective-permute-done.19.refs_3_ = bf16[10,16,256]{2,1,0:T(8,128)(2,1)S(1)} collective-permute-done((bf16[10,16,256]{2,1,0:T(8,128)(2,1)S(1)}, bf16[10,16,256]{2,1,0:T(8,128)(2,1)S(1)}, u32[]{:S(2)}, u32[]{:S(2)}) %collective-permute-start.19) | collective-permute-done | bytes 81952 | tf_op jit(solution)/shard_map/from_x0_y0_z6_core0/ppermute | solution.py:54
  113.9 4.3 %shard_map.97 = (bf16[128,256]{1,0:T(8,128)(2,1)S(1)}, bf16[128,256]{1,0:T(8,128)(2,1)S(1)}, f32[4,128,1024]{2,1,0:T(8,128)S(1)}, bf16[4,128,1024]{2,1,0:T(8,128)(2,1)S(1)}) custom-call(bf16[4,36,16,256]{3,2,1,0:T(8,128)(2,1)S(1)} %shard_map.96.refs_0_, bf16[4,36,16,256]{3,2,1,0:T(8,128)(2,1)S(1)} %collective-permute-done.6.refs_1_, ...), custom_call_target="tpu_custom_call" | custom-call | flops 1000000000 | bytes 10224640 | tf_op jit(solution)/shard_map/pallas_call | solution.py:84
  118.2 4.5 %collective-permute-start.10 = (bf16[4,128,1024]{2,1,0:T(8,128)(2,1)S(1)}, bf16[4,128,1024]{2,1,0:T(8,128)(2,1)S(1)}, u32[]{:S(2)}, u32[]{:S(2)}) collective-permute-start(bf16[4,128,1024]{2,1,0:T(8,128)(2,1)S(1)} %get-tuple-element.31), channel_id=1, source_target_pairs={{0,1},{1,0},{2,3},{3,2},{4,5},{5,4},{6,7},{7,6},{8,9},{9,8},{10,11... | collective-permute-start | bytes 3145736 | tf_op jit(solution)/shard_map/from_x0_y0_z0_core1/ppermute | solution.py:54
  123.9 3.4 %collective-permute-start.22 = (f32[9,16,256]{2,1,0:T(8,128)S(1)}, f32[9,16,256]{2,1,0:T(8,128)S(1)}, u32[]{:S(2)}, u32[]{:S(2)}) collective-permute-start(f32[9,16,256]{2,1,0:T(8,128)S(1)} %slice.40), channel_id=1, source_target_pairs={{0,64},{1,65},{2,66},{3,67},{4,68},{5,69},{6,70},{7,71},{8,72},{9,... | collective-permute-start | bytes 442376 | tf_op jit(solution)/shard_map/from_x2_y0_z0_core0/ppermute | solution.py:54
  128.7 3.6 %collective-permute-done.22.f2 = f32[9,16,256]{2,1,0:T(8,128)S(1)} collective-permute-done((f32[9,16,256]{2,1,0:T(8,128)S(1)}, f32[9,16,256]{2,1,0:T(8,128)S(1)}, u32[]{:S(2)}, u32[]{:S(2)}) %collective-permute-start.22) | collective-permute-done | bytes 147488 | tf_op jit(solution)/shard_map/from_x2_y0_z0_core0/ppermute | solution.py:54
  133.5 1.9 %collective-permute-start.24 = (f32[19,16,256]{2,1,0:T(8,128)S(1)}, f32[19,16,256]{2,1,0:T(8,128)S(1)}, u32[]{:S(2)}, u32[]{:S(2)}) collective-permute-start(f32[19,16,256]{2,1,0:T(8,128)S(1)} %get-tuple-element.45), channel_id=1, source_target_pairs={{0,1},{1,0},{2,3},{3,2},{4,5},{5,4},{6,7},{7,6},{8,9},{9,8},{10,11... | collective-permute-start | bytes 933896 | tf_op jit(solution)/shard_map/from_x0_y0_z0_core1/ppermute | solution.py:54
  138.9 4.6 %shard_map.98 = bf16[2,16,16,1024]{3,2,1,0:T(8,128)(2,1)} custom-call(bf16[4,128,1024]{2,1,0:T(8,128)(2,1)S(1)} %get-tuple-element.29.xp_ref, f32[4,128,1024]{2,1,0:T(8,128)S(1)} %get-tuple-element.30.own_ref, bf16[4,128,1024]{2,1,0:T(8,128)(2,1)S(1)} %collective-permute-done.10.got_ref, f32[1,1024]{1,0:T(1,128)S(1)} %bitcast.14, f32[1,1024]{1,0:T(1,128)S(1)} %bitcast.16, ...), custom_call_target="tpu_custom_call" | custom-call | flops 10000000 | bytes 5316608 | tf_op jit(solution)/shard_map/pallas_call | solution.py:84
  (59 shorter events, 24.8 us)
Async XLA Ops:
  7.4 14.7 %collective-permute-start.4 = (bf16[4,128,1024]{2,1,0:T(8,128)(2,1)S(1)}, bf16[4,128,1024]{2,1,0:T(8,128)(2,1)S(1)}, u32[]{:S(2)}, u32[]{:S(2)}) collective-permute-start(bf16[4,128,1024]{2,1,0:T(8,128)(2,1)S(1)} %get-tuple-element.25.act_own.refs_4_), channel_id=1, source_target_pairs={{0,1},{1,0},{2,3},{3,2},{4,5},{5,4},{6,7},{7,6},{8,9},{9,8},{10,11... | collective-permute-start | bytes 3145736 | tf_op jit(solution)/shard_map/from_x0_y0_z0_core1/ppermute | solution.py:54
  11.8 10.3 %collective-permute-start.5 = (bf16[128,256]{1,0:T(8,128)(2,1)S(1)}, bf16[128,256]{1,0:T(8,128)(2,1)S(1)}, u32[]{:S(2)}, u32[]{:S(2)}) collective-permute-start(bf16[128,256]{1,0:T(8,128)(2,1)S(1)} %get-tuple-element.46), channel_id=1, source_target_pairs={{0,1},{1,0},{2,3},{3,2},{4,5},{5,4},{6,7},{7,6},{8,9},{9,8},{10,11... | collective-permute-start | bytes 196616 | tf_op jit(solution)/shard_map/from_x0_y0_z0_core1/ppermute | solution.py:54
  13.3 15.8 %collective-permute-start.1 = (bf16[36,16,256]{2,1,0:T(8,128)(2,1)S(1)}, bf16[36,16,256]{2,1,0:T(8,128)(2,1)S(1)}, u32[]{:S(2)}, u32[]{:S(2)}) collective-permute-start(bf16[36,16,256]{2,1,0:T(8,128)(2,1)S(1)} %shard_map.93.a0), channel_id=1, source_target_pairs={{0,24},{1,9},{2,26},{3,11},{4,28},{5,13},{6,30},{7,15},{8,0},{9,17... | collective-permute-start | bytes 884744 | tf_op jit(solution)/shard_map/from_x0_y0_z2_core0/ppermute | solution.py:54
  14.6 23.8 %collective-permute-start.2 = (bf16[36,16,256]{2,1,0:T(8,128)(2,1)S(1)}, bf16[36,16,256]{2,1,0:T(8,128)(2,1)S(1)}, u32[]{:S(2)}, u32[]{:S(2)}) collective-permute-start(bf16[36,16,256]{2,1,0:T(8,128)(2,1)S(1)} %shard_map.93.a0), channel_id=1, source_target_pairs={{0,16},{1,17},{2,18},{3,19},{4,20},{5,21},{6,22},{7,23},{8,24},{9,... | collective-permute-start | bytes 884744 | tf_op jit(solution)/shard_map/from_x0_y0_z4_core0/ppermute | solution.py:54
  19.8 18.7 %collective-permute-start.3 = (bf16[36,16,256]{2,1,0:T(8,128)(2,1)S(1)}, bf16[36,16,256]{2,1,0:T(8,128)(2,1)S(1)}, u32[]{:S(2)}, u32[]{:S(2)}) collective-permute-start(bf16[36,16,256]{2,1,0:T(8,128)(2,1)S(1)} %shard_map.93.a0), channel_id=1, source_target_pairs={{0,8},{1,25},{2,10},{3,27},{4,12},{5,29},{6,14},{7,31},{8,16},{9,1... | collective-permute-start | bytes 884744 | tf_op jit(solution)/shard_map/from_x0_y0_z6_core0/ppermute | solution.py:54
  25.4 49.1 %collective-permute-start.11 = (bf16[17,9,16,256]{3,2,1,0:T(8,128)(2,1)S(1)}, bf16[17,9,16,256]{3,2,1,0:T(8,128)(2,1)S(1)}, u32[]{:S(2)}, u32[]{:S(2)}) collective-permute-start(bf16[17,9,16,256]{3,2,1,0:T(8,128)(2,1)S(1)} %get-tuple-element.33), channel_id=1, source_target_pairs={{0,96},{1,33},{2,98},{3,35},{4,100},{5,37},{6,102},{7,39},{8,104},... | collective-permute-start | bytes 3760136 | tf_op jit(solution)/shard_map/from_x1_y0_z0_core0/ppermute | solution.py:54
  26.7 54.6 %collective-permute-start.12 = (bf16[17,9,16,256]{3,2,1,0:T(8,128)(2,1)S(1)}, bf16[17,9,16,256]{3,2,1,0:T(8,128)(2,1)S(1)}, u32[]{:S(2)}, u32[]{:S(2)}) collective-permute-start(bf16[17,9,16,256]{3,2,1,0:T(8,128)(2,1)S(1)} %get-tuple-element.34), channel_id=1, source_target_pairs={{0,64},{1,65},{2,66},{3,67},{4,68},{5,69},{6,70},{7,71},{8,72},{9,... | collective-permute-start | bytes 3760136 | tf_op jit(solution)/shard_map/from_x2_y0_z0_core0/ppermute | solution.py:54
  29.1 53.5 %collective-permute-start.13 = (bf16[17,9,16,256]{3,2,1,0:T(8,128)(2,1)S(1)}, bf16[17,9,16,256]{3,2,1,0:T(8,128)(2,1)S(1)}, u32[]{:S(2)}, u32[]{:S(2)}) collective-permute-start(bf16[17,9,16,256]{3,2,1,0:T(8,128)(2,1)S(1)} %get-tuple-element.35), channel_id=1, source_target_pairs={{0,32},{1,97},{2,34},{3,99},{4,36},{5,101},{6,38},{7,103},{8,40},{... | collective-permute-start | bytes 3760136 | tf_op jit(solution)/shard_map/from_x3_y0_z0_core0/ppermute | solution.py:54
  38.5 22.6 %collective-permute-start.6 = (bf16[4,36,16,256]{3,2,1,0:T(8,128)(2,1)S(1)}, bf16[4,36,16,256]{3,2,1,0:T(8,128)(2,1)S(1)}, u32[]{:S(2)}, u32[]{:S(2)}) collective-permute-start(bf16[4,36,16,256]{3,2,1,0:T(8,128)(2,1)S(1)} %shard_map.96.refs_0_), channel_id=1, source_target_pairs={{0,6},{1,3},{2,0},{3,5},{4,2},{5,7},{6,4},{7,1},{8,14},{9,11},{10,... | collective-permute-start | bytes 3538952 | tf_op jit(solution)/shard_map/from_x0_y1_z0_core0/ppermute | solution.py:54
  61.1 27.2 %collective-permute-start.7 = (bf16[4,36,16,256]{3,2,1,0:T(8,128)(2,1)S(1)}, bf16[4,36,16,256]{3,2,1,0:T(8,128)(2,1)S(1)}, u32[]{:S(2)}, u32[]{:S(2)}) collective-permute-start(bf16[4,36,16,256]{3,2,1,0:T(8,128)(2,1)S(1)} %collective-permute-done.6.refs_1_), channel_id=1, source_target_pairs={{0,6},{1,3},{2,0},{3,5},{4,2},{5,7},{6,4},{7,1},{8,14},{9,11},{10,... | collective-permute-start | bytes 3538952 | tf_op jit(solution)/shard_map/from_x0_y1_z0_core0/ppermute | solution.py:54
  83.2 7.0 %collective-permute-start.14 = (bf16[37,16,256]{2,1,0:T(8,128)(2,1)S(1)}, bf16[37,16,256]{2,1,0:T(8,128)(2,1)S(1)}, u32[]{:S(2)}, u32[]{:S(2)}) collective-permute-start(bf16[37,16,256]{2,1,0:T(8,128)(2,1)S(1)} %get-tuple-element.37), channel_id=1, source_target_pairs={{0,6},{1,3},{2,0},{3,5},{4,2},{5,7},{6,4},{7,1},{8,14},{9,11},{10,... | collective-permute-start | bytes 909320 | tf_op jit(solution)/shard_map/from_x0_y1_z0_core0/ppermute | solution.py:54
  84.6 13.4 %collective-permute-start.15 = (bf16[37,16,256]{2,1,0:T(8,128)(2,1)S(1)}, bf16[37,16,256]{2,1,0:T(8,128)(2,1)S(1)}, u32[]{:S(2)}, u32[]{:S(2)}) collective-permute-start(bf16[37,16,256]{2,1,0:T(8,128)(2,1)S(1)} %get-tuple-element.38), channel_id=1, source_target_pairs={{0,4},{1,5},{2,6},{3,7},{4,0},{5,1},{6,2},{7,3},{8,12},{9,13},{10,... | collective-permute-start | bytes 909320 | tf_op jit(solution)/shard_map/from_x0_y2_z0_core0/ppermute | solution.py:54
  87.2 13.9 %collective-permute-start.16 = (bf16[37,16,256]{2,1,0:T(8,128)(2,1)S(1)}, bf16[37,16,256]{2,1,0:T(8,128)(2,1)S(1)}, u32[]{:S(2)}, u32[]{:S(2)}) collective-permute-start(bf16[37,16,256]{2,1,0:T(8,128)(2,1)S(1)} %get-tuple-element.39), channel_id=1, source_target_pairs={{0,2},{1,7},{2,4},{3,1},{4,6},{5,3},{6,0},{7,5},{8,10},{9,15},{10,... | collective-permute-start | bytes 909320 | tf_op jit(solution)/shard_map/from_x0_y3_z0_core0/ppermute | solution.py:54
  88.3 25.6 %collective-permute-start.8 = (bf16[4,36,16,256]{3,2,1,0:T(8,128)(2,1)S(1)}, bf16[4,36,16,256]{3,2,1,0:T(8,128)(2,1)S(1)}, u32[]{:S(2)}, u32[]{:S(2)}) collective-permute-start(bf16[4,36,16,256]{3,2,1,0:T(8,128)(2,1)S(1)} %collective-permute-done.7.refs_2_), channel_id=1, source_target_pairs={{0,6},{1,3},{2,0},{3,5},{4,2},{5,7},{6,4},{7,1},{8,14},{9,11},{10,... | collective-permute-start | bytes 3538952 | tf_op jit(solution)/shard_map/from_x0_y1_z0_core0/ppermute | solution.py:54
  101.3 6.0 %collective-permute-start.17 = (bf16[10,16,256]{2,1,0:T(8,128)(2,1)S(1)}, bf16[10,16,256]{2,1,0:T(8,128)(2,1)S(1)}, u32[]{:S(2)}, u32[]{:S(2)}) collective-permute-start(bf16[10,16,256]{2,1,0:T(8,128)(2,1)S(1)} %get-tuple-element.41), channel_id=1, source_target_pairs={{0,24},{1,9},{2,26},{3,11},{4,28},{5,13},{6,30},{7,15},{8,0},{9,17... | collective-permute-start | bytes 245768 | tf_op jit(solution)/shard_map/from_x0_y0_z2_core0/ppermute | solution.py:54
  102.1 7.2 %collective-permute-start.18 = (bf16[10,16,256]{2,1,0:T(8,128)(2,1)S(1)}, bf16[10,16,256]{2,1,0:T(8,128)(2,1)S(1)}, u32[]{:S(2)}, u32[]{:S(2)}) collective-permute-start(bf16[10,16,256]{2,1,0:T(8,128)(2,1)S(1)} %get-tuple-element.42), channel_id=1, source_target_pairs={{0,16},{1,17},{2,18},{3,19},{4,20},{5,21},{6,22},{7,23},{8,24},{9,... | collective-permute-start | bytes 245768 | tf_op jit(solution)/shard_map/from_x0_y0_z4_core0/ppermute | solution.py:54
  104.1 9.4 %collective-permute-start.19 = (bf16[10,16,256]{2,1,0:T(8,128)(2,1)S(1)}, bf16[10,16,256]{2,1,0:T(8,128)(2,1)S(1)}, u32[]{:S(2)}, u32[]{:S(2)}) collective-permute-start(bf16[10,16,256]{2,1,0:T(8,128)(2,1)S(1)} %get-tuple-element.43), channel_id=1, source_target_pairs={{0,8},{1,25},{2,10},{3,27},{4,12},{5,29},{6,14},{7,31},{8,16},{9,1... | collective-permute-start | bytes 245768 | tf_op jit(solution)/shard_map/from_x0_y0_z6_core0/ppermute | solution.py:54
  113.5 9.2 %collective-permute-start.20 = (f32[10,16,256]{2,1,0:T(8,128)S(1)}, f32[10,16,256]{2,1,0:T(8,128)S(1)}, u32[]{:S(2)}, u32[]{:S(2)}) collective-permute-start(f32[10,16,256]{2,1,0:T(8,128)S(1)} %shard_map.101), channel_id=1, source_target_pairs={{0,128},{1,129},{2,130},{3,131},{4,132},{5,133},{6,134},{7,135},{8... | collective-permute-start | bytes 491528 | tf_op jit(solution)/shard_map/from_z_low/ppermute | solution.py:65
  118.2 20.6 %collective-permute-start.10 = (bf16[4,128,1024]{2,1,0:T(8,128)(2,1)S(1)}, bf16[4,128,1024]{2,1,0:T(8,128)(2,1)S(1)}, u32[]{:S(2)}, u32[]{:S(2)}) collective-permute-start(bf16[4,128,1024]{2,1,0:T(8,128)(2,1)S(1)} %get-tuple-element.31), channel_id=1, source_target_pairs={{0,1},{1,0},{2,3},{3,2},{4,5},{5,4},{6,7},{7,6},{8,9},{9,8},{10,11... | collective-permute-start | bytes 3145736 | tf_op jit(solution)/shard_map/from_x0_y0_z0_core1/ppermute | solution.py:54
  122.8 5.9 %collective-permute-start.21 = (f32[9,16,256]{2,1,0:T(8,128)S(1)}, f32[9,16,256]{2,1,0:T(8,128)S(1)}, u32[]{:S(2)}, u32[]{:S(2)}) collective-permute-start(f32[9,16,256]{2,1,0:T(8,128)S(1)} %slice.40), channel_id=1, source_target_pairs={{0,96},{1,33},{2,98},{3,35},{4,100},{5,37},{6,102},{7,39},{8,104},... | collective-permute-start | bytes 442376 | tf_op jit(solution)/shard_map/from_x1_y0_z0_core0/ppermute | solution.py:54
  123.9 8.3 %collective-permute-start.22 = (f32[9,16,256]{2,1,0:T(8,128)S(1)}, f32[9,16,256]{2,1,0:T(8,128)S(1)}, u32[]{:S(2)}, u32[]{:S(2)}) collective-permute-start(f32[9,16,256]{2,1,0:T(8,128)S(1)} %slice.40), channel_id=1, source_target_pairs={{0,64},{1,65},{2,66},{3,67},{4,68},{5,69},{6,70},{7,71},{8,72},{9,... | collective-permute-start | bytes 442376 | tf_op jit(solution)/shard_map/from_x2_y0_z0_core0/ppermute | solution.py:54
  127.3 6.1 %collective-permute-start.23 = (f32[9,16,256]{2,1,0:T(8,128)S(1)}, f32[9,16,256]{2,1,0:T(8,128)S(1)}, u32[]{:S(2)}, u32[]{:S(2)}) collective-permute-start(f32[9,16,256]{2,1,0:T(8,128)S(1)} %slice.40), channel_id=1, source_target_pairs={{0,32},{1,97},{2,34},{3,99},{4,36},{5,101},{6,38},{7,103},{8,40},{... | collective-permute-start | bytes 442376 | tf_op jit(solution)/shard_map/from_x3_y0_z0_core0/ppermute | solution.py:54
  133.5 3.2 %collective-permute-start.24 = (f32[19,16,256]{2,1,0:T(8,128)S(1)}, f32[19,16,256]{2,1,0:T(8,128)S(1)}, u32[]{:S(2)}, u32[]{:S(2)}) collective-permute-start(f32[19,16,256]{2,1,0:T(8,128)S(1)} %get-tuple-element.45), channel_id=1, source_target_pairs={{0,1},{1,0},{2,3},{3,2},{4,5},{5,4},{6,7},{7,6},{8,9},{9,8},{10,11... | collective-permute-start | bytes 933896 | tf_op jit(solution)/shard_map/from_x0_y0_z0_core1/ppermute | solution.py:54
  135.5 2.7 %collective-permute-start.9 = (bf16[128,256]{1,0:T(8,128)(2,1)S(1)}, bf16[128,256]{1,0:T(8,128)(2,1)S(1)}, u32[]{:S(2)}, u32[]{:S(2)}) collective-permute-start(bf16[128,256]{1,0:T(8,128)(2,1)S(1)} %get-tuple-element.28), channel_id=1, source_target_pairs={{0,1},{1,0},{2,3},{3,2},{4,5},{5,4},{6,7},{7,6},{8,9},{9,8},{10,11... | collective-permute-start | bytes 196616 | tf_op jit(solution)/shard_map/from_x0_y0_z0_core1/ppermute | solution.py:54
  (8 other events, 22.4 us)

commit v4 on v3

--- a/solution.py
+++ b/solution.py
@@ -17,7 +17,8 @@
 EPS = 1e-05
 MIB = 1024 * 1024
 CHUNK, PER_CHIP, QUARTER = 16, 36, 9
-COST_NORM, COST_WGRAD, COST_CONV, COST_BACK, COST_SUM = 10**10, 2*10**10, 10**9, 10**7, 10**10
+COST_NORM, COST_WGRAD, COST_CONV, COST_BACK, COST_SUM, COST_SPREAD, COST_MARK = 10**10, 2 * 10**10, 10**10, 10**9, 10**10, 10**10, 3 * 10**10
+MOVED_CONV, MOVED_BACK, COST_PLACE = 0, 0, 2 * 10**10
 TAPS = [(ky, kx) for ky in range(3) for kx in range(3)]
 
 
@@ -69,11 +70,16 @@
     return lax.rem(index + jnp.where(core == 0, step, 4 - step), 4)
 
 
-def call(body, outs, args, flops=0, moved=None, scratch=(), specs=None, out_specs=None, grid=None, vmem=8, **kw):
+def call(body, outs, args, flops=0, moved=None, scratch=(), specs=None, out_specs=None, grid=None, vmem=8, after=(), **kw):
+    if after:
+        inner, count = body, len(args)
+        body = lambda *refs: inner(*refs[:count], *refs[count + len(after) :])
+        if specs is None:
+            specs = [pl.BlockSpec(memory_space=pltpu.VMEM)] * count
+        specs = list(specs) + [pl.BlockSpec(memory_space=pl.ANY)] * len(after)
+        args = (*args, *after)
     if moved is None:
-        moved = sum(a.size * a.dtype.itemsize for a in args) + sum(
-            o.size * o.dtype.itemsize for o in outs
-        )
+        moved = sum(a.size * a.dtype.itemsize for a in (*args[: len(args) - len(after)], *outs))
     params = dict(kw)
     if grid is not None:
         params["grid"] = grid
@@ -137,7 +143,7 @@
                 plane_ref[2 * pi + pj, rows, :] = xp.astype(BF)
 
 
-def norm_forward(images, gain, bias):
+def norm_forward(images, gain, bias, after):
     plane = arr((4, 128, CIN), BF)
     vec = pl.BlockSpec((1, LANES), lambda c: (0, c))
     block = pl.BlockSpec((4, 128, LANES), lambda c: (0, 0, c))
@@ -150,10 +156,17 @@
         grid=(CIN // LANES,),
         specs=[pl.BlockSpec((2, 16, 16, LANES), lambda c: (0, 0, 0, c)), vec, vec],
         out_specs=(block, block, pl.BlockSpec((2, 8, LANES), lambda c: (0, 0, c))),
-    )
-
-
-def norm_back_body(xp_ref, own_ref, got_ref, gain_ref, bias_ref, stat_ref, out_ref, *bufs):
+        after=after,
+    )
+
+
+def norm_back_body(
+    xp_ref, own_ref, got_ref, gain_ref, bias_ref, stat_ref, res_own, res_got, out_ref, res_ref, mark, *bufs
+):
+    core = position()[3]
+    for c in range(2):
+        res_ref[:, HALF * c : HALF * c + HALF] = jnp.where(core == c, res_own[...], res_got[...])
+    mark[...] = jnp.zeros_like(mark)
     gain, bias = gain_ref[...], bias_ref[...]
     mean, rstd = stat_ref[0], stat_ref[1]
     hats, grads, one, two = [], [], [], []
@@ -195,19 +208,25 @@
         out_ref[:, :, :, 128 * h : 128 * h + 128] = buf[...].astype(BF).reshape(2, 16, 16, 128)
 
 
-def norm_backward(planes, own, got, gain, bias, stat):
+def norm_backward(planes, own, got, gain, bias, stat, res_own, res_got):
     vec = pl.BlockSpec((1, LANES), lambda c: (0, c))
     block = pl.BlockSpec((4, 128, LANES), lambda c: (0, 0, c))
     return call(
         norm_back_body,
-        (arr((2, 16, 16, CIN), BF),),
-        (planes, own, got, gain.reshape(1, CIN), bias.reshape(1, CIN), stat),
+        (arr((2, 16, 16, CIN), BF), arr((128, COUT), BF), arr((8, 128), F32)),
+        (planes, own, got, gain.reshape(1, CIN), bias.reshape(1, CIN), stat, res_own, res_got),
         flops=COST_BACK,
+        moved=MOVED_BACK,
         scratch=(pltpu.VMEM((512, 128), F32),) * (LANES // 128),
         grid=(CIN // LANES,),
-        specs=[block, block, block, vec, vec, pl.BlockSpec((2, 8, LANES), lambda c: (0, 0, c))],
-        out_specs=(pl.BlockSpec((2, 16, 16, LANES), lambda c: (0, 0, 0, c)),),
-    )[0]
+        specs=[block, block, block, vec, vec, pl.BlockSpec((2, 8, LANES), lambda c: (0, 0, c))]
+        + [pl.BlockSpec((128, HALF), lambda c: (0, 0))] * 2,
+        out_specs=(
+            pl.BlockSpec((2, 16, 16, LANES), lambda c: (0, 0, 0, c)),
+            pl.BlockSpec((128, COUT), lambda c: (0, 0)),
+            pl.BlockSpec((8, 128), lambda c: (0, 0)),
+        ),
+    )
 
 
 def shifted(cot, si, sj):
@@ -239,24 +258,13 @@
 
 
 def wgrad_body(act_own, act_got, cot_own, cot_got, *refs):
-    outs = refs[:4]
-    whole, tail, turned, sem = refs[4:8]
+    ahead, here, behind, far_low, far_high, bias = refs[:6]
+    whole, turned, sem = refs[6:9]
     x, _, _, core = position()
     cot = cot_rows(cot_own, cot_got)
     moved = {(si, sj): shifted(cot, si, sj).astype(BF) for si in range(2) for sj in range(2)}
+    bias[...] = jnp.broadcast_to(jnp.sum(cot, axis=0, keepdims=True), bias.shape)
     copies = []
-
-    def send(src, dst):
-        copies.append(pltpu.make_async_copy(src, dst, sem.at[len(copies)]))
-        copies[-1].start()
-
-    bias = jnp.sum(cot, axis=0, keepdims=True)
-    high = bias.astype(BF).astype(F32)
-    row = lax.broadcasted_iota(jnp.int32, (CHUNK, HALF), 0)
-    tail[...] = jnp.zeros_like(tail)
-    tail[0, 0] = jnp.where(row == 0, high, jnp.where(row == 1, bias - high, 0.0)).astype(BF)
-    for d in range(4):
-        send(tail, outs[d].at[pl.ds(16, 1)])
     ready = set()
     for t, (ky, kx) in enumerate(TAPS):
         (pi, si), (pj, sj) = source(ky), source(kx)
@@ -273,12 +281,16 @@
         for z in range(4):
             if last_tap(z) != t:
                 continue
-            for d in range(4):
-                there = turn(x, d, core)
-                send(
-                    whole.at[pl.ds(4 * z, 4), pl.ds(QUARTER * there, QUARTER)],
-                    outs[d].at[pl.ds(4 * z, 4)],
+            far = far_low if z < 2 else far_high
+            for d, (out, at) in enumerate(((here, z), (ahead, z), (far, z % 2), (behind, z))):
+                copies.append(
+                    pltpu.make_async_copy(
+                        whole.at[pl.ds(4 * z, 4), pl.ds(QUARTER * turn(x, d, core), QUARTER)],
+                        out.at[pl.ds(4 * at, 4)],
+                        sem.at[len(copies)],
+                    )
                 )
+                copies[-1].start()
     for copy in copies:
         copy.wait()
 
@@ -286,40 +298,38 @@
 def wgrad(act_own, act_got, cot_own, cot_got):
     vm = pl.BlockSpec(memory_space=pltpu.VMEM)
     hbm = pl.BlockSpec(memory_space=pl.ANY)
+    full = arr((16, QUARTER, CHUNK, HALF), BF)
+    half = arr((8, QUARTER, CHUNK, HALF), BF)
     return call(
         wgrad_body,
-        (arr((17, QUARTER, CHUNK, HALF), BF),) * 4,
+        (full, full, full, half, half, arr((8, HALF), F32)),
         (act_own, act_got, cot_own, cot_got),
         flops=COST_WGRAD,
         scratch=(
             pltpu.VMEM((16, PER_CHIP, CHUNK, HALF), BF),
-            pltpu.VMEM((1, QUARTER, CHUNK, HALF), BF),
             pltpu.VMEM((4, CIN, 256), BF),
-            pltpu.SemaphoreType.DMA((20,)),
+            pltpu.SemaphoreType.DMA((16,)),
         ),
         specs=[vm] * 4,
-        out_specs=(hbm,) * 4,
+        out_specs=(hbm,) * 5 + (vm,),
         vmem=24,
     )
 
 
 def conv_body(*refs):
-    parts = refs[:4]
-    act_own, act_got, cot_own, cot_got, cbias = refs[4:9]
-    out_own, out_other, dact_own, dact_other = refs[9:13]
-    whole, sem = refs[13], refs[14]
+    here, ahead, behind, far_low, far_high = refs[:5]
+    act_own, act_got, cot_own, cot_got, cbias = refs[5:10]
+    out_own, out_other, dact_own, dact_other = refs[10:14]
+    whole, sem = refs[14], refs[15]
     _, y, _, core = position()
-    copies = [
-        [
-            pltpu.make_async_copy(
-                parts[d].at[z],
-                whole.at[z, turn(y, d, core)],
-                sem.at[4 * z + d],
+    copies = []
+    for z in range(4):
+        far = far_low if z < 2 else far_high
+        copies.append([])
+        for d, part in enumerate((here.at[z], ahead.at[z], far.at[z % 2], behind.at[z])):
+            copies[z].append(
+                pltpu.make_async_copy(part, whole.at[z, turn(y, d, core)], sem.at[4 * z + d])
             )
-            for d in range(4)
-        ]
-        for z in range(4)
-    ]
     for group in copies:
         for copy in group:
             copy.start()
@@ -335,12 +345,12 @@
         return jnp.concatenate(rows, axis=0)
 
     total = jnp.broadcast_to(cbias[...], (256, HALF))
-    here = 0
+    row = 0
     for t, (ky, kx) in enumerate(TAPS):
-        while here < 4 and here * 2304 < (t + 1) * CIN:
-            for copy in copies[here]:
+        while row < 4 and row * 2304 < (t + 1) * CIN:
+            for copy in copies[row]:
                 copy.wait()
-            here += 1
+            row += 1
         (pi, si), (pj, sj) = source(ky), source(kx)
         act = jnp.concatenate([act_own[2 * pi + pj], act_got[2 * pi + pj]], axis=0)
         term = jnp.dot(act, tap(t), preferred_element_type=F32)
@@ -363,7 +373,7 @@
             dact_other[2 * pi + pj] = acc[128:].astype(BF)
 
 
-def conv(parts, act_own, act_got, cot_own, cot_got, cbias):
+def conv(parts, act_own, act_got, cot_own, cot_got, cbias, after):
     vm = pl.BlockSpec(memory_space=pltpu.VMEM)
     hbm = pl.BlockSpec(memory_space=pl.ANY)
     out = arr((128, HALF), BF)
@@ -372,13 +382,15 @@
         (out, out, arr((4, 128, CIN), F32), arr((4, 128, CIN), BF)),
         (*parts, act_own, act_got, cot_own, cot_got, cbias),
         flops=COST_CONV,
+        moved=MOVED_CONV,
         scratch=(
             pltpu.VMEM((4, 4, PER_CHIP, CHUNK, HALF), BF),
             pltpu.SemaphoreType.DMA((16,)),
         ),
-        specs=[hbm] * 4 + [vm] * 5,
+        specs=[hbm] * 5 + [vm] * 5,
         out_specs=(vm,) * 4,
         vmem=32,
+        after=after,
     )
 
 
@@ -389,33 +401,42 @@
     out[pl.ds(18 * (1 - core), 18)] = theirs[...]
 
 
-def spread_z_body(a0, a1, a2, a3, _, out):
+def spread_z_body(a0, a2, a1, a3, out):
     _, _, z, core = position()
     for d, ref in enumerate((a0, a1, a2, a3)):
         out[turn(z, d, core)] = ref[...]
 
 
-def gather_kernel(kernel, core, grads):
-    vm = pl.BlockSpec(memory_space=pltpu.VMEM)
-    anywhere = pl.BlockSpec(memory_space=pl.ANY)
+def chip_block(kernel, core):
     rows = kernel.reshape(18, CHUNK, COUT)
     theirs = fetch(jnp.where(core == 0, rows[:, :, HALF:], rows[:, :, :HALF]), swap=1)
-    block = call(
-        block_body,
-        (arr((PER_CHIP, CHUNK, HALF), BF),),
-        (rows, theirs),
-    )[0]
-    got = [block] + [fetch(block, dz=2 * d) for d in range(1, 4)]
-    level = call(
-        spread_z_body,
-        (arr((4, PER_CHIP, CHUNK, HALF), BF),),
-        (*got, grads),
-        specs=[vm] * 4 + [anywhere],
-    )[0]
-    parts = [level]
-    for _ in range(3):
-        parts.append(fetch(parts[-1], dy=1))
-    return parts
+    return call(block_body, (arr((PER_CHIP, CHUNK, HALF), BF),), (rows, theirs))[0]
+
+
+def mark_body(out):
+    out[...] = jnp.zeros_like(out)
+
+
+def gather_z(block):
+    got = [block] + [fetch(block, dz=2 * d) for d in (2, 1, 3)]
+    mark = call(mark_body, (arr((8, 128), F32),), (), flops=COST_MARK, after=(got[2],))[0]
+    return mark, call(spread_z_body, (arr((4, PER_CHIP, CHUNK, HALF), BF),), got, flops=COST_SPREAD)[0]
+
+
+def across_body(ahead, behind, low, high):
+    low[...] = ahead[:2]
+    high[...] = behind[2:]
+
+
+def gather_y(level, ahead, behind, after):
+    low, high = call(
+        across_body,
+        (arr((2, PER_CHIP, CHUNK, HALF), BF),) * 2,
+        (ahead, behind),
+        vmem=12,
+        after=after,
+    )
+    return level, ahead, behind, fetch(low, dy=1), fetch(high, dy=3)
 
 
 def four(refs, index):
@@ -435,14 +456,22 @@
     return jnp.where(row == 0, high, jnp.where(row == 1, total - high, 0.0)).astype(BF)
 
 
-def sum_x_body(*refs):
-    ins, outs = refs[:4], refs[4:]
+def pass_on_body(ahead, behind, low, high, ahead_out, behind_out):
+    ahead_out[:8] = (ahead[:8].astype(F32) + low[...].astype(F32)).astype(BF)
+    ahead_out[8:] = ahead[8:]
+    behind_out[:8] = behind[:8]
+    behind_out[8:] = (behind[8:].astype(F32) + high[...].astype(F32)).astype(BF)
+
+
+def sum_x_body(own, left, right, bias_ref, *outs):
     _, y, _, core = position()
-    bias = bias_chunk(bias_four(ins, (16, 0)))
+    bias = bias_chunk(bias_ref[0:1])
     for d in range(4):
         there = turn(y, d, core)
         for z in range(4):
-            outs[d][QUARTER * z : QUARTER * z + QUARTER] = four(ins, 4 * z + there).astype(BF)
+            r = 4 * z + there
+            total = own[r].astype(F32) + (left[r].astype(F32) + right[r].astype(F32))
+            outs[d][QUARTER * z : QUARTER * z + QUARTER] = total.astype(BF)
         outs[d][4 * QUARTER] = bias
 
 
@@ -463,42 +492,76 @@
     out[QUARTER] = jnp.where(row == 0, bias_four(ins, QUARTER), 0.0)
 
 
-def place_body(f0, f1, f2, f3, mine, theirs, whole):
+def place_body(*refs):
+    ins, (mine, theirs, whole) = refs[:4], refs[4:]
     x, _, _, core = position()
-    for d, ref in enumerate((f0, f1, f2, f3)):
+    for d, ref in enumerate(ins):
         whole[pl.ds(QUARTER * turn(x, d, core), QUARTER)] = ref[:QUARTER]
     mine[:18] = whole[pl.ds(18 * core, 18)]
     theirs[:18] = whole[pl.ds(18 * (1 - core), 18)]
-    mine[18] = f0[QUARTER]
-    theirs[18] = f0[QUARTER]
-
-
-def reduce_gradient(got, core):
+    bias = four(ins, QUARTER)
+    mine[18] = bias
+    theirs[18] = bias
+
+
+def finish_body(mine, theirs, grad, bias):
+    core = position()[3]
+    for c in range(2):
+        part = jnp.where(core == c, mine[...], theirs[...])
+        grad[:, HALF * c : HALF * c + HALF] = part[:18].reshape(288, HALF)
+        bias[:, HALF * c : HALF * c + HALF] = part[18, 0:1]
+
+
+def reduce_xy(parts, mark, around):
+    ahead, here, behind, far_low, far_high, bias = parts
+    low, high = fetch(far_low, dx=3), fetch(far_high, dx=1)
+    ahead, behind = call(
+        pass_on_body,
+        (arr((16, QUARTER, CHUNK, HALF), BF),) * 2,
+        (ahead, behind, low, high),
+        flops=COST_SUM,
+        vmem=16,
+        after=(mark,),
+    )
     send = call(
         sum_x_body,
         (arr((4 * QUARTER + 1, CHUNK, HALF), BF),) * 4,
+        (here, fetch(ahead, dx=3), fetch(behind, dx=1), bias),
+        flops=COST_SUM,
+        vmem=16,
+    )
+    got = [send[0]] + [fetch(send[4 - d], dy=d) for d in range(1, 4)]
+    return call(
+        sum_y_body,
+        (arr((QUARTER + 1, CHUNK, HALF), BF),) * 4,
         got,
         flops=COST_SUM,
-        vmem=16,
-    )
-    got = [send[0]] + [fetch(send[4 - d], dy=d) for d in range(1, 4)]
-    send = call(sum_y_body, (arr((QUARTER + 1, CHUNK, HALF), BF),) * 4, got, flops=COST_SUM)
+        after=around,
+    )
+
+
+def reduce_z(send):
     got = [send[0]] + [fetch(send[4 - d], dz=2 * d) for d in range(1, 4)]
     part = call(sum_z_body, (arr((QUARTER + 1, CHUNK, HALF), F32),), got, flops=COST_SUM)[0]
-    full = (part + pair_low(part)) * (1.0 / IMAGES)
-    rows = full[:QUARTER]
-    every = [full] + [fetch(rows, dx=d) for d in range(1, 4)]
+    return (part + pair_low(part)) * (1.0 / IMAGES)
+
+
+def spread_x(full, last):
+    every = [full] + [fetch(full, dx=d) for d in range(1, 4)]
     mine, theirs = call(
         place_body,
         (arr((19, CHUNK, HALF), F32),) * 2,
         every,
+        flops=COST_PLACE,
         scratch=(pltpu.VMEM((PER_CHIP, CHUNK, HALF), F32),),
     )
-    got = fetch(theirs, swap=1)
-    both = jnp.where(
-        core == 0, jnp.concatenate([mine, got], axis=-1), jnp.concatenate([got, mine], axis=-1)
-    )
-    return both[:18].reshape(288, COUT), both[18, 0]
+    grad, bias = call(
+        finish_body,
+        (arr((288, COUT), F32), arr((1, COUT), F32)),
+        (mine, fetch(theirs, swap=1)),
+        after=(last,),
+    )
+    return grad, bias.reshape(COUT)
 
 
 def local(images, kernel, gn_gain, gn_bias, conv_bias, cotangent):
@@ -507,24 +570,26 @@
     left, right = cot[:, :HALF], cot[:, HALF:]
     cot_own = jnp.where(core == 0, left, right)
     cot_got = fetch(jnp.where(core == 0, right, left), swap=1)
-    act, planes, stat = norm_forward(images, gn_gain, gn_bias)
+    block = chip_block(kernel, core)
+    act, planes, stat = norm_forward(images, gn_gain, gn_bias, (block,))
     act_got = fetch(act, swap=1)
-    send = wgrad(act, act_got, cot_own, cot_got)
-    got = [send[0]] + [fetch(send[4 - d], dx=d) for d in range(1, 4)]
-    parts = gather_kernel(kernel, core, send[0])
-    kernel_grad, bias_grad = reduce_gradient(got, core)
+    grads = wgrad(act, act_got, cot_own, cot_got)
+    mark, level = gather_z(block)
+    around = fetch(level, dy=1), fetch(level, dy=3)
+    send = reduce_xy(grads, mark, around)
+    parts = gather_y(level, *around, (send[0],))
     cbias = jnp.where(core == 0, conv_bias[:HALF], conv_bias[HALF:]).reshape(1, HALF)
+    full = reduce_z(send)
     out_own, out_other, dact_own, dact_other = conv(
-        parts, act, act_got, cot_own, cot_got, cbias
+        parts, act, act_got, cot_own, cot_got, cbias, (full,)
     )
     dact_got = fetch(dact_other, swap=1)
     out_got = fetch(out_other, swap=1)
-    outputs = jnp.where(
-        core == 0,
-        jnp.concatenate([out_own, out_got], axis=-1),
-        jnp.concatenate([out_got, out_own], axis=-1),
-    ).reshape(cotangent.shape)
-    input_grad = norm_backward(planes, dact_own, dact_got, gn_gain, gn_bias, stat)
+    input_grad, outputs, mark = norm_backward(
+        planes, dact_own, dact_got, gn_gain, gn_bias, stat, out_own, out_got
+    )
+    outputs = outputs.reshape(cotangent.shape)
+    kernel_grad, bias_grad = spread_x(full, mark)
     return outputs, input_grad, kernel_grad, bias_grad
 
 

time: 144 us -> 125 us (0.87)
  waiting for transfers between devices: 72.8 us -> 57.9 us
  starting transfers between devices: 46.8 us -> 44.6 us
  local copies, waits for them, and re-layouts: 4.05 us -> 2.2 us
    ppermute x24 -> x26, waiting for transfers between devices: 72.8 us -> 54.8 us  [fetch(): return lax.ppermute(value, AXES, pairs(dx, dy, dz, swap))]
    ppermute x24 -> x26, starting transfers between devices: 46.7 us -> 43.1 us  [fetch(): return lax.ppermute(value, AXES, pairs(dx, dy, dz, swap))]
    ppermute x1, waiting for transfers between devices: 0.01 us -> 3.07 us  [pair_low(): return lax.ppermute(value, AXES, sorted(out))]
    slice x3 -> x0, local copies, waits for them, and re-layouts: 1.44 us -> none  [the longest x2 1.43 us: reduce_gradient(): return (both[:18].reshape(288, COUT), both[18, 0])]
    pallas_call x10 -> x14, Pallas kernels: 17.4 us -> 18.1 us  [call(): pl.pallas_call(body, out_shape=outs, scratch_shapes=list(scratch), compil...]
  transfers between devices with their start and end apart: 25 -> 27, of which waited for: 17 -> 12; matrix products, arithmetic and copies ran while one was open for 2% -> 0% of each run, Pallas kernels for 6% -> 10%
where the time goes in v4:
time: 125 us
  waiting for transfers between devices  57.9 us (46%)
  starting transfers between devices  44.6 us (36%)
  Pallas kernels  18.1 us (14%)
  local copies, waits for them, and re-layouts  2.2 us (2%)
    ppermute x26, waiting for transfers between devices, fetch(): return lax.ppermute(value, AXES, pairs(dx, dy, dz, swap))  54.8 us
    ppermute x26, starting transfers between devices, fetch(): return lax.ppermute(value, AXES, pairs(dx, dy, dz, swap))  43.1 us
    pallas_call x14, Pallas kernels, call(): pl.pallas_call(body, out_shape=outs, scratch_shapes=list(scratch), compil...  18.1 us
    ppermute x1, waiting for transfers between devices, pair_low(): return lax.ppermute(value, AXES, sorted(out))  3.07 us
  transfers between devices with their start and end apart: 27, of which 12 were waited for; matrix products, arithmetic and copies ran while one was open for 0% of the time, Pallas kernels for 10%

profile of v4, /device:TPU:1, one launch (start us, length us, event | category | flops | bytes accessed | tf_op | source)
XLA Modules:
  0.0 124.6 jit_solution(16292254752611074668)
XLA Ops:
  1.7 3.3 %collective-permute-start = (bf16[18,16,256]{2,1,0:T(8,128)(2,1)S(1)}, bf16[18,16,256]{2,1,0:T(8,128)(2,1)S(1)}, u32[]{:S(2)}, u32[]{:S(2)}) collective-permute-start(bf16[18,16,256]{2,1,0:T(8,128)(2,1)S(1)} %slice_select_fusion), channel_id=1, source_target_pairs={{0,1},{1,0},{2,3},{3,2},{4,5},{5,4},{6,7},{7,6},{8,9},{9,8},{10,11... | collective-permute-start | bytes 442376 | tf_op jit(solution)/shard_map/from_x0_y0_z0_core1/ppermute | solution.py:55
  8.2 4.2 %shard_map.94 = (bf16[4,128,1024]{2,1,0:T(8,128)(2,1)S(1)}, bf16[4,128,1024]{2,1,0:T(8,128)(2,1)S(1)}, f32[2,8,1024]{2,1,0:T(8,128)S(1)}) custom-call(bf16[2,16,16,1024]{3,2,1,0:T(8,128)(2,1)S(1)} %copy-done.3, f32[1,1024]{1,0:T(1,128)S(1)} %bitcast.9, f32[1,1024]{1,0:T(1,128)S(1)} %bitcast.11, bf16[36,16,256]{2,1,0:T(8,128)(2,1)S(1)} %shard_map.93.refs_3_.a0), custom_call_target="tpu_custom_call" | custom-call | flops 10000000000 | bytes 3219456 | tf_op jit(solution)/shard_map/pallas_call | solution.py:90
  14.4 5.1 %collective-permute-start.1 = (bf16[36,16,256]{2,1,0:T(8,128)(2,1)S(1)}, bf16[36,16,256]{2,1,0:T(8,128)(2,1)S(1)}, u32[]{:S(2)}, u32[]{:S(2)}) collective-permute-start(bf16[36,16,256]{2,1,0:T(8,128)(2,1)S(1)} %shard_map.93.refs_3_.a0), channel_id=1, source_target_pairs={{0,16},{1,17},{2,18},{3,19},{4,20},{5,21},{6,22},{7,23},{8,24},{9,... | collective-permute-start | bytes 884744 | tf_op jit(solution)/shard_map/from_x0_y0_z4_core0/ppermute | solution.py:55
  19.5 2.4 %collective-permute-start.3 = (bf16[36,16,256]{2,1,0:T(8,128)(2,1)S(1)}, bf16[36,16,256]{2,1,0:T(8,128)(2,1)S(1)}, u32[]{:S(2)}, u32[]{:S(2)}) collective-permute-start(bf16[36,16,256]{2,1,0:T(8,128)(2,1)S(1)} %shard_map.93.refs_3_.a0), channel_id=1, source_target_pairs={{0,8},{1,25},{2,10},{3,27},{4,12},{5,29},{6,14},{7,31},{8,16},{9,1... | collective-permute-start | bytes 884744 | tf_op jit(solution)/shard_map/from_x0_y0_z6_core0/ppermute | solution.py:55
  21.9 2.7 %shard_map.96 = (bf16[16,9,16,256]{3,2,1,0:T(8,128)(2,1)S(1)}, bf16[16,9,16,256]{3,2,1,0:T(8,128)(2,1)S(1)}, bf16[16,9,16,256]{3,2,1,0:T(8,128)(2,1)S(1)}, bf16[...) custom-call(bf16[4,128,1024]{2,1,0:T(8,128)(2,1)S(1)} %get-tuple-element.37.act_own.refs_5_, ...), custom_call_target="tpu_custom_call" | custom-call | flops 20000000000 | bytes 6955008 | tf_op jit(solution)/shard_map/pallas_call | solution.py:90
  24.6 2.5 %collective-permute-start.8 = (bf16[8,9,16,256]{3,2,1,0:T(8,128)(2,1)S(1)}, bf16[8,9,16,256]{3,2,1,0:T(8,128)(2,1)S(1)}, u32[]{:S(2)}, u32[]{:S(2)}) collective-permute-start(bf16[8,9,16,256]{3,2,1,0:T(8,128)(2,1)S(1)} %get-tuple-element.41), channel_id=1, source_target_pairs={{0,32},{1,97},{2,34},{3,99},{4,36},{5,101},{6,38},{7,103},{8,40},{... | collective-permute-start | bytes 1769480 | tf_op jit(solution)/shard_map/from_x3_y0_z0_core0/ppermute | solution.py:55
  27.2 12.2 %collective-permute-done.8.refs_2_ = bf16[8,9,16,256]{3,2,1,0:T(8,128)(2,1)S(1)} collective-permute-done((bf16[8,9,16,256]{3,2,1,0:T(8,128)(2,1)S(1)}, bf16[8,9,16,256]{3,2,1,0:T(8,128)(2,1)S(1)}, u32[]{:S(2)}, u32[]{:S(2)}) %collective-permute-start.8) | collective-permute-done | bytes 589856 | tf_op jit(solution)/shard_map/from_x3_y0_z0_core0/ppermute | solution.py:55
  39.4 2.3 %collective-permute-done.9.refs_3_ = bf16[8,9,16,256]{3,2,1,0:T(8,128)(2,1)S(1)} collective-permute-done((bf16[8,9,16,256]{3,2,1,0:T(8,128)(2,1)S(1)}, bf16[8,9,16,256]{3,2,1,0:T(8,128)(2,1)S(1)}, u32[]{:S(2)}, u32[]{:S(2)}) %collective-permute-start.9) | collective-permute-done | bytes 589856 | tf_op jit(solution)/shard_map/from_x1_y0_z0_core0/ppermute | solution.py:55
  43.7 1.8 %collective-permute-start.4 = (bf16[4,36,16,256]{3,2,1,0:T(8,128)(2,1)S(1)}, bf16[4,36,16,256]{3,2,1,0:T(8,128)(2,1)S(1)}, u32[]{:S(2)}, u32[]{:S(2)}) collective-permute-start(bf16[4,36,16,256]{3,2,1,0:T(8,128)(2,1)S(1)} %shard_map.95.refs_0_), channel_id=1, source_target_pairs={{0,6},{1,3},{2,0},{3,5},{4,2},{5,7},{6,4},{7,1},{8,14},{9,11},{10,... | collective-permute-start | bytes 3538952 | tf_op jit(solution)/shard_map/from_x0_y1_z0_core0/ppermute | solution.py:55
  45.5 1.7 %collective-permute-start.5 = (bf16[4,36,16,256]{3,2,1,0:T(8,128)(2,1)S(1)}, bf16[4,36,16,256]{3,2,1,0:T(8,128)(2,1)S(1)}, u32[]{:S(2)}, u32[]{:S(2)}) collective-permute-start(bf16[4,36,16,256]{3,2,1,0:T(8,128)(2,1)S(1)} %shard_map.95.refs_0_), channel_id=1, source_target_pairs={{0,2},{1,7},{2,4},{3,1},{4,6},{5,3},{6,0},{7,5},{8,10},{9,15},{10,... | collective-permute-start | bytes 3538952 | tf_op jit(solution)/shard_map/from_x0_y3_z0_core0/ppermute | solution.py:55
  47.2 22.3 %collective-permute-done.10.left = bf16[16,9,16,256]{3,2,1,0:T(8,128)(2,1)S(1)} collective-permute-done((bf16[16,9,16,256]{3,2,1,0:T(8,128)(2,1)S(1)}, bf16[16,9,16,256]{3,2,1,0:T(8,128)(2,1)S(1)}, u32[]{:S(2)}, u32[]{:S(2)}) %collective-permute-start.10) | collective-permute-done | bytes 1179680 | tf_op jit(solution)/shard_map/from_x3_y0_z0_core0/ppermute | solution.py:55
  69.5 1.8 %collective-permute-done.11.right = bf16[16,9,16,256]{3,2,1,0:T(8,128)(2,1)S(1)} collective-permute-done((bf16[16,9,16,256]{3,2,1,0:T(8,128)(2,1)S(1)}, bf16[16,9,16,256]{3,2,1,0:T(8,128)(2,1)S(1)}, u32[]{:S(2)}, u32[]{:S(2)}) %collective-permute-start.11) | collective-permute-done | bytes 1179680 | tf_op jit(solution)/shard_map/from_x1_y0_z0_core0/ppermute | solution.py:55
  72.8 2.9 %collective-permute-start.13 = (bf16[37,16,256]{2,1,0:T(8,128)(2,1)S(1)}, bf16[37,16,256]{2,1,0:T(8,128)(2,1)S(1)}, u32[]{:S(2)}, u32[]{:S(2)}) collective-permute-start(bf16[37,16,256]{2,1,0:T(8,128)(2,1)S(1)} %get-tuple-element.48), channel_id=1, source_target_pairs={{0,4},{1,5},{2,6},{3,7},{4,0},{5,1},{6,2},{7,3},{8,12},{9,13},{10,... | collective-permute-start | bytes 909320 | tf_op jit(solution)/shard_map/from_x0_y2_z0_core0/ppermute | solution.py:55
  76.5 2.8 %collective-permute-done.12.refs_1_ = bf16[37,16,256]{2,1,0:T(8,128)(2,1)S(1)} collective-permute-done((bf16[37,16,256]{2,1,0:T(8,128)(2,1)S(1)}, bf16[37,16,256]{2,1,0:T(8,128)(2,1)S(1)}, u32[]{:S(2)}, u32[]{:S(2)}) %collective-permute-start.12) | collective-permute-done | bytes 303136 | tf_op jit(solution)/shard_map/from_x0_y1_z0_core0/ppermute | solution.py:55
  79.3 8.6 %collective-permute-done.13.refs_2_ = bf16[37,16,256]{2,1,0:T(8,128)(2,1)S(1)} collective-permute-done((bf16[37,16,256]{2,1,0:T(8,128)(2,1)S(1)}, bf16[37,16,256]{2,1,0:T(8,128)(2,1)S(1)}, u32[]{:S(2)}, u32[]{:S(2)}) %collective-permute-start.13) | collective-permute-done | bytes 303136 | tf_op jit(solution)/shard_map/from_x0_y2_z0_core0/ppermute | solution.py:55
  88.0 2.4 %collective-permute-start.17 = (bf16[10,16,256]{2,1,0:T(8,128)(2,1)S(1)}, bf16[10,16,256]{2,1,0:T(8,128)(2,1)S(1)}, u32[]{:S(2)}, u32[]{:S(2)}) collective-permute-start(bf16[10,16,256]{2,1,0:T(8,128)(2,1)S(1)} %get-tuple-element.53), channel_id=1, source_target_pairs={{0,24},{1,9},{2,26},{3,11},{4,28},{5,13},{6,30},{7,15},{8,0},{9,17... | collective-permute-start | bytes 245768 | tf_op jit(solution)/shard_map/from_x0_y0_z2_core0/ppermute | solution.py:55
  91.6 2.4 %collective-permute-start.19 = (bf16[10,16,256]{2,1,0:T(8,128)(2,1)S(1)}, bf16[10,16,256]{2,1,0:T(8,128)(2,1)S(1)}, u32[]{:S(2)}, u32[]{:S(2)}) collective-permute-start(bf16[10,16,256]{2,1,0:T(8,128)(2,1)S(1)} %get-tuple-element.55), channel_id=1, source_target_pairs={{0,8},{1,25},{2,10},{3,27},{4,12},{5,29},{6,14},{7,31},{8,16},{9,1... | collective-permute-start | bytes 245768 | tf_op jit(solution)/shard_map/from_x0_y0_z6_core0/ppermute | solution.py:55
  94.9 2.5 %collective-permute-start.16 = (bf16[2,36,16,256]{3,2,1,0:T(8,128)(2,1)S(1)}, bf16[2,36,16,256]{3,2,1,0:T(8,128)(2,1)S(1)}, u32[]{:S(2)}, u32[]{:S(2)}) collective-permute-start(bf16[2,36,16,256]{3,2,1,0:T(8,128)(2,1)S(1)} %get-tuple-element.52), channel_id=1, source_target_pairs={{0,2},{1,7},{2,4},{3,1},{4,6},{5,3},{6,0},{7,5},{8,10},{9,15},{10,... | collective-permute-start | bytes 1769480 | tf_op jit(solution)/shard_map/from_x0_y3_z0_core0/ppermute | solution.py:55
  100.7 3.1 %collective-permute-done.20 = f32[10,16,256]{2,1,0:T(8,128)S(1)} collective-permute-done((f32[10,16,256]{2,1,0:T(8,128)S(1)}, f32[10,16,256]{2,1,0:T(8,128)S(1)}, u32[]{:S(2)}, u32[]{:S(2)}) %collective-permute-start.20) | collective-permute-done | bytes 163872 | tf_op jit(solution)/shard_map/from_z_low/ppermute | solution.py:66
  105.2 1.8 %collective-permute-start.24 = (f32[10,16,256]{2,1,0:T(8,128)S(1)}, f32[10,16,256]{2,1,0:T(8,128)S(1)}, u32[]{:S(2)}, u32[]{:S(2)}) collective-permute-start(f32[10,16,256]{2,1,0:T(8,128)S(1)} %add_multiply_fusion.refs_10_.refs_0_), channel_id=1, source_target_pairs={{0,64},{1,65},{2,66},{3,67},{4,68},{5,69},{6,70},{7,71},{8,72},{9,... | collective-permute-start | bytes 491528 | tf_op jit(solution)/shard_map/from_x2_y0_z0_core0/ppermute | solution.py:55
  107.0 1.8 %collective-permute-start.25 = (f32[10,16,256]{2,1,0:T(8,128)S(1)}, f32[10,16,256]{2,1,0:T(8,128)S(1)}, u32[]{:S(2)}, u32[]{:S(2)}) collective-permute-start(f32[10,16,256]{2,1,0:T(8,128)S(1)} %add_multiply_fusion.refs_10_.refs_0_), channel_id=1, source_target_pairs={{0,32},{1,97},{2,34},{3,99},{4,36},{5,101},{6,38},{7,103},{8,40},{... | collective-permute-start | bytes 491528 | tf_op jit(solution)/shard_map/from_x3_y0_z0_core0/ppermute | solution.py:55
  109.5 4.3 %shard_map.103 = (bf16[128,256]{1,0:T(8,128)(2,1)S(1)}, bf16[128,256]{1,0:T(8,128)(2,1)S(1)}, f32[4,128,1024]{2,1,0:T(8,128)S(1)}, bf16[4,128,1024]{2,1,0:T(8,128)(2,1)S(1)}) custom-call(bf16[4,36,16,256]{3,2,1,0:T(8,128)(2,1)S(1)} %shard_map.95.refs_0_, bf16[4,36,16,256]{3,2,1,0:T(8,128)(2,1)S(1)} %collective-permute-done.4.refs_4_.refs_0_.refs_1_, ...), custom_call_target="tpu_custom_call" | custom-call | flops 10000000000 | tf_op jit(solution)/shard_map/pallas_call | solution.py:90
  113.8 2.3 %collective-permute-start.21 = (bf16[4,128,1024]{2,1,0:T(8,128)(2,1)S(1)}, bf16[4,128,1024]{2,1,0:T(8,128)(2,1)S(1)}, u32[]{:S(2)}, u32[]{:S(2)}) collective-permute-start(bf16[4,128,1024]{2,1,0:T(8,128)(2,1)S(1)} %get-tuple-element.57), channel_id=1, source_target_pairs={{0,1},{1,0},{2,3},{3,2},{4,5},{5,4},{6,7},{7,6},{8,9},{9,8},{10,11... | collective-permute-start | bytes 3145736 | tf_op jit(solution)/shard_map/from_x0_y0_z0_core1/ppermute | solution.py:55
  119.0 4.7 %shard_map.104 = (bf16[2,16,16,1024]{3,2,1,0:T(8,128)(2,1)}, bf16[128,512]{1,0:T(8,128)(2,1)}, f32[8,128]{1,0:T(8,128)S(1)}) custom-call(bf16[4,128,1024]{2,1,0:T(8,128)(2,1)S(1)} %get-tuple-element.36.xp_ref, f32[4,128,1024]{2,1,0:T(8,128)S(1)} %get-tuple-element.56.own_ref, bf16[4,128,1024]{2,1,0:T(8,128)(2,1)S(1)} %collective-permute-done.21.got_ref, ...), custom_call_target="tpu_custom_call" | custom-call | flops 1000000000 | tf_op jit(solution)/shard_map/pallas_call | solution.py:90
  (60 shorter events, 21.9 us)
Async XLA Ops:
  12.5 9.5 %collective-permute-start.6 = (bf16[4,128,1024]{2,1,0:T(8,128)(2,1)S(1)}, bf16[4,128,1024]{2,1,0:T(8,128)(2,1)S(1)}, u32[]{:S(2)}, u32[]{:S(2)}) collective-permute-start(bf16[4,128,1024]{2,1,0:T(8,128)(2,1)S(1)} %get-tuple-element.37.act_own.refs_5_), channel_id=1, source_target_pairs={{0,1},{1,0},{2,3},{3,2},{4,5},{5,4},{6,7},{7,6},{8,9},{9,8},{10,11... | collective-permute-start | bytes 3145736 | tf_op jit(solution)/shard_map/from_x0_y0_z0_core1/ppermute | solution.py:55
  12.9 9.0 %collective-permute-start.7 = (bf16[128,256]{1,0:T(8,128)(2,1)S(1)}, bf16[128,256]{1,0:T(8,128)(2,1)S(1)}, u32[]{:S(2)}, u32[]{:S(2)}) collective-permute-start(bf16[128,256]{1,0:T(8,128)(2,1)S(1)} %get-tuple-element.68), channel_id=1, source_target_pairs={{0,1},{1,0},{2,3},{3,2},{4,5},{5,4},{6,7},{7,6},{8,9},{9,8},{10,11... | collective-permute-start | bytes 196616 | tf_op jit(solution)/shard_map/from_x0_y0_z0_core1/ppermute | solution.py:55
  13.2 14.0 %collective-permute-start.2 = (bf16[36,16,256]{2,1,0:T(8,128)(2,1)S(1)}, bf16[36,16,256]{2,1,0:T(8,128)(2,1)S(1)}, u32[]{:S(2)}, u32[]{:S(2)}) collective-permute-start(bf16[36,16,256]{2,1,0:T(8,128)(2,1)S(1)} %shard_map.93.refs_3_.a0), channel_id=1, source_target_pairs={{0,24},{1,9},{2,26},{3,11},{4,28},{5,13},{6,30},{7,15},{8,0},{9,17... | collective-permute-start | bytes 884744 | tf_op jit(solution)/shard_map/from_x0_y0_z2_core0/ppermute | solution.py:55
  14.4 29.2 %collective-permute-start.1 = (bf16[36,16,256]{2,1,0:T(8,128)(2,1)S(1)}, bf16[36,16,256]{2,1,0:T(8,128)(2,1)S(1)}, u32[]{:S(2)}, u32[]{:S(2)}) collective-permute-start(bf16[36,16,256]{2,1,0:T(8,128)(2,1)S(1)} %shard_map.93.refs_3_.a0), channel_id=1, source_target_pairs={{0,16},{1,17},{2,18},{3,19},{4,20},{5,21},{6,22},{7,23},{8,24},{9,... | collective-permute-start | bytes 884744 | tf_op jit(solution)/shard_map/from_x0_y0_z4_core0/ppermute | solution.py:55
  19.5 24.1 %collective-permute-start.3 = (bf16[36,16,256]{2,1,0:T(8,128)(2,1)S(1)}, bf16[36,16,256]{2,1,0:T(8,128)(2,1)S(1)}, u32[]{:S(2)}, u32[]{:S(2)}) collective-permute-start(bf16[36,16,256]{2,1,0:T(8,128)(2,1)S(1)} %shard_map.93.refs_3_.a0), channel_id=1, source_target_pairs={{0,8},{1,25},{2,10},{3,27},{4,12},{5,29},{6,14},{7,31},{8,16},{9,1... | collective-permute-start | bytes 884744 | tf_op jit(solution)/shard_map/from_x0_y0_z6_core0/ppermute | solution.py:55
  24.6 14.8 %collective-permute-start.8 = (bf16[8,9,16,256]{3,2,1,0:T(8,128)(2,1)S(1)}, bf16[8,9,16,256]{3,2,1,0:T(8,128)(2,1)S(1)}, u32[]{:S(2)}, u32[]{:S(2)}) collective-permute-start(bf16[8,9,16,256]{3,2,1,0:T(8,128)(2,1)S(1)} %get-tuple-element.41), channel_id=1, source_target_pairs={{0,32},{1,97},{2,34},{3,99},{4,36},{5,101},{6,38},{7,103},{8,40},{... | collective-permute-start | bytes 1769480 | tf_op jit(solution)/shard_map/from_x3_y0_z0_core0/ppermute | solution.py:55
  27.2 14.5 %collective-permute-start.9 = (bf16[8,9,16,256]{3,2,1,0:T(8,128)(2,1)S(1)}, bf16[8,9,16,256]{3,2,1,0:T(8,128)(2,1)S(1)}, u32[]{:S(2)}, u32[]{:S(2)}) collective-permute-start(bf16[8,9,16,256]{3,2,1,0:T(8,128)(2,1)S(1)} %get-tuple-element.42), channel_id=1, source_target_pairs={{0,96},{1,33},{2,98},{3,35},{4,100},{5,37},{6,102},{7,39},{8,104},... | collective-permute-start | bytes 1769480 | tf_op jit(solution)/shard_map/from_x1_y0_z0_core0/ppermute | solution.py:55
  42.1 27.4 %collective-permute-start.10 = (bf16[16,9,16,256]{3,2,1,0:T(8,128)(2,1)S(1)}, bf16[16,9,16,256]{3,2,1,0:T(8,128)(2,1)S(1)}, u32[]{:S(2)}, u32[]{:S(2)}) collective-permute-start(bf16[16,9,16,256]{3,2,1,0:T(8,128)(2,1)S(1)} %get-tuple-element.43), channel_id=1, source_target_pairs={{0,32},{1,97},{2,34},{3,99},{4,36},{5,101},{6,38},{7,103},{8,40},{... | collective-permute-start | bytes 3538952 | tf_op jit(solution)/shard_map/from_x3_y0_z0_core0/ppermute | solution.py:55
  43.4 27.8 %collective-permute-start.11 = (bf16[16,9,16,256]{3,2,1,0:T(8,128)(2,1)S(1)}, bf16[16,9,16,256]{3,2,1,0:T(8,128)(2,1)S(1)}, u32[]{:S(2)}, u32[]{:S(2)}) collective-permute-start(bf16[16,9,16,256]{3,2,1,0:T(8,128)(2,1)S(1)} %get-tuple-element.44), channel_id=1, source_target_pairs={{0,96},{1,33},{2,98},{3,35},{4,100},{5,37},{6,102},{7,39},{8,104},... | collective-permute-start | bytes 3538952 | tf_op jit(solution)/shard_map/from_x1_y0_z0_core0/ppermute | solution.py:55
  43.7 32.8 %collective-permute-start.4 = (bf16[4,36,16,256]{3,2,1,0:T(8,128)(2,1)S(1)}, bf16[4,36,16,256]{3,2,1,0:T(8,128)(2,1)S(1)}, u32[]{:S(2)}, u32[]{:S(2)}) collective-permute-start(bf16[4,36,16,256]{3,2,1,0:T(8,128)(2,1)S(1)} %shard_map.95.refs_0_), channel_id=1, source_target_pairs={{0,6},{1,3},{2,0},{3,5},{4,2},{5,7},{6,4},{7,1},{8,14},{9,11},{10,... | collective-permute-start | bytes 3538952 | tf_op jit(solution)/shard_map/from_x0_y1_z0_core0/ppermute | solution.py:55
  45.5 31.0 %collective-permute-start.5 = (bf16[4,36,16,256]{3,2,1,0:T(8,128)(2,1)S(1)}, bf16[4,36,16,256]{3,2,1,0:T(8,128)(2,1)S(1)}, u32[]{:S(2)}, u32[]{:S(2)}) collective-permute-start(bf16[4,36,16,256]{3,2,1,0:T(8,128)(2,1)S(1)} %shard_map.95.refs_0_), channel_id=1, source_target_pairs={{0,2},{1,7},{2,4},{3,1},{4,6},{5,3},{6,0},{7,5},{8,10},{9,15},{10,... | collective-permute-start | bytes 3538952 | tf_op jit(solution)/shard_map/from_x0_y3_z0_core0/ppermute | solution.py:55
  71.7 7.5 %collective-permute-start.12 = (bf16[37,16,256]{2,1,0:T(8,128)(2,1)S(1)}, bf16[37,16,256]{2,1,0:T(8,128)(2,1)S(1)}, u32[]{:S(2)}, u32[]{:S(2)}) collective-permute-start(bf16[37,16,256]{2,1,0:T(8,128)(2,1)S(1)} %get-tuple-element.47), channel_id=1, source_target_pairs={{0,6},{1,3},{2,0},{3,5},{4,2},{5,7},{6,4},{7,1},{8,14},{9,11},{10,... | collective-permute-start | bytes 909320 | tf_op jit(solution)/shard_map/from_x0_y1_z0_core0/ppermute | solution.py:55
  72.8 15.0 %collective-permute-start.13 = (bf16[37,16,256]{2,1,0:T(8,128)(2,1)S(1)}, bf16[37,16,256]{2,1,0:T(8,128)(2,1)S(1)}, u32[]{:S(2)}, u32[]{:S(2)}) collective-permute-start(bf16[37,16,256]{2,1,0:T(8,128)(2,1)S(1)} %get-tuple-element.48), channel_id=1, source_target_pairs={{0,4},{1,5},{2,6},{3,7},{4,0},{5,1},{6,2},{7,3},{8,12},{9,13},{10,... | collective-permute-start | bytes 909320 | tf_op jit(solution)/shard_map/from_x0_y2_z0_core0/ppermute | solution.py:55
  75.7 12.1 %collective-permute-start.14 = (bf16[37,16,256]{2,1,0:T(8,128)(2,1)S(1)}, bf16[37,16,256]{2,1,0:T(8,128)(2,1)S(1)}, u32[]{:S(2)}, u32[]{:S(2)}) collective-permute-start(bf16[37,16,256]{2,1,0:T(8,128)(2,1)S(1)} %get-tuple-element.49), channel_id=1, source_target_pairs={{0,2},{1,7},{2,4},{3,1},{4,6},{5,3},{6,0},{7,5},{8,10},{9,15},{10,... | collective-permute-start | bytes 909320 | tf_op jit(solution)/shard_map/from_x0_y3_z0_core0/ppermute | solution.py:55
  88.0 9.3 %collective-permute-start.17 = (bf16[10,16,256]{2,1,0:T(8,128)(2,1)S(1)}, bf16[10,16,256]{2,1,0:T(8,128)(2,1)S(1)}, u32[]{:S(2)}, u32[]{:S(2)}) collective-permute-start(bf16[10,16,256]{2,1,0:T(8,128)(2,1)S(1)} %get-tuple-element.53), channel_id=1, source_target_pairs={{0,24},{1,9},{2,26},{3,11},{4,28},{5,13},{6,30},{7,15},{8,0},{9,17... | collective-permute-start | bytes 245768 | tf_op jit(solution)/shard_map/from_x0_y0_z2_core0/ppermute | solution.py:55
  90.4 7.3 %collective-permute-start.18 = (bf16[10,16,256]{2,1,0:T(8,128)(2,1)S(1)}, bf16[10,16,256]{2,1,0:T(8,128)(2,1)S(1)}, u32[]{:S(2)}, u32[]{:S(2)}) collective-permute-start(bf16[10,16,256]{2,1,0:T(8,128)(2,1)S(1)} %get-tuple-element.54), channel_id=1, source_target_pairs={{0,16},{1,17},{2,18},{3,19},{4,20},{5,21},{6,22},{7,23},{8,24},{9,... | collective-permute-start | bytes 245768 | tf_op jit(solution)/shard_map/from_x0_y0_z4_core0/ppermute | solution.py:55
  91.6 7.6 %collective-permute-start.19 = (bf16[10,16,256]{2,1,0:T(8,128)(2,1)S(1)}, bf16[10,16,256]{2,1,0:T(8,128)(2,1)S(1)}, u32[]{:S(2)}, u32[]{:S(2)}) collective-permute-start(bf16[10,16,256]{2,1,0:T(8,128)(2,1)S(1)} %get-tuple-element.55), channel_id=1, source_target_pairs={{0,8},{1,25},{2,10},{3,27},{4,12},{5,29},{6,14},{7,31},{8,16},{9,1... | collective-permute-start | bytes 245768 | tf_op jit(solution)/shard_map/from_x0_y0_z6_core0/ppermute | solution.py:55
  94.1 14.8 %collective-permute-start.15 = (bf16[2,36,16,256]{3,2,1,0:T(8,128)(2,1)S(1)}, bf16[2,36,16,256]{3,2,1,0:T(8,128)(2,1)S(1)}, u32[]{:S(2)}, u32[]{:S(2)}) collective-permute-start(bf16[2,36,16,256]{3,2,1,0:T(8,128)(2,1)S(1)} %get-tuple-element.51), channel_id=1, source_target_pairs={{0,6},{1,3},{2,0},{3,5},{4,2},{5,7},{6,4},{7,1},{8,14},{9,11},{10,... | collective-permute-start | bytes 1769480 | tf_op jit(solution)/shard_map/from_x0_y1_z0_core0/ppermute | solution.py:55
  94.9 14.6 %collective-permute-start.16 = (bf16[2,36,16,256]{3,2,1,0:T(8,128)(2,1)S(1)}, bf16[2,36,16,256]{3,2,1,0:T(8,128)(2,1)S(1)}, u32[]{:S(2)}, u32[]{:S(2)}) collective-permute-start(bf16[2,36,16,256]{3,2,1,0:T(8,128)(2,1)S(1)} %get-tuple-element.52), channel_id=1, source_target_pairs={{0,2},{1,7},{2,4},{3,1},{4,6},{5,3},{6,0},{7,5},{8,10},{9,15},{10,... | collective-permute-start | bytes 1769480 | tf_op jit(solution)/shard_map/from_x0_y3_z0_core0/ppermute | solution.py:55
  103.8 12.3 %collective-permute-start.23 = (f32[10,16,256]{2,1,0:T(8,128)S(1)}, f32[10,16,256]{2,1,0:T(8,128)S(1)}, u32[]{:S(2)}, u32[]{:S(2)}) collective-permute-start(f32[10,16,256]{2,1,0:T(8,128)S(1)} %add_multiply_fusion.refs_10_.refs_0_), channel_id=1, source_target_pairs={{0,96},{1,33},{2,98},{3,35},{4,100},{5,37},{6,102},{7,39},{8,104},... | collective-permute-start | bytes 491528 | tf_op jit(solution)/shard_map/from_x1_y0_z0_core0/ppermute | solution.py:55
  105.2 10.9 %collective-permute-start.24 = (f32[10,16,256]{2,1,0:T(8,128)S(1)}, f32[10,16,256]{2,1,0:T(8,128)S(1)}, u32[]{:S(2)}, u32[]{:S(2)}) collective-permute-start(f32[10,16,256]{2,1,0:T(8,128)S(1)} %add_multiply_fusion.refs_10_.refs_0_), channel_id=1, source_target_pairs={{0,64},{1,65},{2,66},{3,67},{4,68},{5,69},{6,70},{7,71},{8,72},{9,... | collective-permute-start | bytes 491528 | tf_op jit(solution)/shard_map/from_x2_y0_z0_core0/ppermute | solution.py:55
  107.0 9.2 %collective-permute-start.25 = (f32[10,16,256]{2,1,0:T(8,128)S(1)}, f32[10,16,256]{2,1,0:T(8,128)S(1)}, u32[]{:S(2)}, u32[]{:S(2)}) collective-permute-start(f32[10,16,256]{2,1,0:T(8,128)S(1)} %add_multiply_fusion.refs_10_.refs_0_), channel_id=1, source_target_pairs={{0,32},{1,97},{2,34},{3,99},{4,36},{5,101},{6,38},{7,103},{8,40},{... | collective-permute-start | bytes 491528 | tf_op jit(solution)/shard_map/from_x3_y0_z0_core0/ppermute | solution.py:55
  113.8 5.2 %collective-permute-start.21 = (bf16[4,128,1024]{2,1,0:T(8,128)(2,1)S(1)}, bf16[4,128,1024]{2,1,0:T(8,128)(2,1)S(1)}, u32[]{:S(2)}, u32[]{:S(2)}) collective-permute-start(bf16[4,128,1024]{2,1,0:T(8,128)(2,1)S(1)} %get-tuple-element.57), channel_id=1, source_target_pairs={{0,1},{1,0},{2,3},{3,2},{4,5},{5,4},{6,7},{7,6},{8,9},{9,8},{10,11... | collective-permute-start | bytes 3145736 | tf_op jit(solution)/shard_map/from_x0_y0_z0_core1/ppermute | solution.py:55
  116.3 7.4 %collective-permute-start.26 = (f32[19,16,256]{2,1,0:T(8,128)S(1)}, f32[19,16,256]{2,1,0:T(8,128)S(1)}, u32[]{:S(2)}, u32[]{:S(2)}) collective-permute-start(f32[19,16,256]{2,1,0:T(8,128)S(1)} %get-tuple-element.64), channel_id=1, source_target_pairs={{0,1},{1,0},{2,3},{3,2},{4,5},{5,4},{6,7},{7,6},{8,9},{9,8},{10,11... | collective-permute-start | bytes 933896 | tf_op jit(solution)/shard_map/from_x0_y0_z0_core1/ppermute | solution.py:55
  (9 other events, 35.8 us)

commit v5 on v4

--- a/solution.py
+++ b/solution.py
@@ -120,112 +120,125 @@
     return jnp.where(row == 0, a, jnp.where(row == 1, b, 0.0))
 
 
-def norm_body(x_ref, gain_ref, bias_ref, act_ref, plane_ref, stat_ref, *bufs):
-    x = x_ref[...].astype(F32).reshape(2, 256, LANES)
-    sums = [jnp.sum(x[i], axis=0, keepdims=True) for i in range(2)]
-    mean = group_mean(stack_rows(*sums))
-    sq = [jnp.sum(jnp.square(x[i] - mean[i : i + 1]), axis=0, keepdims=True) for i in range(2)]
-    rstd = lax.rsqrt(group_mean(stack_rows(*sq)) + EPS)
-    stat_ref[0] = mean
-    stat_ref[1] = rstd
-    for h, buf in enumerate(bufs):
-        buf[...] = x[:, :, 128 * h : 128 * h + 128].reshape(512, 128)
-    gain, bias = gain_ref[...], bias_ref[...]
-    for pj in range(2):
-        part = jnp.concatenate([buf[pl.ds(pj, 256, stride=2), :] for buf in bufs], axis=-1)
-        part = part.reshape(2, 8, 2, 8, LANES)
-        for pi in range(2):
-            for i in range(2):
-                xp = part[i, :, pi].reshape(64, LANES)
-                y = (xp - mean[i : i + 1]) * rstd[i : i + 1] * gain + bias
-                rows = slice(64 * i, 64 * i + 64)
-                act_ref[2 * pi + pj, rows, :] = (y * jax.nn.sigmoid(y)).astype(BF)
-                plane_ref[2 * pi + pj, rows, :] = xp.astype(BF)
+def norm_body(x_hbm, gain_ref, bias_ref, act_ref, plane_ref, stat_ref, raw, *rest):
+    bufs, sem = rest[:2], rest[2]
+    count = CIN // LANES
+    copies = [
+        pltpu.make_async_copy(
+            x_hbm.at[:, :, :, pl.ds(LANES * n, LANES)], raw.at[n], sem.at[n]
+        )
+        for n in range(count)
+    ]
+    for copy in copies:
+        copy.start()
+    for n, copy in enumerate(copies):
+        lanes = slice(LANES * n, LANES * n + LANES)
+        copy.wait()
+        x = raw[n].astype(F32).reshape(2, 256, LANES)
+        sums = [jnp.sum(x[i], axis=0, keepdims=True) for i in range(2)]
+        mean = group_mean(stack_rows(*sums))
+        sq = [jnp.sum(jnp.square(x[i] - mean[i : i + 1]), axis=0, keepdims=True) for i in range(2)]
+        rstd = lax.rsqrt(group_mean(stack_rows(*sq)) + EPS)
+        stat_ref[0, :, lanes] = mean
+        stat_ref[1, :, lanes] = rstd
+        for h, buf in enumerate(bufs):
+            buf[n % 2] = x[:, :, 128 * h : 128 * h + 128].reshape(512, 128)
+        gain, bias = gain_ref[:, lanes], bias_ref[:, lanes]
+        for pj in range(2):
+            part = jnp.concatenate(
+                [buf[n % 2, pl.ds(pj, 256, stride=2), :] for buf in bufs], axis=-1
+            )
+            part = part.reshape(2, 8, 2, 8, LANES)
+            for pi in range(2):
+                for i in range(2):
+                    xp = part[i, :, pi].reshape(64, LANES)
+                    y = (xp - mean[i : i + 1]) * rstd[i : i + 1] * gain + bias
+                    rows = slice(64 * i, 64 * i + 64)
+                    act_ref[2 * pi + pj, rows, lanes] = (y * jax.nn.sigmoid(y)).astype(BF)
+                    plane_ref[2 * pi + pj, rows, lanes] = xp.astype(BF)
 
 
 def norm_forward(images, gain, bias, after):
+    vm = pl.BlockSpec(memory_space=pltpu.VMEM)
     plane = arr((4, 128, CIN), BF)
-    vec = pl.BlockSpec((1, LANES), lambda c: (0, c))
-    block = pl.BlockSpec((4, 128, LANES), lambda c: (0, 0, c))
     return call(
         norm_body,
         (plane, plane, arr((2, 8, CIN), F32)),
         (images, gain.reshape(1, CIN), bias.reshape(1, CIN)),
         flops=COST_NORM,
-        scratch=(pltpu.VMEM((512, 128), F32),) * (LANES // 128),
-        grid=(CIN // LANES,),
-        specs=[pl.BlockSpec((2, 16, 16, LANES), lambda c: (0, 0, 0, c)), vec, vec],
-        out_specs=(block, block, pl.BlockSpec((2, 8, LANES), lambda c: (0, 0, c))),
+        scratch=(pltpu.VMEM((CIN // LANES, 2, 16, 16, LANES), BF),)
+        + (pltpu.VMEM((2, 512, 128), F32),) * (LANES // 128)
+        + (pltpu.SemaphoreType.DMA((CIN // LANES,)),),
+        specs=[pl.BlockSpec(memory_space=pltpu.HBM), vm, vm],
+        out_specs=(vm, vm, vm),
         after=after,
     )
 
 
-def norm_back_body(
-    xp_ref, own_ref, got_ref, gain_ref, bias_ref, stat_ref, res_own, res_got, out_ref, res_ref, mark, *bufs
-):
+def norm_back_body(*refs):
+    xp_ref, own_ref, got_ref, gain_ref, bias_ref, stat_ref, res_own, res_got = refs[:8]
+    out_ref, res_ref, mark = refs[8:11]
+    bufs = refs[11:]
     core = position()[3]
     for c in range(2):
         res_ref[:, HALF * c : HALF * c + HALF] = jnp.where(core == c, res_own[...], res_got[...])
     mark[...] = jnp.zeros_like(mark)
-    gain, bias = gain_ref[...], bias_ref[...]
-    mean, rstd = stat_ref[0], stat_ref[1]
-    hats, grads, one, two = [], [], [], []
-    for i in range(2):
-        rows = slice(64 * i, 64 * i + 64)
-        m, r = mean[i : i + 1], rstd[i : i + 1]
-        h_list, g_list, s1, s2 = [], [], 0.0, 0.0
-        for p in range(4):
-            hat = (xp_ref[p, rows, :].astype(F32) - m) * r
-            y = hat * gain + bias
-            s = jax.nn.sigmoid(y)
-            d = own_ref[p, rows, :] + got_ref[p, rows, :].astype(F32)
-            g = d * (s * (1.0 + y * (1.0 - s))) * gain
-            s1 = s1 + jnp.sum(g, axis=0, keepdims=True)
-            s2 = s2 + jnp.sum(g * hat, axis=0, keepdims=True)
-            h_list.append(hat)
-            g_list.append(g)
-        hats.append(h_list)
-        grads.append(g_list)
-        one.append(s1)
-        two.append(s2)
-    mean1 = group_mean(stack_rows(*one))
-    mean2 = group_mean(stack_rows(*two))
-    for pj in range(2):
-        parts = []
+    for n in range(CIN // LANES):
+        lanes = slice(LANES * n, LANES * n + LANES)
+        gain, bias = gain_ref[:, lanes], bias_ref[:, lanes]
+        mean, rstd = stat_ref[0, :, lanes], stat_ref[1, :, lanes]
+        hats, grads, one, two = [], [], [], []
         for i in range(2):
-            both = []
-            for pi in range(2):
-                p = 2 * pi + pj
-                dx = rstd[i : i + 1] * (
-                    grads[i][p] - mean1[i : i + 1] - hats[i][p] * mean2[i : i + 1]
-                )
-                both.append(dx.reshape(8, 1, 8, LANES))
-            parts.append(jnp.concatenate(both, axis=1).reshape(128, LANES))
-        rows = jnp.concatenate(parts, axis=0)
+            rows = slice(64 * i, 64 * i + 64)
+            m, r = mean[i : i + 1], rstd[i : i + 1]
+            h_list, g_list, s1, s2 = [], [], 0.0, 0.0
+            for p in range(4):
+                hat = (xp_ref[p, rows, lanes].astype(F32) - m) * r
+                y = hat * gain + bias
+                s = jax.nn.sigmoid(y)
+                d = own_ref[p, rows, lanes] + got_ref[p, rows, lanes].astype(F32)
+                g = d * (s * (1.0 + y * (1.0 - s))) * gain
+                s1 = s1 + jnp.sum(g, axis=0, keepdims=True)
+                s2 = s2 + jnp.sum(g * hat, axis=0, keepdims=True)
+                h_list.append(hat)
+                g_list.append(g)
+            hats.append(h_list)
+            grads.append(g_list)
+            one.append(s1)
+            two.append(s2)
+        mean1 = group_mean(stack_rows(*one))
+        mean2 = group_mean(stack_rows(*two))
+        for pj in range(2):
+            parts = []
+            for i in range(2):
+                both = []
+                for pi in range(2):
+                    p = 2 * pi + pj
+                    dx = rstd[i : i + 1] * (
+                        grads[i][p] - mean1[i : i + 1] - hats[i][p] * mean2[i : i + 1]
+                    )
+                    both.append(dx.reshape(8, 1, 8, LANES))
+                parts.append(jnp.concatenate(both, axis=1).reshape(128, LANES))
+            rows = jnp.concatenate(parts, axis=0)
+            for h, buf in enumerate(bufs):
+                buf[n % 2, pl.ds(pj, 256, stride=2), :] = rows[:, 128 * h : 128 * h + 128]
         for h, buf in enumerate(bufs):
-            buf[pl.ds(pj, 256, stride=2), :] = rows[:, 128 * h : 128 * h + 128]
-    for h, buf in enumerate(bufs):
-        out_ref[:, :, :, 128 * h : 128 * h + 128] = buf[...].astype(BF).reshape(2, 16, 16, 128)
+            at = slice(LANES * n + 128 * h, LANES * n + 128 * h + 128)
+            out_ref[:, :, :, at] = buf[n % 2].astype(BF).reshape(2, 16, 16, 128)
 
 
 def norm_backward(planes, own, got, gain, bias, stat, res_own, res_got):
-    vec = pl.BlockSpec((1, LANES), lambda c: (0, c))
-    block = pl.BlockSpec((4, 128, LANES), lambda c: (0, 0, c))
+    vm = pl.BlockSpec(memory_space=pltpu.VMEM)
     return call(
         norm_back_body,
         (arr((2, 16, 16, CIN), BF), arr((128, COUT), BF), arr((8, 128), F32)),
         (planes, own, got, gain.reshape(1, CIN), bias.reshape(1, CIN), stat, res_own, res_got),
         flops=COST_BACK,
         moved=MOVED_BACK,
-        scratch=(pltpu.VMEM((512, 128), F32),) * (LANES // 128),
-        grid=(CIN // LANES,),
-        specs=[block, block, block, vec, vec, pl.BlockSpec((2, 8, LANES), lambda c: (0, 0, c))]
-        + [pl.BlockSpec((128, HALF), lambda c: (0, 0))] * 2,
-        out_specs=(
-            pl.BlockSpec((2, 16, 16, LANES), lambda c: (0, 0, 0, c)),
-            pl.BlockSpec((128, COUT), lambda c: (0, 0)),
-            pl.BlockSpec((8, 128), lambda c: (0, 0)),
-        ),
+        scratch=(pltpu.VMEM((2, 512, 128), F32),) * (LANES // 128),
+        specs=[vm] * 8,
+        out_specs=(vm,) * 3,
+        vmem=16,
     )
 
 
@@ -456,6 +469,10 @@
     return jnp.where(row == 0, high, jnp.where(row == 1, total - high, 0.0)).astype(BF)
 
 
+def own_and_sent(shape):
+    return (arr(shape, F32),) + (arr(shape, BF),) * 3
+
+
 def pass_on_body(ahead, behind, low, high, ahead_out, behind_out):
     ahead_out[:8] = (ahead[:8].astype(F32) + low[...].astype(F32)).astype(BF)
     ahead_out[8:] = ahead[8:]
@@ -471,8 +488,8 @@
         for z in range(4):
             r = 4 * z + there
             total = own[r].astype(F32) + (left[r].astype(F32) + right[r].astype(F32))
-            outs[d][QUARTER * z : QUARTER * z + QUARTER] = total.astype(BF)
-        outs[d][4 * QUARTER] = bias
+            outs[d][QUARTER * z : QUARTER * z + QUARTER] = total.astype(outs[d].dtype)
+        outs[d][4 * QUARTER] = bias.astype(outs[d].dtype)
 
 
 def sum_y_body(*refs):
@@ -481,8 +498,9 @@
     bias = bias_chunk(bias_four(ins, 4 * QUARTER))
     for d in range(4):
         there = turn(z, d, core)
-        outs[d][:QUARTER] = four(ins, pl.ds(QUARTER * there, QUARTER)).astype(BF)
-        outs[d][QUARTER] = bias
+        total = four(ins, pl.ds(QUARTER * there, QUARTER))
+        outs[d][:QUARTER] = total.astype(outs[d].dtype)
+        outs[d][QUARTER] = bias.astype(outs[d].dtype)
 
 
 def sum_z_body(*refs):
@@ -490,6 +508,11 @@
     out[:QUARTER] = four(ins, pl.ds(0, QUARTER))
     row = lax.broadcasted_iota(jnp.int32, (CHUNK, HALF), 0)
     out[QUARTER] = jnp.where(row == 0, bias_four(ins, QUARTER), 0.0)
+
+
+def round_body(part, got, out):
+    out[:QUARTER] = ((part[:QUARTER] + got[:QUARTER]) * (1.0 / IMAGES)).astype(BF)
+    out[QUARTER] = bias_chunk((part[QUARTER, 0:1] + got[QUARTER, 0:1]) * (1.0 / IMAGES))
 
 
 def place_body(*refs):
@@ -499,7 +522,7 @@
         whole[pl.ds(QUARTER * turn(x, d, core), QUARTER)] = ref[:QUARTER]
     mine[:18] = whole[pl.ds(18 * core, 18)]
     theirs[:18] = whole[pl.ds(18 * (1 - core), 18)]
-    bias = four(ins, QUARTER)
+    bias = bias_chunk(bias_four(ins, QUARTER))
     mine[18] = bias
     theirs[18] = bias
 
@@ -507,9 +530,9 @@
 def finish_body(mine, theirs, grad, bias):
     core = position()[3]
     for c in range(2):
-        part = jnp.where(core == c, mine[...], theirs[...])
+        part = jnp.where(core == c, mine[...], theirs[...]).astype(F32)
         grad[:, HALF * c : HALF * c + HALF] = part[:18].reshape(288, HALF)
-        bias[:, HALF * c : HALF * c + HALF] = part[18, 0:1]
+        bias[:, HALF * c : HALF * c + HALF] = part[18, 0:1] + part[18, 1:2]
 
 
 def reduce_xy(parts, mark, around):
@@ -525,7 +548,7 @@
     )
     send = call(
         sum_x_body,
-        (arr((4 * QUARTER + 1, CHUNK, HALF), BF),) * 4,
+        own_and_sent((4 * QUARTER + 1, CHUNK, HALF)),
         (here, fetch(ahead, dx=3), fetch(behind, dx=1), bias),
         flops=COST_SUM,
         vmem=16,
@@ -533,7 +556,7 @@
     got = [send[0]] + [fetch(send[4 - d], dy=d) for d in range(1, 4)]
     return call(
         sum_y_body,
-        (arr((QUARTER + 1, CHUNK, HALF), BF),) * 4,
+        own_and_sent((QUARTER + 1, CHUNK, HALF)),
         got,
         flops=COST_SUM,
         after=around,
@@ -543,17 +566,19 @@
 def reduce_z(send):
     got = [send[0]] + [fetch(send[4 - d], dz=2 * d) for d in range(1, 4)]
     part = call(sum_z_body, (arr((QUARTER + 1, CHUNK, HALF), F32),), got, flops=COST_SUM)[0]
-    return (part + pair_low(part)) * (1.0 / IMAGES)
+    return call(
+        round_body, (arr((QUARTER + 1, CHUNK, HALF), BF),), (part, pair_low(part))
+    )[0]
 
 
 def spread_x(full, last):
     every = [full] + [fetch(full, dx=d) for d in range(1, 4)]
     mine, theirs = call(
         place_body,
-        (arr((19, CHUNK, HALF), F32),) * 2,
+        (arr((19, CHUNK, HALF), BF),) * 2,
         every,
         flops=COST_PLACE,
-        scratch=(pltpu.VMEM((PER_CHIP, CHUNK, HALF), F32),),
+        scratch=(pltpu.VMEM((PER_CHIP, CHUNK, HALF), BF),),
     )
     grad, bias = call(
         finish_body,

time: 125 us -> 123 us (0.984)
  waiting for transfers between devices: 57.9 us -> 56.4 us
  Pallas kernels: 18.1 us -> 16.7 us
    ppermute x1, starting transfers between devices: 1.47 us -> 3.77 us  [pair_low(): return lax.ppermute(value, AXES, sorted(out))]
    ppermute x26, starting transfers between devices: 43.1 us -> 41.6 us  [fetch(): return lax.ppermute(value, AXES, pairs(dx, dy, dz, swap))]
    pallas_call x14 -> x15, Pallas kernels: 18.1 us -> 16.7 us  [call(): pl.pallas_call(body, out_shape=outs, scratch_shapes=list(scratch), compil...]
    ppermute x26, waiting for transfers between devices: 54.8 us -> 53.4 us  [fetch(): return lax.ppermute(value, AXES, pairs(dx, dy, dz, swap))]
  transfers between devices with their start and end apart: 27 -> 27, of which waited for: 12 -> 11; matrix products, arithmetic and copies ran while one was open for 0% -> 0% of each run, Pallas kernels for 10% -> 10%
where the time goes in v5:
time: 123 us
  waiting for transfers between devices  56.4 us (46%)
  starting transfers between devices  45.4 us (37%)
  Pallas kernels  16.7 us (14%)
  local copies, waits for them, and re-layouts  2.2 us (2%)
    ppermute x26, waiting for transfers between devices, fetch(): return lax.ppermute(value, AXES, pairs(dx, dy, dz, swap))  53.4 us
    ppermute x26, starting transfers between devices, fetch(): return lax.ppermute(value, AXES, pairs(dx, dy, dz, swap))  41.6 us
    pallas_call x15, Pallas kernels, call(): pl.pallas_call(body, out_shape=outs, scratch_shapes=list(scratch), compil...  16.7 us
    ppermute x1, starting transfers between devices, pair_low(): return lax.ppermute(value, AXES, sorted(out))  3.77 us
    ppermute x1, waiting for transfers between devices, pair_low(): return lax.ppermute(value, AXES, sorted(out))  3 us
  transfers between devices with their start and end apart: 27, of which 11 were waited for; matrix products, arithmetic and copies ran while one was open for 0% of the time, Pallas kernels for 10%

profile of v5, /device:TPU:1, one launch (start us, length us, event | category | flops | bytes accessed | tf_op | source)
XLA Modules:
  0.0 122.6 jit_solution(4384261094523679784)
XLA Ops:
  1.7 3.3 %collective-permute-start = (bf16[18,16,256]{2,1,0:T(8,128)(2,1)S(1)}, bf16[18,16,256]{2,1,0:T(8,128)(2,1)S(1)}, u32[]{:S(2)}, u32[]{:S(2)}) collective-permute-start(bf16[18,16,256]{2,1,0:T(8,128)(2,1)S(1)} %slice_select_fusion), channel_id=1, source_target_pairs={{0,1},{1,0},{2,3},{3,2},{4,5},{5,4},{6,7},{7,6},{8,9},{9,8},{10,11... | collective-permute-start | bytes 442376 | tf_op jit(solution)/shard_map/from_x0_y0_z0_core1/ppermute | solution.py:55
  8.2 3.9 %shard_map.94 = (bf16[4,128,1024]{2,1,0:T(8,128)(2,1)S(1)}, bf16[4,128,1024]{2,1,0:T(8,128)(2,1)S(1)}, f32[2,8,1024]{2,1,0:T(8,128)S(1)}) custom-call(bf16[2,16,16,1024]{3,2,1,0:T(8,128)(2,1)S(1)} %copy-done.3, f32[1,1024]{1,0:T(1,128)S(1)} %bitcast.9, f32[1,1024]{1,0:T(1,128)S(1)} %bitcast.11, bf16[36,16,256]{2,1,0:T(8,128)(2,1)S(1)} %shard_map.93.refs_3_.a0), custom_call_target="tpu_custom_call" | custom-call | flops 10000000000 | bytes 3219456 | tf_op jit(solution)/shard_map/pallas_call | solution.py:90
  14.1 5.1 %collective-permute-start.1 = (bf16[36,16,256]{2,1,0:T(8,128)(2,1)S(1)}, bf16[36,16,256]{2,1,0:T(8,128)(2,1)S(1)}, u32[]{:S(2)}, u32[]{:S(2)}) collective-permute-start(bf16[36,16,256]{2,1,0:T(8,128)(2,1)S(1)} %shard_map.93.refs_3_.a0), channel_id=1, source_target_pairs={{0,16},{1,17},{2,18},{3,19},{4,20},{5,21},{6,22},{7,23},{8,24},{9,... | collective-permute-start | bytes 884744 | tf_op jit(solution)/shard_map/from_x0_y0_z4_core0/ppermute | solution.py:55
  19.2 2.4 %collective-permute-start.3 = (bf16[36,16,256]{2,1,0:T(8,128)(2,1)S(1)}, bf16[36,16,256]{2,1,0:T(8,128)(2,1)S(1)}, u32[]{:S(2)}, u32[]{:S(2)}) collective-permute-start(bf16[36,16,256]{2,1,0:T(8,128)(2,1)S(1)} %shard_map.93.refs_3_.a0), channel_id=1, source_target_pairs={{0,8},{1,25},{2,10},{3,27},{4,12},{5,29},{6,14},{7,31},{8,16},{9,1... | collective-permute-start | bytes 884744 | tf_op jit(solution)/shard_map/from_x0_y0_z6_core0/ppermute | solution.py:55
  21.6 2.7 %shard_map.96 = (bf16[16,9,16,256]{3,2,1,0:T(8,128)(2,1)S(1)}, bf16[16,9,16,256]{3,2,1,0:T(8,128)(2,1)S(1)}, bf16[16,9,16,256]{3,2,1,0:T(8,128)(2,1)S(1)}, bf16[...) custom-call(bf16[4,128,1024]{2,1,0:T(8,128)(2,1)S(1)} %get-tuple-element.37.act_own.refs_5_, ...), custom_call_target="tpu_custom_call" | custom-call | flops 20000000000 | bytes 6955008 | tf_op jit(solution)/shard_map/pallas_call | solution.py:90
  24.3 2.6 %collective-permute-start.8 = (bf16[8,9,16,256]{3,2,1,0:T(8,128)(2,1)S(1)}, bf16[8,9,16,256]{3,2,1,0:T(8,128)(2,1)S(1)}, u32[]{:S(2)}, u32[]{:S(2)}) collective-permute-start(bf16[8,9,16,256]{3,2,1,0:T(8,128)(2,1)S(1)} %get-tuple-element.41), channel_id=1, source_target_pairs={{0,32},{1,97},{2,34},{3,99},{4,36},{5,101},{6,38},{7,103},{8,40},{... | collective-permute-start | bytes 1769480 | tf_op jit(solution)/shard_map/from_x3_y0_z0_core0/ppermute | solution.py:55
  26.9 12.2 %collective-permute-done.8.refs_2_ = bf16[8,9,16,256]{3,2,1,0:T(8,128)(2,1)S(1)} collective-permute-done((bf16[8,9,16,256]{3,2,1,0:T(8,128)(2,1)S(1)}, bf16[8,9,16,256]{3,2,1,0:T(8,128)(2,1)S(1)}, u32[]{:S(2)}, u32[]{:S(2)}) %collective-permute-start.8) | collective-permute-done | bytes 589856 | tf_op jit(solution)/shard_map/from_x3_y0_z0_core0/ppermute | solution.py:55
  39.1 2.3 %collective-permute-done.9.refs_3_ = bf16[8,9,16,256]{3,2,1,0:T(8,128)(2,1)S(1)} collective-permute-done((bf16[8,9,16,256]{3,2,1,0:T(8,128)(2,1)S(1)}, bf16[8,9,16,256]{3,2,1,0:T(8,128)(2,1)S(1)}, u32[]{:S(2)}, u32[]{:S(2)}) %collective-permute-start.9) | collective-permute-done | bytes 589856 | tf_op jit(solution)/shard_map/from_x1_y0_z0_core0/ppermute | solution.py:55
  43.4 2.0 %collective-permute-start.4 = (bf16[4,36,16,256]{3,2,1,0:T(8,128)(2,1)S(1)}, bf16[4,36,16,256]{3,2,1,0:T(8,128)(2,1)S(1)}, u32[]{:S(2)}, u32[]{:S(2)}) collective-permute-start(bf16[4,36,16,256]{3,2,1,0:T(8,128)(2,1)S(1)} %shard_map.95.refs_0_), channel_id=1, source_target_pairs={{0,6},{1,3},{2,0},{3,5},{4,2},{5,7},{6,4},{7,1},{8,14},{9,11},{10,... | collective-permute-start | bytes 3538952 | tf_op jit(solution)/shard_map/from_x0_y1_z0_core0/ppermute | solution.py:55
  46.9 22.3 %collective-permute-done.10.left = bf16[16,9,16,256]{3,2,1,0:T(8,128)(2,1)S(1)} collective-permute-done((bf16[16,9,16,256]{3,2,1,0:T(8,128)(2,1)S(1)}, bf16[16,9,16,256]{3,2,1,0:T(8,128)(2,1)S(1)}, u32[]{:S(2)}, u32[]{:S(2)}) %collective-permute-start.10) | collective-permute-done | bytes 1179680 | tf_op jit(solution)/shard_map/from_x3_y0_z0_core0/ppermute | solution.py:55
  69.2 1.8 %collective-permute-done.11.right = bf16[16,9,16,256]{3,2,1,0:T(8,128)(2,1)S(1)} collective-permute-done((bf16[16,9,16,256]{3,2,1,0:T(8,128)(2,1)S(1)}, bf16[16,9,16,256]{3,2,1,0:T(8,128)(2,1)S(1)}, u32[]{:S(2)}, u32[]{:S(2)}) %collective-permute-start.11) | collective-permute-done | bytes 1179680 | tf_op jit(solution)/shard_map/from_x1_y0_z0_core0/ppermute | solution.py:55
  72.5 2.9 %collective-permute-start.13 = (bf16[37,16,256]{2,1,0:T(8,128)(2,1)S(1)}, bf16[37,16,256]{2,1,0:T(8,128)(2,1)S(1)}, u32[]{:S(2)}, u32[]{:S(2)}) collective-permute-start(bf16[37,16,256]{2,1,0:T(8,128)(2,1)S(1)} %get-tuple-element.48), channel_id=1, source_target_pairs={{0,4},{1,5},{2,6},{3,7},{4,0},{5,1},{6,2},{7,3},{8,12},{9,13},{10,... | collective-permute-start | bytes 909320 | tf_op jit(solution)/shard_map/from_x0_y2_z0_core0/ppermute | solution.py:55
  76.2 2.8 %collective-permute-done.12.refs_1_ = bf16[37,16,256]{2,1,0:T(8,128)(2,1)S(1)} collective-permute-done((bf16[37,16,256]{2,1,0:T(8,128)(2,1)S(1)}, bf16[37,16,256]{2,1,0:T(8,128)(2,1)S(1)}, u32[]{:S(2)}, u32[]{:S(2)}) %collective-permute-start.12) | collective-permute-done | bytes 303136 | tf_op jit(solution)/shard_map/from_x0_y1_z0_core0/ppermute | solution.py:55
  79.0 8.5 %collective-permute-done.13.refs_2_ = bf16[37,16,256]{2,1,0:T(8,128)(2,1)S(1)} collective-permute-done((bf16[37,16,256]{2,1,0:T(8,128)(2,1)S(1)}, bf16[37,16,256]{2,1,0:T(8,128)(2,1)S(1)}, u32[]{:S(2)}, u32[]{:S(2)}) %collective-permute-start.13) | collective-permute-done | bytes 303136 | tf_op jit(solution)/shard_map/from_x0_y2_z0_core0/ppermute | solution.py:55
  87.7 2.4 %collective-permute-start.17 = (bf16[10,16,256]{2,1,0:T(8,128)(2,1)S(1)}, bf16[10,16,256]{2,1,0:T(8,128)(2,1)S(1)}, u32[]{:S(2)}, u32[]{:S(2)}) collective-permute-start(bf16[10,16,256]{2,1,0:T(8,128)(2,1)S(1)} %get-tuple-element.53), channel_id=1, source_target_pairs={{0,24},{1,9},{2,26},{3,11},{4,28},{5,13},{6,30},{7,15},{8,0},{9,17... | collective-permute-start | bytes 245768 | tf_op jit(solution)/shard_map/from_x0_y0_z2_core0/ppermute | solution.py:55
  91.3 2.4 %collective-permute-start.19 = (bf16[10,16,256]{2,1,0:T(8,128)(2,1)S(1)}, bf16[10,16,256]{2,1,0:T(8,128)(2,1)S(1)}, u32[]{:S(2)}, u32[]{:S(2)}) collective-permute-start(bf16[10,16,256]{2,1,0:T(8,128)(2,1)S(1)} %get-tuple-element.55), channel_id=1, source_target_pairs={{0,8},{1,25},{2,10},{3,27},{4,12},{5,29},{6,14},{7,31},{8,16},{9,1... | collective-permute-start | bytes 245768 | tf_op jit(solution)/shard_map/from_x0_y0_z6_core0/ppermute | solution.py:55
  94.5 2.5 %collective-permute-start.16 = (bf16[2,36,16,256]{3,2,1,0:T(8,128)(2,1)S(1)}, bf16[2,36,16,256]{3,2,1,0:T(8,128)(2,1)S(1)}, u32[]{:S(2)}, u32[]{:S(2)}) collective-permute-start(bf16[2,36,16,256]{3,2,1,0:T(8,128)(2,1)S(1)} %get-tuple-element.52), channel_id=1, source_target_pairs={{0,2},{1,7},{2,4},{3,1},{4,6},{5,3},{6,0},{7,5},{8,10},{9,15},{10,... | collective-permute-start | bytes 1769480 | tf_op jit(solution)/shard_map/from_x0_y3_z0_core0/ppermute | solution.py:55
  97.5 3.8 %collective-permute-start.20 = (f32[10,16,256]{2,1,0:T(8,128)S(1)}, f32[10,16,256]{2,1,0:T(8,128)S(1)}, u32[]{:S(2)}, u32[]{:S(2)}) collective-permute-start(f32[10,16,256]{2,1,0:T(8,128)S(1)} %shard_map.102.part), channel_id=1, source_target_pairs={{0,128},{1,129},{2,130},{3,131},{4,132},{5,133},{6,134},{7,135},{8... | collective-permute-start | bytes 491528 | tf_op jit(solution)/shard_map/from_z_low/ppermute | solution.py:66
  101.3 3.0 %collective-permute-done.20.got = f32[10,16,256]{2,1,0:T(8,128)S(1)} collective-permute-done((f32[10,16,256]{2,1,0:T(8,128)S(1)}, f32[10,16,256]{2,1,0:T(8,128)S(1)}, u32[]{:S(2)}, u32[]{:S(2)}) %collective-permute-start.20) | collective-permute-done | bytes 163872 | tf_op jit(solution)/shard_map/from_z_low/ppermute | solution.py:66
  104.9 2.0 %collective-permute-start.24 = (bf16[10,16,256]{2,1,0:T(8,128)(2,1)S(1)}, bf16[10,16,256]{2,1,0:T(8,128)(2,1)S(1)}, u32[]{:S(2)}, u32[]{:S(2)}) collective-permute-start(bf16[10,16,256]{2,1,0:T(8,128)(2,1)S(1)} %shard_map.103.refs_10_.refs_0_), channel_id=1, source_target_pairs={{0,64},{1,65},{2,66},{3,67},{4,68},{5,69},{6,70},{7,71},{8,72},{9,... | collective-permute-start | bytes 245768 | tf_op jit(solution)/shard_map/from_x2_y0_z0_core0/ppermute | solution.py:55
  106.9 1.7 %collective-permute-start.25 = (bf16[10,16,256]{2,1,0:T(8,128)(2,1)S(1)}, bf16[10,16,256]{2,1,0:T(8,128)(2,1)S(1)}, u32[]{:S(2)}, u32[]{:S(2)}) collective-permute-start(bf16[10,16,256]{2,1,0:T(8,128)(2,1)S(1)} %shard_map.103.refs_10_.refs_0_), channel_id=1, source_target_pairs={{0,32},{1,97},{2,34},{3,99},{4,36},{5,101},{6,38},{7,103},{8,40},{... | collective-permute-start | bytes 245768 | tf_op jit(solution)/shard_map/from_x3_y0_z0_core0/ppermute | solution.py:55
  109.2 4.4 %shard_map.104 = (bf16[128,256]{1,0:T(8,128)(2,1)S(1)}, bf16[128,256]{1,0:T(8,128)(2,1)S(1)}, f32[4,128,1024]{2,1,0:T(8,128)S(1)}, bf16[4,128,1024]{2,1,0:T(8,128)(2,1)S(1)}) custom-call(bf16[4,36,16,256]{3,2,1,0:T(8,128)(2,1)S(1)} %shard_map.95.refs_0_, bf16[4,36,16,256]{3,2,1,0:T(8,128)(2,1)S(1)} %collective-permute-done.4.refs_4_.refs_0_.refs_1_, ...), custom_call_target="tpu_custom_call" | custom-call | flops 10000000000 | tf_op jit(solution)/shard_map/pallas_call | solution.py:90
  113.5 2.1 %collective-permute-start.21 = (bf16[4,128,1024]{2,1,0:T(8,128)(2,1)S(1)}, bf16[4,128,1024]{2,1,0:T(8,128)(2,1)S(1)}, u32[]{:S(2)}, u32[]{:S(2)}) collective-permute-start(bf16[4,128,1024]{2,1,0:T(8,128)(2,1)S(1)} %get-tuple-element.57), channel_id=1, source_target_pairs={{0,1},{1,0},{2,3},{3,2},{4,5},{5,4},{6,7},{7,6},{8,9},{9,8},{10,11... | collective-permute-start | bytes 3145736 | tf_op jit(solution)/shard_map/from_x0_y0_z0_core1/ppermute | solution.py:55
  118.1 3.6 %shard_map.105 = (bf16[2,16,16,1024]{3,2,1,0:T(8,128)(2,1)}, bf16[128,512]{1,0:T(8,128)(2,1)}, f32[8,128]{1,0:T(8,128)S(1)}) custom-call(bf16[4,128,1024]{2,1,0:T(8,128)(2,1)S(1)} %get-tuple-element.36.refs_0_, f32[4,128,1024]{2,1,0:T(8,128)S(1)} %get-tuple-element.56.refs_1_, bf16[4,128,1024]{2,1,0:T(8,128)(2,1)S(1)} %collective-permute-done.21.refs_2_, ...), custom_call_target="tpu_custom_call" | custom-call | flops 1000000000 | tf_op jit(solution)/shard_map/pallas_call | solution.py:90
  (60 shorter events, 19.0 us)
Async XLA Ops:
  12.1 9.5 %collective-permute-start.6 = (bf16[4,128,1024]{2,1,0:T(8,128)(2,1)S(1)}, bf16[4,128,1024]{2,1,0:T(8,128)(2,1)S(1)}, u32[]{:S(2)}, u32[]{:S(2)}) collective-permute-start(bf16[4,128,1024]{2,1,0:T(8,128)(2,1)S(1)} %get-tuple-element.37.act_own.refs_5_), channel_id=1, source_target_pairs={{0,1},{1,0},{2,3},{3,2},{4,5},{5,4},{6,7},{7,6},{8,9},{9,8},{10,11... | collective-permute-start | bytes 3145736 | tf_op jit(solution)/shard_map/from_x0_y0_z0_core1/ppermute | solution.py:55
  12.6 9.0 %collective-permute-start.7 = (bf16[128,256]{1,0:T(8,128)(2,1)S(1)}, bf16[128,256]{1,0:T(8,128)(2,1)S(1)}, u32[]{:S(2)}, u32[]{:S(2)}) collective-permute-start(bf16[128,256]{1,0:T(8,128)(2,1)S(1)} %get-tuple-element.68), channel_id=1, source_target_pairs={{0,1},{1,0},{2,3},{3,2},{4,5},{5,4},{6,7},{7,6},{8,9},{9,8},{10,11... | collective-permute-start | bytes 196616 | tf_op jit(solution)/shard_map/from_x0_y0_z0_core1/ppermute | solution.py:55
  12.8 14.1 %collective-permute-start.2 = (bf16[36,16,256]{2,1,0:T(8,128)(2,1)S(1)}, bf16[36,16,256]{2,1,0:T(8,128)(2,1)S(1)}, u32[]{:S(2)}, u32[]{:S(2)}) collective-permute-start(bf16[36,16,256]{2,1,0:T(8,128)(2,1)S(1)} %shard_map.93.refs_3_.a0), channel_id=1, source_target_pairs={{0,24},{1,9},{2,26},{3,11},{4,28},{5,13},{6,30},{7,15},{8,0},{9,17... | collective-permute-start | bytes 884744 | tf_op jit(solution)/shard_map/from_x0_y0_z2_core0/ppermute | solution.py:55
  14.1 29.2 %collective-permute-start.1 = (bf16[36,16,256]{2,1,0:T(8,128)(2,1)S(1)}, bf16[36,16,256]{2,1,0:T(8,128)(2,1)S(1)}, u32[]{:S(2)}, u32[]{:S(2)}) collective-permute-start(bf16[36,16,256]{2,1,0:T(8,128)(2,1)S(1)} %shard_map.93.refs_3_.a0), channel_id=1, source_target_pairs={{0,16},{1,17},{2,18},{3,19},{4,20},{5,21},{6,22},{7,23},{8,24},{9,... | collective-permute-start | bytes 884744 | tf_op jit(solution)/shard_map/from_x0_y0_z4_core0/ppermute | solution.py:55
  19.2 24.1 %collective-permute-start.3 = (bf16[36,16,256]{2,1,0:T(8,128)(2,1)S(1)}, bf16[36,16,256]{2,1,0:T(8,128)(2,1)S(1)}, u32[]{:S(2)}, u32[]{:S(2)}) collective-permute-start(bf16[36,16,256]{2,1,0:T(8,128)(2,1)S(1)} %shard_map.93.refs_3_.a0), channel_id=1, source_target_pairs={{0,8},{1,25},{2,10},{3,27},{4,12},{5,29},{6,14},{7,31},{8,16},{9,1... | collective-permute-start | bytes 884744 | tf_op jit(solution)/shard_map/from_x0_y0_z6_core0/ppermute | solution.py:55
  24.3 14.8 %collective-permute-start.8 = (bf16[8,9,16,256]{3,2,1,0:T(8,128)(2,1)S(1)}, bf16[8,9,16,256]{3,2,1,0:T(8,128)(2,1)S(1)}, u32[]{:S(2)}, u32[]{:S(2)}) collective-permute-start(bf16[8,9,16,256]{3,2,1,0:T(8,128)(2,1)S(1)} %get-tuple-element.41), channel_id=1, source_target_pairs={{0,32},{1,97},{2,34},{3,99},{4,36},{5,101},{6,38},{7,103},{8,40},{... | collective-permute-start | bytes 1769480 | tf_op jit(solution)/shard_map/from_x3_y0_z0_core0/ppermute | solution.py:55
  26.9 14.5 %collective-permute-start.9 = (bf16[8,9,16,256]{3,2,1,0:T(8,128)(2,1)S(1)}, bf16[8,9,16,256]{3,2,1,0:T(8,128)(2,1)S(1)}, u32[]{:S(2)}, u32[]{:S(2)}) collective-permute-start(bf16[8,9,16,256]{3,2,1,0:T(8,128)(2,1)S(1)} %get-tuple-element.42), channel_id=1, source_target_pairs={{0,96},{1,33},{2,98},{3,35},{4,100},{5,37},{6,102},{7,39},{8,104},... | collective-permute-start | bytes 1769480 | tf_op jit(solution)/shard_map/from_x1_y0_z0_core0/ppermute | solution.py:55
  41.8 27.4 %collective-permute-start.10 = (bf16[16,9,16,256]{3,2,1,0:T(8,128)(2,1)S(1)}, bf16[16,9,16,256]{3,2,1,0:T(8,128)(2,1)S(1)}, u32[]{:S(2)}, u32[]{:S(2)}) collective-permute-start(bf16[16,9,16,256]{3,2,1,0:T(8,128)(2,1)S(1)} %get-tuple-element.43), channel_id=1, source_target_pairs={{0,32},{1,97},{2,34},{3,99},{4,36},{5,101},{6,38},{7,103},{8,40},{... | collective-permute-start | bytes 3538952 | tf_op jit(solution)/shard_map/from_x3_y0_z0_core0/ppermute | solution.py:55
  43.1 27.9 %collective-permute-start.11 = (bf16[16,9,16,256]{3,2,1,0:T(8,128)(2,1)S(1)}, bf16[16,9,16,256]{3,2,1,0:T(8,128)(2,1)S(1)}, u32[]{:S(2)}, u32[]{:S(2)}) collective-permute-start(bf16[16,9,16,256]{3,2,1,0:T(8,128)(2,1)S(1)} %get-tuple-element.44), channel_id=1, source_target_pairs={{0,96},{1,33},{2,98},{3,35},{4,100},{5,37},{6,102},{7,39},{8,104},... | collective-permute-start | bytes 3538952 | tf_op jit(solution)/shard_map/from_x1_y0_z0_core0/ppermute | solution.py:55
  43.4 32.8 %collective-permute-start.4 = (bf16[4,36,16,256]{3,2,1,0:T(8,128)(2,1)S(1)}, bf16[4,36,16,256]{3,2,1,0:T(8,128)(2,1)S(1)}, u32[]{:S(2)}, u32[]{:S(2)}) collective-permute-start(bf16[4,36,16,256]{3,2,1,0:T(8,128)(2,1)S(1)} %shard_map.95.refs_0_), channel_id=1, source_target_pairs={{0,6},{1,3},{2,0},{3,5},{4,2},{5,7},{6,4},{7,1},{8,14},{9,11},{10,... | collective-permute-start | bytes 3538952 | tf_op jit(solution)/shard_map/from_x0_y1_z0_core0/ppermute | solution.py:55
  45.4 30.8 %collective-permute-start.5 = (bf16[4,36,16,256]{3,2,1,0:T(8,128)(2,1)S(1)}, bf16[4,36,16,256]{3,2,1,0:T(8,128)(2,1)S(1)}, u32[]{:S(2)}, u32[]{:S(2)}) collective-permute-start(bf16[4,36,16,256]{3,2,1,0:T(8,128)(2,1)S(1)} %shard_map.95.refs_0_), channel_id=1, source_target_pairs={{0,2},{1,7},{2,4},{3,1},{4,6},{5,3},{6,0},{7,5},{8,10},{9,15},{10,... | collective-permute-start | bytes 3538952 | tf_op jit(solution)/shard_map/from_x0_y3_z0_core0/ppermute | solution.py:55
  71.4 7.6 %collective-permute-start.12 = (bf16[37,16,256]{2,1,0:T(8,128)(2,1)S(1)}, bf16[37,16,256]{2,1,0:T(8,128)(2,1)S(1)}, u32[]{:S(2)}, u32[]{:S(2)}) collective-permute-start(bf16[37,16,256]{2,1,0:T(8,128)(2,1)S(1)} %get-tuple-element.47), channel_id=1, source_target_pairs={{0,6},{1,3},{2,0},{3,5},{4,2},{5,7},{6,4},{7,1},{8,14},{9,11},{10,... | collective-permute-start | bytes 909320 | tf_op jit(solution)/shard_map/from_x0_y1_z0_core0/ppermute | solution.py:55
  72.5 15.1 %collective-permute-start.13 = (bf16[37,16,256]{2,1,0:T(8,128)(2,1)S(1)}, bf16[37,16,256]{2,1,0:T(8,128)(2,1)S(1)}, u32[]{:S(2)}, u32[]{:S(2)}) collective-permute-start(bf16[37,16,256]{2,1,0:T(8,128)(2,1)S(1)} %get-tuple-element.48), channel_id=1, source_target_pairs={{0,4},{1,5},{2,6},{3,7},{4,0},{5,1},{6,2},{7,3},{8,12},{9,13},{10,... | collective-permute-start | bytes 909320 | tf_op jit(solution)/shard_map/from_x0_y2_z0_core0/ppermute | solution.py:55
  75.4 12.1 %collective-permute-start.14 = (bf16[37,16,256]{2,1,0:T(8,128)(2,1)S(1)}, bf16[37,16,256]{2,1,0:T(8,128)(2,1)S(1)}, u32[]{:S(2)}, u32[]{:S(2)}) collective-permute-start(bf16[37,16,256]{2,1,0:T(8,128)(2,1)S(1)} %get-tuple-element.49), channel_id=1, source_target_pairs={{0,2},{1,7},{2,4},{3,1},{4,6},{5,3},{6,0},{7,5},{8,10},{9,15},{10,... | collective-permute-start | bytes 909320 | tf_op jit(solution)/shard_map/from_x0_y3_z0_core0/ppermute | solution.py:55
  87.7 9.3 %collective-permute-start.17 = (bf16[10,16,256]{2,1,0:T(8,128)(2,1)S(1)}, bf16[10,16,256]{2,1,0:T(8,128)(2,1)S(1)}, u32[]{:S(2)}, u32[]{:S(2)}) collective-permute-start(bf16[10,16,256]{2,1,0:T(8,128)(2,1)S(1)} %get-tuple-element.53), channel_id=1, source_target_pairs={{0,24},{1,9},{2,26},{3,11},{4,28},{5,13},{6,30},{7,15},{8,0},{9,17... | collective-permute-start | bytes 245768 | tf_op jit(solution)/shard_map/from_x0_y0_z2_core0/ppermute | solution.py:55
  90.1 7.3 %collective-permute-start.18 = (bf16[10,16,256]{2,1,0:T(8,128)(2,1)S(1)}, bf16[10,16,256]{2,1,0:T(8,128)(2,1)S(1)}, u32[]{:S(2)}, u32[]{:S(2)}) collective-permute-start(bf16[10,16,256]{2,1,0:T(8,128)(2,1)S(1)} %get-tuple-element.54), channel_id=1, source_target_pairs={{0,16},{1,17},{2,18},{3,19},{4,20},{5,21},{6,22},{7,23},{8,24},{9,... | collective-permute-start | bytes 245768 | tf_op jit(solution)/shard_map/from_x0_y0_z4_core0/ppermute | solution.py:55
  91.3 6.1 %collective-permute-start.19 = (bf16[10,16,256]{2,1,0:T(8,128)(2,1)S(1)}, bf16[10,16,256]{2,1,0:T(8,128)(2,1)S(1)}, u32[]{:S(2)}, u32[]{:S(2)}) collective-permute-start(bf16[10,16,256]{2,1,0:T(8,128)(2,1)S(1)} %get-tuple-element.55), channel_id=1, source_target_pairs={{0,8},{1,25},{2,10},{3,27},{4,12},{5,29},{6,14},{7,31},{8,16},{9,1... | collective-permute-start | bytes 245768 | tf_op jit(solution)/shard_map/from_x0_y0_z6_core0/ppermute | solution.py:55
  93.7 14.9 %collective-permute-start.15 = (bf16[2,36,16,256]{3,2,1,0:T(8,128)(2,1)S(1)}, bf16[2,36,16,256]{3,2,1,0:T(8,128)(2,1)S(1)}, u32[]{:S(2)}, u32[]{:S(2)}) collective-permute-start(bf16[2,36,16,256]{3,2,1,0:T(8,128)(2,1)S(1)} %get-tuple-element.51), channel_id=1, source_target_pairs={{0,6},{1,3},{2,0},{3,5},{4,2},{5,7},{6,4},{7,1},{8,14},{9,11},{10,... | collective-permute-start | bytes 1769480 | tf_op jit(solution)/shard_map/from_x0_y1_z0_core0/ppermute | solution.py:55
  94.5 14.7 %collective-permute-start.16 = (bf16[2,36,16,256]{3,2,1,0:T(8,128)(2,1)S(1)}, bf16[2,36,16,256]{3,2,1,0:T(8,128)(2,1)S(1)}, u32[]{:S(2)}, u32[]{:S(2)}) collective-permute-start(bf16[2,36,16,256]{3,2,1,0:T(8,128)(2,1)S(1)} %get-tuple-element.52), channel_id=1, source_target_pairs={{0,2},{1,7},{2,4},{3,1},{4,6},{5,3},{6,0},{7,5},{8,10},{9,15},{10,... | collective-permute-start | bytes 1769480 | tf_op jit(solution)/shard_map/from_x0_y3_z0_core0/ppermute | solution.py:55
  97.5 6.8 %collective-permute-start.20 = (f32[10,16,256]{2,1,0:T(8,128)S(1)}, f32[10,16,256]{2,1,0:T(8,128)S(1)}, u32[]{:S(2)}, u32[]{:S(2)}) collective-permute-start(f32[10,16,256]{2,1,0:T(8,128)S(1)} %shard_map.102.part), channel_id=1, source_target_pairs={{0,128},{1,129},{2,130},{3,131},{4,132},{5,133},{6,134},{7,135},{8... | collective-permute-start | bytes 491528 | tf_op jit(solution)/shard_map/from_z_low/ppermute | solution.py:66
  104.3 11.5 %collective-permute-start.23 = (bf16[10,16,256]{2,1,0:T(8,128)(2,1)S(1)}, bf16[10,16,256]{2,1,0:T(8,128)(2,1)S(1)}, u32[]{:S(2)}, u32[]{:S(2)}) collective-permute-start(bf16[10,16,256]{2,1,0:T(8,128)(2,1)S(1)} %shard_map.103.refs_10_.refs_0_), channel_id=1, source_target_pairs={{0,96},{1,33},{2,98},{3,35},{4,100},{5,37},{6,102},{7,39},{8,104},... | collective-permute-start | bytes 245768 | tf_op jit(solution)/shard_map/from_x1_y0_z0_core0/ppermute | solution.py:55
  104.9 10.8 %collective-permute-start.24 = (bf16[10,16,256]{2,1,0:T(8,128)(2,1)S(1)}, bf16[10,16,256]{2,1,0:T(8,128)(2,1)S(1)}, u32[]{:S(2)}, u32[]{:S(2)}) collective-permute-start(bf16[10,16,256]{2,1,0:T(8,128)(2,1)S(1)} %shard_map.103.refs_10_.refs_0_), channel_id=1, source_target_pairs={{0,64},{1,65},{2,66},{3,67},{4,68},{5,69},{6,70},{7,71},{8,72},{9,... | collective-permute-start | bytes 245768 | tf_op jit(solution)/shard_map/from_x2_y0_z0_core0/ppermute | solution.py:55
  106.9 8.9 %collective-permute-start.25 = (bf16[10,16,256]{2,1,0:T(8,128)(2,1)S(1)}, bf16[10,16,256]{2,1,0:T(8,128)(2,1)S(1)}, u32[]{:S(2)}, u32[]{:S(2)}) collective-permute-start(bf16[10,16,256]{2,1,0:T(8,128)(2,1)S(1)} %shard_map.103.refs_10_.refs_0_), channel_id=1, source_target_pairs={{0,32},{1,97},{2,34},{3,99},{4,36},{5,101},{6,38},{7,103},{8,40},{... | collective-permute-start | bytes 245768 | tf_op jit(solution)/shard_map/from_x3_y0_z0_core0/ppermute | solution.py:55
  115.8 5.8 %collective-permute-start.26 = (bf16[19,16,256]{2,1,0:T(8,128)(2,1)S(1)}, bf16[19,16,256]{2,1,0:T(8,128)(2,1)S(1)}, u32[]{:S(2)}, u32[]{:S(2)}) collective-permute-start(bf16[19,16,256]{2,1,0:T(8,128)(2,1)S(1)} %get-tuple-element.64), channel_id=1, source_target_pairs={{0,1},{1,0},{2,3},{3,2},{4,5},{5,4},{6,7},{7,6},{8,9},{9,8},{10,11... | collective-permute-start | bytes 466952 | tf_op jit(solution)/shard_map/from_x0_y0_z0_core1/ppermute | solution.py:55
  (9 other events, 37.3 us)

commit v6 on v5

--- a/solution.py
+++ b/solution.py
@@ -175,29 +175,51 @@
     )
 
 
+def norm_prepare_body(xp_ref, gain_ref, bias_ref, stat_ref, hat_ref, slope_ref):
+    for n in range(CIN // LANES):
+        lanes = slice(LANES * n, LANES * n + LANES)
+        gain, bias = gain_ref[:, lanes], bias_ref[:, lanes]
+        for i in range(2):
+            rows = slice(64 * i, 64 * i + 64)
+            m, r = stat_ref[0, i : i + 1, lanes], stat_ref[1, i : i + 1, lanes]
+            for p in range(4):
+                hat = (xp_ref[p, rows, lanes].astype(F32) - m) * r
+                y = hat * gain + bias
+                s = jax.nn.sigmoid(y)
+                hat_ref[p, rows, lanes] = hat
+                slope_ref[p, rows, lanes] = s * (1.0 + y * (1.0 - s)) * gain
+
+
+def norm_prepare(planes, gain, bias, stat, after):
+    return call(
+        norm_prepare_body,
+        (arr((4, 128, CIN), F32),) * 2,
+        (planes, gain.reshape(1, CIN), bias.reshape(1, CIN), stat),
+        flops=10**9,
+        vmem=12,
+        after=after,
+    )
+
+
 def norm_back_body(*refs):
-    xp_ref, own_ref, got_ref, gain_ref, bias_ref, stat_ref, res_own, res_got = refs[:8]
-    out_ref, res_ref, mark = refs[8:11]
-    bufs = refs[11:]
+    hat_ref, slope_ref, own_ref, got_ref, stat_ref, res_own, res_got = refs[:7]
+    out_ref, res_ref, mark = refs[7:10]
+    bufs = refs[10:]
     core = position()[3]
     for c in range(2):
         res_ref[:, HALF * c : HALF * c + HALF] = jnp.where(core == c, res_own[...], res_got[...])
     mark[...] = jnp.zeros_like(mark)
     for n in range(CIN // LANES):
         lanes = slice(LANES * n, LANES * n + LANES)
-        gain, bias = gain_ref[:, lanes], bias_ref[:, lanes]
-        mean, rstd = stat_ref[0, :, lanes], stat_ref[1, :, lanes]
+        rstd = stat_ref[1, :, lanes]
         hats, grads, one, two = [], [], [], []
         for i in range(2):
             rows = slice(64 * i, 64 * i + 64)
-            m, r = mean[i : i + 1], rstd[i : i + 1]
             h_list, g_list, s1, s2 = [], [], 0.0, 0.0
             for p in range(4):
-                hat = (xp_ref[p, rows, lanes].astype(F32) - m) * r
-                y = hat * gain + bias
-                s = jax.nn.sigmoid(y)
+                hat = hat_ref[p, rows, lanes]
                 d = own_ref[p, rows, lanes] + got_ref[p, rows, lanes].astype(F32)
-                g = d * (s * (1.0 + y * (1.0 - s))) * gain
+                g = d * slope_ref[p, rows, lanes]
                 s1 = s1 + jnp.sum(g, axis=0, keepdims=True)
                 s2 = s2 + jnp.sum(g * hat, axis=0, keepdims=True)
                 h_list.append(hat)
@@ -227,16 +249,16 @@
             out_ref[:, :, :, at] = buf[n % 2].astype(BF).reshape(2, 16, 16, 128)
 
 
-def norm_backward(planes, own, got, gain, bias, stat, res_own, res_got):
+def norm_backward(hat, slope, own, got, stat, res_own, res_got):
     vm = pl.BlockSpec(memory_space=pltpu.VMEM)
     return call(
         norm_back_body,
         (arr((2, 16, 16, CIN), BF), arr((128, COUT), BF), arr((8, 128), F32)),
-        (planes, own, got, gain.reshape(1, CIN), bias.reshape(1, CIN), stat, res_own, res_got),
+        (hat, slope, own, got, stat, res_own, res_got),
         flops=COST_BACK,
         moved=MOVED_BACK,
         scratch=(pltpu.VMEM((2, 512, 128), F32),) * (LANES // 128),
-        specs=[vm] * 8,
+        specs=[vm] * 7,
         out_specs=(vm,) * 3,
         vmem=16,
     )
@@ -535,7 +557,7 @@
         bias[:, HALF * c : HALF * c + HALF] = part[18, 0:1] + part[18, 1:2]
 
 
-def reduce_xy(parts, mark, around):
+def reduce_xy(parts, mark, around, ready):
     ahead, here, behind, far_low, far_high, bias = parts
     low, high = fetch(far_low, dx=3), fetch(far_high, dx=1)
     ahead, behind = call(
@@ -552,6 +574,7 @@
         (here, fetch(ahead, dx=3), fetch(behind, dx=1), bias),
         flops=COST_SUM,
         vmem=16,
+        after=ready,
     )
     got = [send[0]] + [fetch(send[4 - d], dy=d) for d in range(1, 4)]
     return call(
@@ -601,7 +624,8 @@
     grads = wgrad(act, act_got, cot_own, cot_got)
     mark, level = gather_z(block)
     around = fetch(level, dy=1), fetch(level, dy=3)
-    send = reduce_xy(grads, mark, around)
+    hat, slope = norm_prepare(planes, gn_gain, gn_bias, stat, (level,))
+    send = reduce_xy(grads, mark, around, (slope,))
     parts = gather_y(level, *around, (send[0],))
     cbias = jnp.where(core == 0, conv_bias[:HALF], conv_bias[HALF:]).reshape(1, HALF)
     full = reduce_z(send)
@@ -611,7 +635,7 @@
     dact_got = fetch(dact_other, swap=1)
     out_got = fetch(out_other, swap=1)
     input_grad, outputs, mark = norm_backward(
-        planes, dact_own, dact_got, gn_gain, gn_bias, stat, out_own, out_got
+        hat, slope, dact_own, dact_got, stat, out_own, out_got
     )
     outputs = outputs.reshape(cotangent.shape)
     kernel_grad, bias_grad = spread_x(full, mark)

time: 123 us -> 122 us (level)
    pallas_call x15 -> x16, Pallas kernels: 16.7 us -> 17.2 us  [call(): pl.pallas_call(body, out_shape=outs, scratch_shapes=list(scratch), compil...]
where the time goes in v6:
time: 122 us
  waiting for transfers between devices  55.6 us (46%)
  starting transfers between devices  45.4 us (37%)
  Pallas kernels  17.2 us (14%)
  local copies, waits for them, and re-layouts  2.2 us (2%)
    ppermute x26, waiting for transfers between devices, fetch(): return lax.ppermute(value, AXES, pairs(dx, dy, dz, swap))  52.6 us
    ppermute x26, starting transfers between devices, fetch(): return lax.ppermute(value, AXES, pairs(dx, dy, dz, swap))  42.1 us
    pallas_call x16, Pallas kernels, call(): pl.pallas_call(body, out_shape=outs, scratch_shapes=list(scratch), compil...  17.2 us
    ppermute x1, starting transfers between devices, pair_low(): return lax.ppermute(value, AXES, sorted(out))  3.36 us
    ppermute x1, waiting for transfers between devices, pair_low(): return lax.ppermute(value, AXES, sorted(out))  3 us
  transfers between devices with their start and end apart: 27, of which 11 were waited for; matrix products, arithmetic and copies ran while one was open for 0% of the time, Pallas kernels for 10%

profile of v6, /device:TPU:1, one launch (start us, length us, event | category | flops | bytes accessed | tf_op | source)
XLA Modules:
  0.0 122.2 jit_solution(3852639887447367883)
XLA Ops:
  1.7 3.3 %collective-permute-start = (bf16[18,16,256]{2,1,0:T(8,128)(2,1)S(1)}, bf16[18,16,256]{2,1,0:T(8,128)(2,1)S(1)}, u32[]{:S(2)}, u32[]{:S(2)}) collective-permute-start(bf16[18,16,256]{2,1,0:T(8,128)(2,1)S(1)} %slice_select_fusion), channel_id=1, source_target_pairs={{0,1},{1,0},{2,3},{3,2},{4,5},{5,4},{6,7},{7,6},{8,9},{9,8},{10,11... | collective-permute-start | bytes 442376 | tf_op jit(solution)/shard_map/from_x0_y0_z0_core1/ppermute | solution.py:55
  8.2 3.9 %shard_map.94 = (bf16[4,128,1024]{2,1,0:T(8,128)(2,1)S(1)}, bf16[4,128,1024]{2,1,0:T(8,128)(2,1)S(1)}, f32[2,8,1024]{2,1,0:T(8,128)S(1)}) custom-call(bf16[2,16,16,1024]{3,2,1,0:T(8,128)(2,1)S(1)} %copy-done.1, f32[1,1024]{1,0:T(1,128)S(1)} %bitcast.10, f32[1,1024]{1,0:T(1,128)S(1)} %bitcast.12, bf16[36,16,256]{2,1,0:T(8,128)(2,1)S(1)} %shard_map.93.refs_3_.a0), custom_call_target="tpu_custom_call" | custom-call | flops 10000000000 | bytes 3219456 | tf_op jit(solution)/shard_map/pallas_call | solution.py:90
  14.1 5.1 %collective-permute-start.1 = (bf16[36,16,256]{2,1,0:T(8,128)(2,1)S(1)}, bf16[36,16,256]{2,1,0:T(8,128)(2,1)S(1)}, u32[]{:S(2)}, u32[]{:S(2)}) collective-permute-start(bf16[36,16,256]{2,1,0:T(8,128)(2,1)S(1)} %shard_map.93.refs_3_.a0), channel_id=1, source_target_pairs={{0,16},{1,17},{2,18},{3,19},{4,20},{5,21},{6,22},{7,23},{8,24},{9,... | collective-permute-start | bytes 884744 | tf_op jit(solution)/shard_map/from_x0_y0_z4_core0/ppermute | solution.py:55
  19.2 2.4 %collective-permute-start.3 = (bf16[36,16,256]{2,1,0:T(8,128)(2,1)S(1)}, bf16[36,16,256]{2,1,0:T(8,128)(2,1)S(1)}, u32[]{:S(2)}, u32[]{:S(2)}) collective-permute-start(bf16[36,16,256]{2,1,0:T(8,128)(2,1)S(1)} %shard_map.93.refs_3_.a0), channel_id=1, source_target_pairs={{0,8},{1,25},{2,10},{3,27},{4,12},{5,29},{6,14},{7,31},{8,16},{9,1... | collective-permute-start | bytes 884744 | tf_op jit(solution)/shard_map/from_x0_y0_z6_core0/ppermute | solution.py:55
  21.6 2.7 %shard_map.97 = (bf16[16,9,16,256]{3,2,1,0:T(8,128)(2,1)S(1)}, bf16[16,9,16,256]{3,2,1,0:T(8,128)(2,1)S(1)}, bf16[16,9,16,256]{3,2,1,0:T(8,128)(2,1)S(1)}, bf16[...) custom-call(bf16[4,128,1024]{2,1,0:T(8,128)(2,1)S(1)} %get-tuple-element.42.act_own.refs_5_, ...), custom_call_target="tpu_custom_call" | custom-call | flops 20000000000 | bytes 6955008 | tf_op jit(solution)/shard_map/pallas_call | solution.py:90
  24.3 2.6 %collective-permute-start.8 = (bf16[8,9,16,256]{3,2,1,0:T(8,128)(2,1)S(1)}, bf16[8,9,16,256]{3,2,1,0:T(8,128)(2,1)S(1)}, u32[]{:S(2)}, u32[]{:S(2)}) collective-permute-start(bf16[8,9,16,256]{3,2,1,0:T(8,128)(2,1)S(1)} %get-tuple-element.46), channel_id=1, source_target_pairs={{0,32},{1,97},{2,34},{3,99},{4,36},{5,101},{6,38},{7,103},{8,40},{... | collective-permute-start | bytes 1769480 | tf_op jit(solution)/shard_map/from_x3_y0_z0_core0/ppermute | solution.py:55
  26.9 12.2 %collective-permute-done.8.refs_2_ = bf16[8,9,16,256]{3,2,1,0:T(8,128)(2,1)S(1)} collective-permute-done((bf16[8,9,16,256]{3,2,1,0:T(8,128)(2,1)S(1)}, bf16[8,9,16,256]{3,2,1,0:T(8,128)(2,1)S(1)}, u32[]{:S(2)}, u32[]{:S(2)}) %collective-permute-start.8) | collective-permute-done | bytes 589856 | tf_op jit(solution)/shard_map/from_x3_y0_z0_core0/ppermute | solution.py:55
  39.1 2.3 %collective-permute-done.9.refs_3_ = bf16[8,9,16,256]{3,2,1,0:T(8,128)(2,1)S(1)} collective-permute-done((bf16[8,9,16,256]{3,2,1,0:T(8,128)(2,1)S(1)}, bf16[8,9,16,256]{3,2,1,0:T(8,128)(2,1)S(1)}, u32[]{:S(2)}, u32[]{:S(2)}) %collective-permute-start.9) | collective-permute-done | bytes 589856 | tf_op jit(solution)/shard_map/from_x1_y0_z0_core0/ppermute | solution.py:55
  43.4 2.0 %collective-permute-start.4 = (bf16[4,36,16,256]{3,2,1,0:T(8,128)(2,1)S(1)}, bf16[4,36,16,256]{3,2,1,0:T(8,128)(2,1)S(1)}, u32[]{:S(2)}, u32[]{:S(2)}) collective-permute-start(bf16[4,36,16,256]{3,2,1,0:T(8,128)(2,1)S(1)} %shard_map.95.refs_4_.refs_0_), channel_id=1, source_target_pairs={{0,6},{1,3},{2,0},{3,5},{4,2},{5,7},{6,4},{7,1},{8,14},{9,11},{10,... | collective-permute-start | bytes 3538952 | tf_op jit(solution)/shard_map/from_x0_y1_z0_core0/ppermute | solution.py:55
  47.7 21.5 %collective-permute-done.10.refs_1_ = bf16[16,9,16,256]{3,2,1,0:T(8,128)(2,1)S(1)} collective-permute-done((bf16[16,9,16,256]{3,2,1,0:T(8,128)(2,1)S(1)}, bf16[16,9,16,256]{3,2,1,0:T(8,128)(2,1)S(1)}, u32[]{:S(2)}, u32[]{:S(2)}) %collective-permute-start.10) | collective-permute-done | bytes 1179680 | tf_op jit(solution)/shard_map/from_x3_y0_z0_core0/ppermute | solution.py:55
  69.2 1.8 %collective-permute-done.11.refs_2_ = bf16[16,9,16,256]{3,2,1,0:T(8,128)(2,1)S(1)} collective-permute-done((bf16[16,9,16,256]{3,2,1,0:T(8,128)(2,1)S(1)}, bf16[16,9,16,256]{3,2,1,0:T(8,128)(2,1)S(1)}, u32[]{:S(2)}, u32[]{:S(2)}) %collective-permute-start.11) | collective-permute-done | bytes 1179680 | tf_op jit(solution)/shard_map/from_x1_y0_z0_core0/ppermute | solution.py:55
  72.5 2.9 %collective-permute-start.13 = (bf16[37,16,256]{2,1,0:T(8,128)(2,1)S(1)}, bf16[37,16,256]{2,1,0:T(8,128)(2,1)S(1)}, u32[]{:S(2)}, u32[]{:S(2)}) collective-permute-start(bf16[37,16,256]{2,1,0:T(8,128)(2,1)S(1)} %get-tuple-element.53), channel_id=1, source_target_pairs={{0,4},{1,5},{2,6},{3,7},{4,0},{5,1},{6,2},{7,3},{8,12},{9,13},{10,... | collective-permute-start | bytes 909320 | tf_op jit(solution)/shard_map/from_x0_y2_z0_core0/ppermute | solution.py:55
  76.2 2.8 %collective-permute-done.12.refs_1_ = bf16[37,16,256]{2,1,0:T(8,128)(2,1)S(1)} collective-permute-done((bf16[37,16,256]{2,1,0:T(8,128)(2,1)S(1)}, bf16[37,16,256]{2,1,0:T(8,128)(2,1)S(1)}, u32[]{:S(2)}, u32[]{:S(2)}) %collective-permute-start.12) | collective-permute-done | bytes 303136 | tf_op jit(solution)/shard_map/from_x0_y1_z0_core0/ppermute | solution.py:55
  79.0 8.5 %collective-permute-done.13.refs_2_ = bf16[37,16,256]{2,1,0:T(8,128)(2,1)S(1)} collective-permute-done((bf16[37,16,256]{2,1,0:T(8,128)(2,1)S(1)}, bf16[37,16,256]{2,1,0:T(8,128)(2,1)S(1)}, u32[]{:S(2)}, u32[]{:S(2)}) %collective-permute-start.13) | collective-permute-done | bytes 303136 | tf_op jit(solution)/shard_map/from_x0_y2_z0_core0/ppermute | solution.py:55
  87.7 2.4 %collective-permute-start.17 = (bf16[10,16,256]{2,1,0:T(8,128)(2,1)S(1)}, bf16[10,16,256]{2,1,0:T(8,128)(2,1)S(1)}, u32[]{:S(2)}, u32[]{:S(2)}) collective-permute-start(bf16[10,16,256]{2,1,0:T(8,128)(2,1)S(1)} %get-tuple-element.58), channel_id=1, source_target_pairs={{0,24},{1,9},{2,26},{3,11},{4,28},{5,13},{6,30},{7,15},{8,0},{9,17... | collective-permute-start | bytes 245768 | tf_op jit(solution)/shard_map/from_x0_y0_z2_core0/ppermute | solution.py:55
  91.3 2.4 %collective-permute-start.19 = (bf16[10,16,256]{2,1,0:T(8,128)(2,1)S(1)}, bf16[10,16,256]{2,1,0:T(8,128)(2,1)S(1)}, u32[]{:S(2)}, u32[]{:S(2)}) collective-permute-start(bf16[10,16,256]{2,1,0:T(8,128)(2,1)S(1)} %get-tuple-element.60), channel_id=1, source_target_pairs={{0,8},{1,25},{2,10},{3,27},{4,12},{5,29},{6,14},{7,31},{8,16},{9,1... | collective-permute-start | bytes 245768 | tf_op jit(solution)/shard_map/from_x0_y0_z6_core0/ppermute | solution.py:55
  94.5 2.5 %collective-permute-start.16 = (bf16[2,36,16,256]{3,2,1,0:T(8,128)(2,1)S(1)}, bf16[2,36,16,256]{3,2,1,0:T(8,128)(2,1)S(1)}, u32[]{:S(2)}, u32[]{:S(2)}) collective-permute-start(bf16[2,36,16,256]{3,2,1,0:T(8,128)(2,1)S(1)} %get-tuple-element.57), channel_id=1, source_target_pairs={{0,2},{1,7},{2,4},{3,1},{4,6},{5,3},{6,0},{7,5},{8,10},{9,15},{10,... | collective-permute-start | bytes 1769480 | tf_op jit(solution)/shard_map/from_x0_y3_z0_core0/ppermute | solution.py:55
  97.5 3.4 %collective-permute-start.20 = (f32[10,16,256]{2,1,0:T(8,128)S(1)}, f32[10,16,256]{2,1,0:T(8,128)S(1)}, u32[]{:S(2)}, u32[]{:S(2)}) collective-permute-start(f32[10,16,256]{2,1,0:T(8,128)S(1)} %shard_map.103.part), channel_id=1, source_target_pairs={{0,128},{1,129},{2,130},{3,131},{4,132},{5,133},{6,134},{7,135},{8... | collective-permute-start | bytes 491528 | tf_op jit(solution)/shard_map/from_z_low/ppermute | solution.py:66
  100.8 3.0 %collective-permute-done.20.got = f32[10,16,256]{2,1,0:T(8,128)S(1)} collective-permute-done((f32[10,16,256]{2,1,0:T(8,128)S(1)}, f32[10,16,256]{2,1,0:T(8,128)S(1)}, u32[]{:S(2)}, u32[]{:S(2)}) %collective-permute-start.20) | collective-permute-done | bytes 163872 | tf_op jit(solution)/shard_map/from_z_low/ppermute | solution.py:66
  104.9 2.0 %collective-permute-start.24 = (bf16[10,16,256]{2,1,0:T(8,128)(2,1)S(1)}, bf16[10,16,256]{2,1,0:T(8,128)(2,1)S(1)}, u32[]{:S(2)}, u32[]{:S(2)}) collective-permute-start(bf16[10,16,256]{2,1,0:T(8,128)(2,1)S(1)} %shard_map.104.refs_10_.refs_0_), channel_id=1, source_target_pairs={{0,64},{1,65},{2,66},{3,67},{4,68},{5,69},{6,70},{7,71},{8,72},{9,... | collective-permute-start | bytes 245768 | tf_op jit(solution)/shard_map/from_x2_y0_z0_core0/ppermute | solution.py:55
  106.9 1.8 %collective-permute-start.25 = (bf16[10,16,256]{2,1,0:T(8,128)(2,1)S(1)}, bf16[10,16,256]{2,1,0:T(8,128)(2,1)S(1)}, u32[]{:S(2)}, u32[]{:S(2)}) collective-permute-start(bf16[10,16,256]{2,1,0:T(8,128)(2,1)S(1)} %shard_map.104.refs_10_.refs_0_), channel_id=1, source_target_pairs={{0,32},{1,97},{2,34},{3,99},{4,36},{5,101},{6,38},{7,103},{8,40},{... | collective-permute-start | bytes 245768 | tf_op jit(solution)/shard_map/from_x3_y0_z0_core0/ppermute | solution.py:55
  109.2 4.4 %shard_map.105 = (bf16[128,256]{1,0:T(8,128)(2,1)S(1)}, bf16[128,256]{1,0:T(8,128)(2,1)S(1)}, f32[4,128,1024]{2,1,0:T(8,128)S(1)}, bf16[4,128,1024]{2,1,0:T(8,128)(2,1)S(1)}) custom-call(bf16[4,36,16,256]{3,2,1,0:T(8,128)(2,1)S(1)} %shard_map.95.refs_4_.refs_0_, bf16[4,36,16,256]{3,2,1,0:T(8,128)(2,1)S(1)} %collective-permute-done.4.refs_4_.refs_0_.refs_1_, ...), custom_call_target="tpu_custom_call" | custom-call | flops 10000000000 | tf_op jit(solution)/shard_map/pallas_call | solution.py:90
  113.5 2.1 %collective-permute-start.21 = (bf16[4,128,1024]{2,1,0:T(8,128)(2,1)S(1)}, bf16[4,128,1024]{2,1,0:T(8,128)(2,1)S(1)}, u32[]{:S(2)}, u32[]{:S(2)}) collective-permute-start(bf16[4,128,1024]{2,1,0:T(8,128)(2,1)S(1)} %get-tuple-element.62), channel_id=1, source_target_pairs={{0,1},{1,0},{2,3},{3,2},{4,5},{5,4},{6,7},{7,6},{8,9},{9,8},{10,11... | collective-permute-start | bytes 3145736 | tf_op jit(solution)/shard_map/from_x0_y0_z0_core1/ppermute | solution.py:55
  118.0 3.3 %shard_map.106 = (bf16[2,16,16,1024]{3,2,1,0:T(8,128)(2,1)}, bf16[128,512]{1,0:T(8,128)(2,1)}, f32[8,128]{1,0:T(8,128)S(1)}) custom-call(f32[4,128,1024]{2,1,0:T(8,128)S(1)} %get-tuple-element.40.refs_0_, f32[4,128,1024]{2,1,0:T(8,128)S(1)} %get-tuple-element.41.refs_4_.refs_1_, f32[4,128,1024]{2,1,0:T(8,128)S(1)} %get-tuple-element.61.refs_2_, ...), custom_call_target="tpu_custom_call" | custom-call | flops 1000000000 | tf_op jit(solution)/shard_map/pallas_call | solution.py:90
  (61 shorter events, 20.2 us)
Async XLA Ops:
  12.1 9.5 %collective-permute-start.6 = (bf16[4,128,1024]{2,1,0:T(8,128)(2,1)S(1)}, bf16[4,128,1024]{2,1,0:T(8,128)(2,1)S(1)}, u32[]{:S(2)}, u32[]{:S(2)}) collective-permute-start(bf16[4,128,1024]{2,1,0:T(8,128)(2,1)S(1)} %get-tuple-element.42.act_own.refs_5_), channel_id=1, source_target_pairs={{0,1},{1,0},{2,3},{3,2},{4,5},{5,4},{6,7},{7,6},{8,9},{9,8},{10,11... | collective-permute-start | bytes 3145736 | tf_op jit(solution)/shard_map/from_x0_y0_z0_core1/ppermute | solution.py:55
  12.6 9.0 %collective-permute-start.7 = (bf16[128,256]{1,0:T(8,128)(2,1)S(1)}, bf16[128,256]{1,0:T(8,128)(2,1)S(1)}, u32[]{:S(2)}, u32[]{:S(2)}) collective-permute-start(bf16[128,256]{1,0:T(8,128)(2,1)S(1)} %get-tuple-element.72), channel_id=1, source_target_pairs={{0,1},{1,0},{2,3},{3,2},{4,5},{5,4},{6,7},{7,6},{8,9},{9,8},{10,11... | collective-permute-start | bytes 196616 | tf_op jit(solution)/shard_map/from_x0_y0_z0_core1/ppermute | solution.py:55
  12.8 14.1 %collective-permute-start.2 = (bf16[36,16,256]{2,1,0:T(8,128)(2,1)S(1)}, bf16[36,16,256]{2,1,0:T(8,128)(2,1)S(1)}, u32[]{:S(2)}, u32[]{:S(2)}) collective-permute-start(bf16[36,16,256]{2,1,0:T(8,128)(2,1)S(1)} %shard_map.93.refs_3_.a0), channel_id=1, source_target_pairs={{0,24},{1,9},{2,26},{3,11},{4,28},{5,13},{6,30},{7,15},{8,0},{9,17... | collective-permute-start | bytes 884744 | tf_op jit(solution)/shard_map/from_x0_y0_z2_core0/ppermute | solution.py:55
  14.1 29.2 %collective-permute-start.1 = (bf16[36,16,256]{2,1,0:T(8,128)(2,1)S(1)}, bf16[36,16,256]{2,1,0:T(8,128)(2,1)S(1)}, u32[]{:S(2)}, u32[]{:S(2)}) collective-permute-start(bf16[36,16,256]{2,1,0:T(8,128)(2,1)S(1)} %shard_map.93.refs_3_.a0), channel_id=1, source_target_pairs={{0,16},{1,17},{2,18},{3,19},{4,20},{5,21},{6,22},{7,23},{8,24},{9,... | collective-permute-start | bytes 884744 | tf_op jit(solution)/shard_map/from_x0_y0_z4_core0/ppermute | solution.py:55
  19.2 24.1 %collective-permute-start.3 = (bf16[36,16,256]{2,1,0:T(8,128)(2,1)S(1)}, bf16[36,16,256]{2,1,0:T(8,128)(2,1)S(1)}, u32[]{:S(2)}, u32[]{:S(2)}) collective-permute-start(bf16[36,16,256]{2,1,0:T(8,128)(2,1)S(1)} %shard_map.93.refs_3_.a0), channel_id=1, source_target_pairs={{0,8},{1,25},{2,10},{3,27},{4,12},{5,29},{6,14},{7,31},{8,16},{9,1... | collective-permute-start | bytes 884744 | tf_op jit(solution)/shard_map/from_x0_y0_z6_core0/ppermute | solution.py:55
  24.3 14.8 %collective-permute-start.8 = (bf16[8,9,16,256]{3,2,1,0:T(8,128)(2,1)S(1)}, bf16[8,9,16,256]{3,2,1,0:T(8,128)(2,1)S(1)}, u32[]{:S(2)}, u32[]{:S(2)}) collective-permute-start(bf16[8,9,16,256]{3,2,1,0:T(8,128)(2,1)S(1)} %get-tuple-element.46), channel_id=1, source_target_pairs={{0,32},{1,97},{2,34},{3,99},{4,36},{5,101},{6,38},{7,103},{8,40},{... | collective-permute-start | bytes 1769480 | tf_op jit(solution)/shard_map/from_x3_y0_z0_core0/ppermute | solution.py:55
  26.9 14.5 %collective-permute-start.9 = (bf16[8,9,16,256]{3,2,1,0:T(8,128)(2,1)S(1)}, bf16[8,9,16,256]{3,2,1,0:T(8,128)(2,1)S(1)}, u32[]{:S(2)}, u32[]{:S(2)}) collective-permute-start(bf16[8,9,16,256]{3,2,1,0:T(8,128)(2,1)S(1)} %get-tuple-element.47), channel_id=1, source_target_pairs={{0,96},{1,33},{2,98},{3,35},{4,100},{5,37},{6,102},{7,39},{8,104},... | collective-permute-start | bytes 1769480 | tf_op jit(solution)/shard_map/from_x1_y0_z0_core0/ppermute | solution.py:55
  41.8 27.4 %collective-permute-start.10 = (bf16[16,9,16,256]{3,2,1,0:T(8,128)(2,1)S(1)}, bf16[16,9,16,256]{3,2,1,0:T(8,128)(2,1)S(1)}, u32[]{:S(2)}, u32[]{:S(2)}) collective-permute-start(bf16[16,9,16,256]{3,2,1,0:T(8,128)(2,1)S(1)} %get-tuple-element.48), channel_id=1, source_target_pairs={{0,32},{1,97},{2,34},{3,99},{4,36},{5,101},{6,38},{7,103},{8,40},{... | collective-permute-start | bytes 3538952 | tf_op jit(solution)/shard_map/from_x3_y0_z0_core0/ppermute | solution.py:55
  43.1 27.9 %collective-permute-start.11 = (bf16[16,9,16,256]{3,2,1,0:T(8,128)(2,1)S(1)}, bf16[16,9,16,256]{3,2,1,0:T(8,128)(2,1)S(1)}, u32[]{:S(2)}, u32[]{:S(2)}) collective-permute-start(bf16[16,9,16,256]{3,2,1,0:T(8,128)(2,1)S(1)} %get-tuple-element.49), channel_id=1, source_target_pairs={{0,96},{1,33},{2,98},{3,35},{4,100},{5,37},{6,102},{7,39},{8,104},... | collective-permute-start | bytes 3538952 | tf_op jit(solution)/shard_map/from_x1_y0_z0_core0/ppermute | solution.py:55
  43.4 32.8 %collective-permute-start.4 = (bf16[4,36,16,256]{3,2,1,0:T(8,128)(2,1)S(1)}, bf16[4,36,16,256]{3,2,1,0:T(8,128)(2,1)S(1)}, u32[]{:S(2)}, u32[]{:S(2)}) collective-permute-start(bf16[4,36,16,256]{3,2,1,0:T(8,128)(2,1)S(1)} %shard_map.95.refs_4_.refs_0_), channel_id=1, source_target_pairs={{0,6},{1,3},{2,0},{3,5},{4,2},{5,7},{6,4},{7,1},{8,14},{9,11},{10,... | collective-permute-start | bytes 3538952 | tf_op jit(solution)/shard_map/from_x0_y1_z0_core0/ppermute | solution.py:55
  45.4 30.8 %collective-permute-start.5 = (bf16[4,36,16,256]{3,2,1,0:T(8,128)(2,1)S(1)}, bf16[4,36,16,256]{3,2,1,0:T(8,128)(2,1)S(1)}, u32[]{:S(2)}, u32[]{:S(2)}) collective-permute-start(bf16[4,36,16,256]{3,2,1,0:T(8,128)(2,1)S(1)} %shard_map.95.refs_4_.refs_0_), channel_id=1, source_target_pairs={{0,2},{1,7},{2,4},{3,1},{4,6},{5,3},{6,0},{7,5},{8,10},{9,15},{10,... | collective-permute-start | bytes 3538952 | tf_op jit(solution)/shard_map/from_x0_y3_z0_core0/ppermute | solution.py:55
  71.4 7.6 %collective-permute-start.12 = (bf16[37,16,256]{2,1,0:T(8,128)(2,1)S(1)}, bf16[37,16,256]{2,1,0:T(8,128)(2,1)S(1)}, u32[]{:S(2)}, u32[]{:S(2)}) collective-permute-start(bf16[37,16,256]{2,1,0:T(8,128)(2,1)S(1)} %get-tuple-element.52), channel_id=1, source_target_pairs={{0,6},{1,3},{2,0},{3,5},{4,2},{5,7},{6,4},{7,1},{8,14},{9,11},{10,... | collective-permute-start | bytes 909320 | tf_op jit(solution)/shard_map/from_x0_y1_z0_core0/ppermute | solution.py:55
  72.5 15.1 %collective-permute-start.13 = (bf16[37,16,256]{2,1,0:T(8,128)(2,1)S(1)}, bf16[37,16,256]{2,1,0:T(8,128)(2,1)S(1)}, u32[]{:S(2)}, u32[]{:S(2)}) collective-permute-start(bf16[37,16,256]{2,1,0:T(8,128)(2,1)S(1)} %get-tuple-element.53), channel_id=1, source_target_pairs={{0,4},{1,5},{2,6},{3,7},{4,0},{5,1},{6,2},{7,3},{8,12},{9,13},{10,... | collective-permute-start | bytes 909320 | tf_op jit(solution)/shard_map/from_x0_y2_z0_core0/ppermute | solution.py:55
  75.4 12.1 %collective-permute-start.14 = (bf16[37,16,256]{2,1,0:T(8,128)(2,1)S(1)}, bf16[37,16,256]{2,1,0:T(8,128)(2,1)S(1)}, u32[]{:S(2)}, u32[]{:S(2)}) collective-permute-start(bf16[37,16,256]{2,1,0:T(8,128)(2,1)S(1)} %get-tuple-element.54), channel_id=1, source_target_pairs={{0,2},{1,7},{2,4},{3,1},{4,6},{5,3},{6,0},{7,5},{8,10},{9,15},{10,... | collective-permute-start | bytes 909320 | tf_op jit(solution)/shard_map/from_x0_y3_z0_core0/ppermute | solution.py:55
  87.7 9.3 %collective-permute-start.17 = (bf16[10,16,256]{2,1,0:T(8,128)(2,1)S(1)}, bf16[10,16,256]{2,1,0:T(8,128)(2,1)S(1)}, u32[]{:S(2)}, u32[]{:S(2)}) collective-permute-start(bf16[10,16,256]{2,1,0:T(8,128)(2,1)S(1)} %get-tuple-element.58), channel_id=1, source_target_pairs={{0,24},{1,9},{2,26},{3,11},{4,28},{5,13},{6,30},{7,15},{8,0},{9,17... | collective-permute-start | bytes 245768 | tf_op jit(solution)/shard_map/from_x0_y0_z2_core0/ppermute | solution.py:55
  90.1 7.3 %collective-permute-start.18 = (bf16[10,16,256]{2,1,0:T(8,128)(2,1)S(1)}, bf16[10,16,256]{2,1,0:T(8,128)(2,1)S(1)}, u32[]{:S(2)}, u32[]{:S(2)}) collective-permute-start(bf16[10,16,256]{2,1,0:T(8,128)(2,1)S(1)} %get-tuple-element.59), channel_id=1, source_target_pairs={{0,16},{1,17},{2,18},{3,19},{4,20},{5,21},{6,22},{7,23},{8,24},{9,... | collective-permute-start | bytes 245768 | tf_op jit(solution)/shard_map/from_x0_y0_z4_core0/ppermute | solution.py:55
  91.3 6.1 %collective-permute-start.19 = (bf16[10,16,256]{2,1,0:T(8,128)(2,1)S(1)}, bf16[10,16,256]{2,1,0:T(8,128)(2,1)S(1)}, u32[]{:S(2)}, u32[]{:S(2)}) collective-permute-start(bf16[10,16,256]{2,1,0:T(8,128)(2,1)S(1)} %get-tuple-element.60), channel_id=1, source_target_pairs={{0,8},{1,25},{2,10},{3,27},{4,12},{5,29},{6,14},{7,31},{8,16},{9,1... | collective-permute-start | bytes 245768 | tf_op jit(solution)/shard_map/from_x0_y0_z6_core0/ppermute | solution.py:55
  93.7 14.9 %collective-permute-start.15 = (bf16[2,36,16,256]{3,2,1,0:T(8,128)(2,1)S(1)}, bf16[2,36,16,256]{3,2,1,0:T(8,128)(2,1)S(1)}, u32[]{:S(2)}, u32[]{:S(2)}) collective-permute-start(bf16[2,36,16,256]{3,2,1,0:T(8,128)(2,1)S(1)} %get-tuple-element.56), channel_id=1, source_target_pairs={{0,6},{1,3},{2,0},{3,5},{4,2},{5,7},{6,4},{7,1},{8,14},{9,11},{10,... | collective-permute-start | bytes 1769480 | tf_op jit(solution)/shard_map/from_x0_y1_z0_core0/ppermute | solution.py:55
  94.5 14.7 %collective-permute-start.16 = (bf16[2,36,16,256]{3,2,1,0:T(8,128)(2,1)S(1)}, bf16[2,36,16,256]{3,2,1,0:T(8,128)(2,1)S(1)}, u32[]{:S(2)}, u32[]{:S(2)}) collective-permute-start(bf16[2,36,16,256]{3,2,1,0:T(8,128)(2,1)S(1)} %get-tuple-element.57), channel_id=1, source_target_pairs={{0,2},{1,7},{2,4},{3,1},{4,6},{5,3},{6,0},{7,5},{8,10},{9,15},{10,... | collective-permute-start | bytes 1769480 | tf_op jit(solution)/shard_map/from_x0_y3_z0_core0/ppermute | solution.py:55
  97.5 6.4 %collective-permute-start.20 = (f32[10,16,256]{2,1,0:T(8,128)S(1)}, f32[10,16,256]{2,1,0:T(8,128)S(1)}, u32[]{:S(2)}, u32[]{:S(2)}) collective-permute-start(f32[10,16,256]{2,1,0:T(8,128)S(1)} %shard_map.103.part), channel_id=1, source_target_pairs={{0,128},{1,129},{2,130},{3,131},{4,132},{5,133},{6,134},{7,135},{8... | collective-permute-start | bytes 491528 | tf_op jit(solution)/shard_map/from_z_low/ppermute | solution.py:66
  103.9 11.9 %collective-permute-start.23 = (bf16[10,16,256]{2,1,0:T(8,128)(2,1)S(1)}, bf16[10,16,256]{2,1,0:T(8,128)(2,1)S(1)}, u32[]{:S(2)}, u32[]{:S(2)}) collective-permute-start(bf16[10,16,256]{2,1,0:T(8,128)(2,1)S(1)} %shard_map.104.refs_10_.refs_0_), channel_id=1, source_target_pairs={{0,96},{1,33},{2,98},{3,35},{4,100},{5,37},{6,102},{7,39},{8,104},... | collective-permute-start | bytes 245768 | tf_op jit(solution)/shard_map/from_x1_y0_z0_core0/ppermute | solution.py:55
  104.9 10.8 %collective-permute-start.24 = (bf16[10,16,256]{2,1,0:T(8,128)(2,1)S(1)}, bf16[10,16,256]{2,1,0:T(8,128)(2,1)S(1)}, u32[]{:S(2)}, u32[]{:S(2)}) collective-permute-start(bf16[10,16,256]{2,1,0:T(8,128)(2,1)S(1)} %shard_map.104.refs_10_.refs_0_), channel_id=1, source_target_pairs={{0,64},{1,65},{2,66},{3,67},{4,68},{5,69},{6,70},{7,71},{8,72},{9,... | collective-permute-start | bytes 245768 | tf_op jit(solution)/shard_map/from_x2_y0_z0_core0/ppermute | solution.py:55
  106.9 8.9 %collective-permute-start.25 = (bf16[10,16,256]{2,1,0:T(8,128)(2,1)S(1)}, bf16[10,16,256]{2,1,0:T(8,128)(2,1)S(1)}, u32[]{:S(2)}, u32[]{:S(2)}) collective-permute-start(bf16[10,16,256]{2,1,0:T(8,128)(2,1)S(1)} %shard_map.104.refs_10_.refs_0_), channel_id=1, source_target_pairs={{0,32},{1,97},{2,34},{3,99},{4,36},{5,101},{6,38},{7,103},{8,40},{... | collective-permute-start | bytes 245768 | tf_op jit(solution)/shard_map/from_x3_y0_z0_core0/ppermute | solution.py:55
  115.8 5.5 %collective-permute-start.26 = (bf16[19,16,256]{2,1,0:T(8,128)(2,1)S(1)}, bf16[19,16,256]{2,1,0:T(8,128)(2,1)S(1)}, u32[]{:S(2)}, u32[]{:S(2)}) collective-permute-start(bf16[19,16,256]{2,1,0:T(8,128)(2,1)S(1)} %get-tuple-element.68), channel_id=1, source_target_pairs={{0,1},{1,0},{2,3},{3,2},{4,5},{5,4},{6,7},{7,6},{8,9},{9,8},{10,11... | collective-permute-start | bytes 466952 | tf_op jit(solution)/shard_map/from_x0_y0_z0_core1/ppermute | solution.py:55
  (9 other events, 36.8 us)
